TPU v7x, 512 devices: a whole 4x4x16 slice. The times are simulated.
512 devices in a mesh: tm: 16 (over x, z_lo), height: 4 (over y), head: 8 (over z_hi, core).
Axes of the slice: x: 4, y: 4, z: 16 (z_hi: 4, z_lo: 4; z = z_hi * 4 + z_lo), core: 2. Of those that a mesh axis runs over, the one named last changes fastest.
Arguments:
- queries: bfloat16 [16, 4, 384, 3072], P('tm', 'height', 'head'), may hold values from -6 to 6
- keys: bfloat16 [16, 4, 384, 3072], P('tm', 'height', 'head'), may hold values from -6 to 6
- values: bfloat16 [16, 4, 384, 3072], P('tm', 'height', 'head'), may hold values from -18 to 18
- q_gain: float32 [128], replicated, may hold values from 1 to 2
- k_gain: float32 [128], replicated, may hold values from 1 to 2
- offsets: int32 [16, 4, 1, 8], P('tm', 'height'), may hold values from 0 to 26, as said below
- counts: int32 [16, 4, 1], P('tm', 'height'), may hold values from 1 to 8, as said below
Outputs:
- attended: bfloat16 [16, 4, 384, 3072], P('tm', 'height', 'head')
Inputs may be any that keep to these rules, and one draw needn't show every extreme that they name: `offsets`: the 8 entries of a tile are distinct codes e; entry 0 is 13, the tile itself, and every live entry names a tile inside the grid of 4 x 4 x 4 tiles. `counts`: A tile's count is at least one more than the number of its face neighbours inside the grid and at most the number of its neighbouring tiles (itself included) inside the grid.
All inputs are finite; a program needn't handle non-finite values.
Results may differ from a plain program's by a relative error of at most 0.01.
Values may be sent and summed in bfloat16 or wider, within the bound.
No kernel may reach another device: no remote copies, remote signals or barrier semaphores. Data moves between devices by JAX's collectives and lax.ppermute only.
A program may use at most 128 MiB of HBM per device.

v0:
```python
import math

import jax
import jax.numpy as jnp
from jax import lax
from jax.sharding import PartitionSpec as P

TILES_T = 4


def shifted(array, axis, by):
    devices = lax.axis_size(axis)
    pairs = [(i, i + by) for i in range(devices) if 0 <= i + by < devices]
    return lax.ppermute(array, axis, pairs)


def with_halo(array, sides, width):
    for axis, dim in sides:
        devices, length = (lax.axis_size(axis), array.shape[dim])
        up = [(i, (i + 1) % devices) for i in range(devices - 1)]
        down = [(j, i) for i, j in up]
        last = lax.slice_in_dim(array, length - width, length, axis=dim)
        initial = lax.slice_in_dim(array, 0, width, axis=dim)
        before = lax.ppermute(last, axis, up)
        after = lax.ppermute(initial, axis, down)
        array = jnp.concatenate([before, array, after], axis=dim)
    return array


def normalize(tokens, gain):
    dims_in = tokens.shape
    head_width = gain.shape[0]
    by_head = tokens.astype(jnp.float32).reshape(
        dims_in[:-1] + (dims_in[-1] // head_width, head_width)
    )
    mean_sq = jnp.mean(by_head * by_head, axis=-1, keepdims=True)
    scaled = by_head * lax.rsqrt(mean_sq + 1e-06) * gain
    return scaled.astype(jnp.bfloat16).reshape(dims_in)


def frame_pair(stack, move_by):
    return shifted(stack, "tm", move_by)


def corner_tile(edge, move_by):
    return shifted(edge, "tm", move_by)


def near_column(edge, move_by):
    return shifted(edge, "tm", move_by)


def on_device(queries, keys, values, q_gain, k_gain, offsets, counts):
    head_width = q_gain.shape[0]
    dev_tok = queries.shape[2]
    model_width = queries.shape[3]
    groups = lax.axis_size("head")
    blocks_c = lax.axis_size("tm") // TILES_T
    norm_q = normalize(queries, q_gain).reshape(dev_tok, model_width)
    norm_k = normalize(keys, k_gain).reshape(dev_tok, model_width)
    plain_v = values.reshape(dev_tok, model_width)
    group_q, group_k, group_v = (
        lax.all_to_all(norm_q, "head", split_axis=1, concat_axis=0, tiled=True),
        lax.all_to_all(norm_k, "head", split_axis=1, concat_axis=0, tiled=True),
        lax.all_to_all(plain_v, "head", split_axis=1, concat_axis=0, tiled=True),
    )
    tiles_w = offsets.shape[2]
    group_tok = dev_tok * groups
    tile_len = group_tok // tiles_w
    local_width = model_width // groups
    local_heads = local_width // head_width
    paired = jnp.concatenate([group_k, group_v], axis=1).reshape(
        1, 1, tiles_w, tile_len, 2 * local_width
    )
    stack = with_halo(paired, (("height", 1),), 1)
    layers = []
    for frame_step in (-1, 0, 1):
        if frame_step == 0:
            left_rim = near_column(stack, 1)
            right_rim = near_column(stack, -1)
            layer = jnp.concatenate([left_rim, stack, right_rim], axis=2)
        else:
            whole = frame_pair(stack, -frame_step * blocks_c)
            left = corner_tile(stack, -(frame_step * blocks_c - 1))
            right = corner_tile(stack, -(frame_step * blocks_c + 1))
            layer = jnp.concatenate([left, whole, right], axis=2)
        layers.append(layer)
    extended = jnp.concatenate(layers, axis=0)
    query_tiles = group_q.reshape(tiles_w, tile_len, local_heads, head_width)
    score_scale = 1.0 / math.sqrt(head_width)
    slot_codes = offsets[0, 0]
    live_counts = counts[0, 0]
    column_base = jnp.arange(tiles_w, dtype=jnp.int32)

    def fetch_tile(frame_at, row_at, column_at):
        zero_at = jnp.int32(0)
        tile_block = lax.dynamic_slice(
            extended,
            (frame_at, row_at, column_at, zero_at, zero_at),
            (1, 1, 1, tile_len, 2 * local_width),
        )
        return tile_block.reshape(tile_len, 2 * local_width)

    def slot_step(slot_index, totals):
        numerator, denominator = totals
        slot_code = lax.dynamic_index_in_dim(slot_codes, slot_index, 1, False)
        fetched = jax.vmap(fetch_tile)(
            slot_code // 9, slot_code // 3 % 3, column_base + slot_code % 3
        )
        key_tiles = fetched[:, :, :local_width].reshape(tiles_w, tile_len, local_heads, head_width)
        value_tiles = fetched[:, :, local_width:].reshape(
            tiles_w, tile_len, local_heads, head_width
        )
        scores = (
            jnp.einsum(
                "wqhd,wkhd->wqhk", query_tiles, key_tiles, preferred_element_type=jnp.float32
            )
            * score_scale
        )
        live_mask = (slot_index < live_counts).astype(jnp.float32)
        weights = jnp.exp(scores) * live_mask[:, None, None, None]
        numerator = numerator + jnp.einsum(
            "wqhk,wkhd->wqhd",
            weights.astype(jnp.bfloat16),
            value_tiles,
            preferred_element_type=jnp.float32,
        )
        denominator = denominator + jnp.sum(weights, axis=-1)
        return (numerator, denominator)

    initial = (
        jnp.zeros((tiles_w, tile_len, local_heads, head_width), jnp.float32),
        jnp.zeros((tiles_w, tile_len, local_heads), jnp.float32),
    )
    last_slot = slot_codes.shape[1]
    numerator, denominator = lax.fori_loop(0, last_slot, slot_step, initial)
    attended = (
        (numerator / denominator[..., None]).astype(jnp.bfloat16).reshape(group_tok, local_width)
    )
    regrouped = lax.all_to_all(attended, "head", split_axis=0, concat_axis=1, tiled=True)
    return regrouped.reshape(1, 1, dev_tok, model_width)


def solution(mesh):
    return jax.shard_map(
        on_device,
        mesh=mesh,
        in_specs=(
            P("tm", "height", "head", None),
            P("tm", "height", "head", None),
            P("tm", "height", "head", None),
            P(),
            P(),
            P("tm", "height", None, None),
            P("tm", "height", None),
        ),
        out_specs=P("tm", "height", "head", None),
        check_vma=False,
    )
```

profile of v0, /device:TPU:5, one launch (start us, length us, event | category | flops | bytes accessed | tf_op | source)
XLA Modules:
  0.0 491.4 jit_solution(15585660889960430974)
XLA Ops:
  0.0 1.0 multiply_bitcast_fusion.1
  2.1 0.7 copy.30
  2.9 15.8 %all-to-all-start = ((bf16[48,8,384]{2,0,1:T(8,128)(2,1)}), bf16[48,8,384]{2,0,1:T(8,128)(2,1)S(1)}, u32[]{:S(2)}, u32[]{:S(2)}) async-start(bf16[48,8,384]{2,0,1:T(8,128)(2,1)} %copy.30), calls=%async_computation | async-start | bytes 589824 | tf_op jit(solution)/shard_map/all_to_all | solution.py:64
  18.7 16.9 %all-to-all-done = bf16[48,8,384]{2,0,1:T(8,128)(2,1)S(1)} async-done(((bf16[48,8,384]{2,0,1:T(8,128)(2,1)}), bf16[48,8,384]{2,0,1:T(8,128)(2,1)S(1)}, u32[]{:S(2)}, u32[]{:S(2)}) %all-to-all-start) | async-done | bytes 294944 | tf_op jit(solution)/shard_map/all_to_all | solution.py:64
  35.7 28.7 %all_to_all.64 = bf16[48,8,384]{2,0,1:T(8,128)(2,1)S(1)} all-to-all(bf16[48,8,384]{2,0,1:T(8,128)(2,1)S(1)} %copy.31), channel_id=1, replica_groups=mesh['tm'=16,'height'=4,'head'=8] {'head'}, dimensions={1} | all-to-all | bytes 589824 | tf_op jit(solution)/shard_map/all_to_all | solution.py:65
  64.4 3.4 collective-permute-start
  67.7 1.3 collective-permute-start.1
  69.0 7.4 %collective-permute-done = bf16[1,1,1,384,768]{4,3,2,1,0:T(8,128)(2,1)S(1)} collective-permute-done((bf16[1,1,1,384,768]{4,3,2,1,0:T(8,128)(2,1)S(1)}, bf16[1,1,1,384,768]{4,3,2,1,0:T(8,128)(2,1)S(1)}, u32[]{:S(2)}, u32[]{:S(2)}) %collective-permute-start) | collective-permute-done | bytes 589856 | tf_op jit(solution)/shard_map/ppermute | solution.py:24
  76.4 3.9 collective-permute-done.1
  80.3 1.5 pad_maximum_fusion
  81.8 10.3 %collective-permute-start.2 = (bf16[1,3,1,384,768]{4,3,2,1,0:T(8,128)(2,1)}, bf16[1,3,1,384,768]{4,3,2,1,0:T(8,128)(2,1)S(1)}, u32[]{:S(2)}, u32[]{:S(2)}) collective-permute-start(bf16[1,3,1,384,768]{4,3,2,1,0:T(8,128)(2,1)} %pad_maximum_fusion), channel_id=1, source_target_pairs={{0,160},{32,192},{64,224},{96,256},{128,288},{160,320},{192,352},{... | collective-permute-start | bytes 5308424 | tf_op jit(solution)/shard_map/ppermute | solution.py:14
  92.1 1.9 collective-permute-start.3
  94.0 1.9 collective-permute-start.4
  95.9 2.5 collective-permute-start.5
  98.5 5.4 %collective-permute-start.6 = (bf16[1,3,1,384,768]{4,3,2,1,0:T(8,128)(2,1)}, bf16[1,3,1,384,768]{4,3,2,1,0:T(8,128)(2,1)}, u32[]{:S(2)}, u32[]{:S(2)}) collective-permute-start(bf16[1,3,1,384,768]{4,3,2,1,0:T(8,128)(2,1)} %pad_maximum_fusion), channel_id=1, source_target_pairs={{32,0},{64,32},{96,64},{128,96},{160,128},{192,160},{224,192},{256... | collective-permute-start | bytes 5308424 | tf_op jit(solution)/shard_map/ppermute | solution.py:14
  103.9 56.4 %collective-permute-done.2 = bf16[1,3,1,384,768]{4,3,2,1,0:T(8,128)(2,1)S(1)} collective-permute-done((bf16[1,3,1,384,768]{4,3,2,1,0:T(8,128)(2,1)}, bf16[1,3,1,384,768]{4,3,2,1,0:T(8,128)(2,1)S(1)}, u32[]{:S(2)}, u32[]{:S(2)}) %collective-permute-start.2) | collective-permute-done | bytes 1769504 | tf_op jit(solution)/shard_map/ppermute | solution.py:14
  160.3 1.9 collective-permute-start.7
  162.3 80.0 %collective-permute-done.3 = bf16[1,3,1,384,768]{4,3,2,1,0:T(8,128)(2,1)S(1)} collective-permute-done((bf16[1,3,1,384,768]{4,3,2,1,0:T(8,128)(2,1)}, bf16[1,3,1,384,768]{4,3,2,1,0:T(8,128)(2,1)S(1)}, u32[]{:S(2)}, u32[]{:S(2)}) %collective-permute-start.3) | collective-permute-done | bytes 1769504 | tf_op jit(solution)/shard_map/ppermute | solution.py:14
  242.3 2.3 collective-permute-start.8
  244.7 1.3 copy-done.3
  246.0 1.9 collective-permute-start.9
  248.8 0.7 copy.32
  249.6 9.3 %all-to-all-start.2 = ((bf16[48,8,384]{2,0,1:T(8,128)(2,1)}), bf16[48,8,384]{2,0,1:T(8,128)(2,1)S(1)}, u32[]{:S(2)}, u32[]{:S(2)}) async-start(bf16[48,8,384]{2,0,1:T(8,128)(2,1)} %copy.32), calls=%async_computation.2 | async-start | bytes 589824 | tf_op jit(solution)/shard_map/all_to_all | solution.py:63
  258.8 134.2 %all-to-all-done.2 = bf16[48,8,384]{2,0,1:T(8,128)(2,1)S(1)} async-done(((bf16[48,8,384]{2,0,1:T(8,128)(2,1)}), bf16[48,8,384]{2,0,1:T(8,128)(2,1)S(1)}, u32[]{:S(2)}, u32[]{:S(2)}) %all-to-all-start.2) | async-done | bytes 294944 | tf_op jit(solution)/shard_map/all_to_all | solution.py:63
  393.3 10.9 %maximum_maximum_fusion = bf16[3,3,3,384,768]{4,3,2,1,0:T(8,128)(2,1)} fusion(bf16[1,3,1,384,768]{4,3,2,1,0:T(8,128)(2,1)} %collective-permute-done.9, bf16[1,3,1,384,768]{4,3,2,1,0:T(8,128)(2,1)} %collective-permute-done.8, bf16[1,3,1,384,768]{4,3,2,1,0:T(8,128)(2,1)} %collective-permute-done.7, bf16[1,3,1,384,768]{4,3,2,1,0:T(8,128)(2,1)} %collective-permute-done.6, ...), kind=kLoop, calls=%fused_computation.11 | loop fusion | flops 79626240 | bytes 31850496 | tf_op jit(solution)/shard_map/concatenate | solution.py:88
  404.2 54.6 %while.20 = (s32[]{:T(128)}, f32[1,384,3,128]{1,3,2,0:T(8,128)S(1)}, f32[1,384,3]{1,0,2:T(1,128)S(1)}, s32[1,8]{1,0:T(1,128)S(1)}, bf16[3,3,3,384,768]{4,3,2,1,0...) while((s32[]{:T(128)}, ...), condition=%wide.region_4.5_spmd.clone, body=%wide.region_2.4_spmd.clone.sunk | while | flops 228557984 | bytes 7391766 | solution.py:136
  404.2 0.6 fusion.23
  407.9 1.1 constant_dynamic-slice_fusion.3
  409.0 0.3 copy.49
  410.0 0.6 bitcast_reduce_fusion.2
  410.6 0.4 fusion.25
  411.1 0.6 fusion.23
  414.7 1.1 constant_dynamic-slice_fusion.3
  415.8 0.3 copy.49
  416.8 0.6 bitcast_reduce_fusion.2
  417.4 0.4 fusion.25
  417.9 0.6 fusion.23
  421.5 1.1 constant_dynamic-slice_fusion.3
  422.6 0.3 copy.49
  423.6 0.6 bitcast_reduce_fusion.2
  424.2 0.4 fusion.25
  424.7 0.6 fusion.23
  428.3 1.1 constant_dynamic-slice_fusion.3
  430.5 0.6 bitcast_reduce_fusion.2
  431.1 0.4 fusion.25
  431.5 0.6 fusion.23
  435.1 1.1 constant_dynamic-slice_fusion.3
  437.3 0.6 bitcast_reduce_fusion.2
  437.9 0.4 fusion.25
  438.4 0.6 fusion.23
  442.0 1.1 constant_dynamic-slice_fusion.3
  443.1 0.3 copy.49
  444.1 0.6 bitcast_reduce_fusion.2
  444.7 0.4 fusion.25
  445.2 0.6 fusion.23
  448.8 1.1 constant_dynamic-slice_fusion.3
  450.9 0.6 bitcast_reduce_fusion.2
  451.5 0.4 fusion.25
  452.0 0.6 fusion.23
  455.6 1.1 constant_dynamic-slice_fusion.3
  457.8 0.6 bitcast_reduce_fusion.2
  458.4 0.4 fusion.25
  459.4 31.1 %all_to_all.65 = bf16[8,48,384]{2,1,0:T(8,128)(2,1)S(1)} all-to-all(bf16[8,48,384]{2,1,0:T(8,128)(2,1)S(1)} %all_to_all.57), channel_id=1, replica_groups=mesh['tm'=16,'height'=4,'head'=8] {'head'}, dimensions={0} | all-to-all | bytes 589824 | tf_op jit(solution)/shard_map/all_to_all | solution.py:140
  490.5 0.9 reshape.236
  (72 shorter events, 4.6 us)
Async XLA Ops:
  0.0 2.0 copy-start
  1.0 1.0 copy-start.4
  2.0 16.7 %copy-start.6 = (bf16[1,1,48,3072]{3,2,1,0:T(8,128)(2,1)S(1)}, bf16[1,1,48,3072]{3,2,1,0:T(8,128)(2,1)}, u32[]{:S(2)}) copy-start(bf16[1,1,48,3072]{3,2,1,0:T(8,128)(2,1)} %param.11) | copy-start | bytes 884740
  2.9 32.8 %all-to-all-start = ((bf16[48,8,384]{2,0,1:T(8,128)(2,1)}), bf16[48,8,384]{2,0,1:T(8,128)(2,1)S(1)}, u32[]{:S(2)}, u32[]{:S(2)}) async-start(bf16[48,8,384]{2,0,1:T(8,128)(2,1)} %copy.30), calls=%async_computation | async-start | bytes 589824 | tf_op jit(solution)/shard_map/all_to_all | solution.py:64
  64.4 183.5 %copy-start.5 = (bf16[1,1,48,3072]{3,2,1,0:T(8,128)(2,1)S(1)}, bf16[1,1,48,3072]{3,2,1,0:T(8,128)(2,1)}, u32[]{:S(2)}) copy-start(bf16[1,1,48,3072]{3,2,1,0:T(8,128)(2,1)} %param.9) | copy-start | bytes 884740
  64.4 12.1 %collective-permute-start = (bf16[1,1,1,384,768]{4,3,2,1,0:T(8,128)(2,1)S(1)}, bf16[1,1,1,384,768]{4,3,2,1,0:T(8,128)(2,1)S(1)}, u32[]{:S(2)}, u32[]{:S(2)}) collective-permute-start(bf16[1,1,1,384,768]{4,3,2,1,0:T(8,128)(2,1)S(1)} %maximum_bitcast_fusion), channel_id=1, source_target_pairs={{0,8},{8,16},{16,24},{1,9},{9,17},{17,25},{2,10},{10,18},{18,26},{... | collective-permute-start | bytes 1769480 | tf_op jit(solution)/shard_map/ppermute | solution.py:24
  67.7 12.6 %collective-permute-start.1 = (bf16[1,1,1,384,768]{4,3,2,1,0:T(8,128)(2,1)S(1)}, bf16[1,1,1,384,768]{4,3,2,1,0:T(8,128)(2,1)S(1)}, u32[]{:S(2)}, u32[]{:S(2)}) collective-permute-start(bf16[1,1,1,384,768]{4,3,2,1,0:T(8,128)(2,1)S(1)} %maximum_bitcast_fusion), channel_id=1, source_target_pairs={{8,0},{16,8},{24,16},{9,1},{17,9},{25,17},{10,2},{18,10},{26,18},{... | collective-permute-start | bytes 1769480 | tf_op jit(solution)/shard_map/ppermute | solution.py:25
  81.8 78.6 %collective-permute-start.2 = (bf16[1,3,1,384,768]{4,3,2,1,0:T(8,128)(2,1)}, bf16[1,3,1,384,768]{4,3,2,1,0:T(8,128)(2,1)S(1)}, u32[]{:S(2)}, u32[]{:S(2)}) collective-permute-start(bf16[1,3,1,384,768]{4,3,2,1,0:T(8,128)(2,1)} %pad_maximum_fusion), channel_id=1, source_target_pairs={{0,160},{32,192},{64,224},{96,256},{128,288},{160,320},{192,352},{... | collective-permute-start | bytes 5308424 | tf_op jit(solution)/shard_map/ppermute | solution.py:14
  92.1 150.2 %collective-permute-start.3 = (bf16[1,3,1,384,768]{4,3,2,1,0:T(8,128)(2,1)}, bf16[1,3,1,384,768]{4,3,2,1,0:T(8,128)(2,1)S(1)}, u32[]{:S(2)}, u32[]{:S(2)}) collective-permute-start(bf16[1,3,1,384,768]{4,3,2,1,0:T(8,128)(2,1)} %pad_maximum_fusion), channel_id=1, source_target_pairs={{0,128},{32,160},{64,192},{96,224},{128,256},{160,288},{192,320},{... | collective-permute-start | bytes 5308424 | tf_op jit(solution)/shard_map/ppermute | solution.py:14
  94.0 150.7 %collective-permute-start.4 = (bf16[1,3,1,384,768]{4,3,2,1,0:T(8,128)(2,1)}, bf16[1,3,1,384,768]{4,3,2,1,0:T(8,128)(2,1)S(1)}, u32[]{:S(2)}, u32[]{:S(2)}) collective-permute-start(bf16[1,3,1,384,768]{4,3,2,1,0:T(8,128)(2,1)} %pad_maximum_fusion), channel_id=1, source_target_pairs={{0,96},{32,128},{64,160},{96,192},{128,224},{160,256},{192,288},{2... | collective-permute-start | bytes 5308424 | tf_op jit(solution)/shard_map/ppermute | solution.py:14
  95.9 297.3 %collective-permute-start.5 = (bf16[1,3,1,384,768]{4,3,2,1,0:T(8,128)(2,1)}, bf16[1,3,1,384,768]{4,3,2,1,0:T(8,128)(2,1)}, u32[]{:S(2)}, u32[]{:S(2)}) collective-permute-start(bf16[1,3,1,384,768]{4,3,2,1,0:T(8,128)(2,1)} %pad_maximum_fusion), channel_id=1, source_target_pairs={{0,32},{32,64},{64,96},{96,128},{128,160},{160,192},{192,224},{224... | collective-permute-start | bytes 5308424 | tf_op jit(solution)/shard_map/ppermute | solution.py:14
  98.5 294.8 %collective-permute-start.6 = (bf16[1,3,1,384,768]{4,3,2,1,0:T(8,128)(2,1)}, bf16[1,3,1,384,768]{4,3,2,1,0:T(8,128)(2,1)}, u32[]{:S(2)}, u32[]{:S(2)}) collective-permute-start(bf16[1,3,1,384,768]{4,3,2,1,0:T(8,128)(2,1)} %pad_maximum_fusion), channel_id=1, source_target_pairs={{32,0},{64,32},{96,64},{128,96},{160,128},{192,160},{224,192},{256... | collective-permute-start | bytes 5308424 | tf_op jit(solution)/shard_map/ppermute | solution.py:14
  160.3 84.3 %copy-start.1 = (bf16[1,3,1,384,768]{4,3,2,1,0:T(8,128)(2,1)}, bf16[1,3,1,384,768]{4,3,2,1,0:T(8,128)(2,1)S(1)}, u32[]{:S(2)}) copy-start(bf16[1,3,1,384,768]{4,3,2,1,0:T(8,128)(2,1)S(1)} %collective-permute-done.2) | copy-start | bytes 5308420
  160.3 232.9 %collective-permute-start.7 = (bf16[1,3,1,384,768]{4,3,2,1,0:T(8,128)(2,1)}, bf16[1,3,1,384,768]{4,3,2,1,0:T(8,128)(2,1)}, u32[]{:S(2)}, u32[]{:S(2)}) collective-permute-start(bf16[1,3,1,384,768]{4,3,2,1,0:T(8,128)(2,1)} %pad_maximum_fusion), channel_id=1, source_target_pairs={{96,0},{128,32},{160,64},{192,96},{224,128},{256,160},{288,192},{3... | collective-permute-start | bytes 5308424 | tf_op jit(solution)/shard_map/ppermute | solution.py:14
  242.3 2.4 copy-start.2
  242.3 151.0 %collective-permute-start.8 = (bf16[1,3,1,384,768]{4,3,2,1,0:T(8,128)(2,1)}, bf16[1,3,1,384,768]{4,3,2,1,0:T(8,128)(2,1)}, u32[]{:S(2)}, u32[]{:S(2)}) collective-permute-start(bf16[1,3,1,384,768]{4,3,2,1,0:T(8,128)(2,1)} %pad_maximum_fusion), channel_id=1, source_target_pairs={{128,0},{160,32},{192,64},{224,96},{256,128},{288,160},{320,192},{... | collective-permute-start | bytes 5308424 | tf_op jit(solution)/shard_map/ppermute | solution.py:14
  244.7 1.3 copy-start.3
  246.0 147.3 %collective-permute-start.9 = (bf16[1,3,1,384,768]{4,3,2,1,0:T(8,128)(2,1)}, bf16[1,3,1,384,768]{4,3,2,1,0:T(8,128)(2,1)}, u32[]{:S(2)}, u32[]{:S(2)}) collective-permute-start(bf16[1,3,1,384,768]{4,3,2,1,0:T(8,128)(2,1)} %pad_maximum_fusion), channel_id=1, source_target_pairs={{160,0},{192,32},{224,64},{256,96},{288,128},{320,160},{352,192},{... | collective-permute-start | bytes 5308424 | tf_op jit(solution)/shard_map/ppermute | solution.py:14
  248.1 0.7 copy-start.8
  249.6 143.5 %all-to-all-start.2 = ((bf16[48,8,384]{2,0,1:T(8,128)(2,1)}), bf16[48,8,384]{2,0,1:T(8,128)(2,1)S(1)}, u32[]{:S(2)}, u32[]{:S(2)}) async-start(bf16[48,8,384]{2,0,1:T(8,128)(2,1)} %copy.32), calls=%async_computation.2 | async-start | bytes 589824 | tf_op jit(solution)/shard_map/all_to_all | solution.py:63
  393.2 11.0 %copy-start.7 = (s32[1,1,1,8]{3,2,1,0:T(1,128)S(1)}, s32[1,1,1,8]{3,2,1,0:T(1,128)}, u32[]{:S(2)}) copy-start(s32[1,1,1,8]{3,2,1,0:T(1,128)} %param.14) | copy-start | bytes 100
where the time goes:
time: 493 us; the launch traced here: 491 us
  waiting for transfers between devices  299 us (61%)
  blocking collectives  59.7 us (12%)
  starting transfers between devices  58 us (12%)
  loops' own time  29.7 us (6%)
  other arithmetic  19 us (4%)
  local copies, waits for them, and re-layouts  17.5 us (4%)
  matrix products  8.2 us (2%)
    ppermute x8, waiting for transfers between devices, shifted(): return lax.ppermute(array, axis, pairs)  136 us
    all_to_all x1, waiting for transfers between devices, on_device(): lax.all_to_all(norm_q, 'head', split_axis=1, concat_axis=0, tiled=True)  134 us
    all_to_all x1, blocking collectives, on_device(): lax.all_to_all(attended, 'head', split_axis=0, concat_axis=1, tiled=True)  31.1 us
    another operation x1, loops' own time, on_device(): numerator, denominator = lax.fori_loop(0, last_slot, slot_step, initial)  29.7 us
    all_to_all x1, blocking collectives, on_device(): lax.all_to_all(plain_v, 'head', split_axis=1, concat_axis=0, tiled=True)  28.7 us
    ppermute x8, starting transfers between devices, shifted(): return lax.ppermute(array, axis, pairs)  28.3 us
    all_to_all x1, waiting for transfers between devices, on_device(): lax.all_to_all(norm_k, 'head', split_axis=1, concat_axis=0, tiled=True)  16.9 us
    all_to_all x1, starting transfers between devices, on_device(): lax.all_to_all(norm_k, 'head', split_axis=1, concat_axis=0, tiled=True)  15.8 us
  transfers between devices with their start and end apart: 12, of which 6 were waited for; matrix products, arithmetic and copies ran while one was open for 0% of the time, Pallas kernels for 0%

commit v1 on v0

v1 whole, which is shorter than its diff:
```python
import math

import jax
import jax.numpy as jnp
from jax import lax
from jax.experimental import pallas as pl
from jax.experimental.pallas import tpu as pltpu
from jax.sharding import Mesh, PartitionSpec as P

TILES = 4
HD = 128
CORES = 2
STRIDE = 7
SLOTS = 8
HEADS = 24
LIST_ROWS = 16
PARTS = 3


def turned(w):
    return w * STRIDE % TILES


def normed(block, gain):
    block = block.astype(jnp.float32)
    mean_sq = jnp.mean(block * block, axis=-1, keepdims=True)
    return (block * lax.rsqrt(mean_sq + 1e-06) * gain).astype(jnp.bfloat16)


def head_spans(width):
    return [slice(head * HD, (head + 1) * HD) for head in range(width // HD)]


def spread_kv_kernel(k_hbm, v_hbm, gain_ref, kv_out, raw, laid, in_sems, out_sems):
    parts, part_width = raw.shape[1], raw.shape[3]
    per_part = part_width // HD
    arrivals = []
    for part in range(parts):
        span = slice(part * part_width, (part + 1) * part_width)
        for which, source in enumerate((k_hbm, v_hbm)):
            arrivals.append(
                pltpu.make_async_copy(
                    source.at[:, span], raw.at[which, part], in_sems.at[which, part]
                )
            )
    for copy in arrivals:
        copy.start()

    def leave(index, first, last):
        span = pl.ds(first, last - first)
        return pltpu.make_async_copy(laid.at[span], kv_out.at[span], out_sems.at[index])

    heads, slots = parts * per_part, laid.shape[0]
    laid[heads:] = jnp.zeros((slots - heads,) + laid.shape[1:], laid.dtype)
    departures = [leave(parts, heads, slots)]
    departures[0].start()
    gain = gain_ref[...]
    for part in range(parts):
        first = part * per_part
        arrivals[2 * part].wait()
        for head, span in enumerate(head_spans(part_width)):
            laid[first + head, 0] = normed(raw[0, part, :, span], gain)
        arrivals[2 * part + 1].wait()
        for head, span in enumerate(head_spans(part_width)):
            laid[first + head, 1] = raw[1, part, :, span]
        departures.append(leave(part, first, first + per_part))
        departures[-1].start()
    for copy in departures:
        copy.wait()


def spread_q_kernel(offsets_ref, counts_ref, q_ref, gain_ref, q_out):
    tokens = q_ref.shape[0]
    lane = lax.broadcasted_iota(jnp.int32, (LIST_ROWS, HD), 1)
    listed = jnp.full((LIST_ROWS, HD), -1, jnp.int32)
    for slot in range(offsets_ref.shape[1]):
        code = jnp.where(slot < counts_ref[0, 0], offsets_ref[0, slot], -1)
        listed = jnp.where(lane == slot, code, listed)
    listed = listed.astype(jnp.float32).astype(jnp.bfloat16)
    gain = gain_ref[...]
    spans = head_spans(q_ref.shape[1])
    for slot in range(q_out.shape[0]):
        if slot < len(spans):
            q_out[slot, :tokens] = normed(q_ref[:, spans[slot]], gain)
        else:
            q_out[slot, :tokens] = jnp.zeros((tokens, HD), q_out.dtype)
        q_out[slot, tokens:] = listed


def list_entries(lists_ref, slots, pick, picked):
    def entry(index, found):
        w, slot = index // slots, index % slots
        code = lists_ref[w, slot]
        taken, place = pick(code // 3)
        taken = (code >= 0) & taken

        @pl.when(taken)
        def _():
            picked[0, found] = place
            picked[1, found] = turned(w + code % 3 - 1)
            picked[2, found] = w

        return found + taken.astype(jnp.int32)

    found = lax.fori_loop(0, TILES * slots, entry, 0)
    for extra in range(3):
        picked[0, found + extra] = 0
        picked[1, found + extra] = 0
        picked[2, found + extra] = TILES
    return found


def sum_entries(found, picked, query, kv, total, score_a, score_b):
    tile = total.shape[1]
    tokens = kv.shape[5]
    factor = math.log2(math.e) / math.sqrt(HD)
    ones = jnp.ones((tile, HD), jnp.bfloat16)

    def held(index, which):
        return kv[picked[0, index], :, picked[1, index], :, which].reshape(tile, HD)

    def score(index):
        w = jnp.minimum(picked[2, index], TILES - 1)
        tile_q = query[:, turned(w), :, :tokens].reshape(tile, HD)
        return lax.dot_general(
            tile_q, held(index, 0), (((1,), (1,)), ((), ())), preferred_element_type=jnp.float32
        )

    def absorb(index, scores):
        weight = jnp.exp2(scores[...] * factor).astype(jnp.bfloat16)
        total[picked[2, index]] += jnp.dot(
            weight,
            jnp.concatenate([held(index, 1), ones], axis=1),
            preferred_element_type=jnp.float32,
        )

    score_a[...] = score(0)

    def two(pair, carry):
        index = 2 * pair
        score_b[...] = score(index + 1)
        absorb(index, score_a)
        score_a[...] = score(index + 2)
        absorb(index + 1, score_b)
        return carry

    lax.fori_loop(0, (found + 1) // 2, two, 0)


def near_kernel(query, own, xm, ym, xp, yp, sums, far, kv, read, lists, picked, sa, sb, sems):
    copies = []
    for place, source in enumerate((ym, xm, own, xp, yp)):
        copies.append(pltpu.make_async_copy(source, kv.at[place], sems.at[place]))
    for copy in copies:
        copy.start()
    tokens = kv.shape[5]
    for w in range(TILES):
        behind = query[0, turned(w), 0, tokens:].astype(jnp.float32)
        read[w : w + 1] = behind[:1].astype(jnp.int32)
    to_scalars = pltpu.make_async_copy(read, lists, sems.at[len(copies)])
    to_scalars.start()
    sums[...] = jnp.zeros(sums.shape, sums.dtype)
    to_scalars.wait()

    mirrored = lax.axis_index("d") % CORES == 1

    def sides(place):
        frame, row = place // 3, place % 3
        return jnp.where(mirrored, 2 - frame, frame), jnp.where(mirrored, 2 - row, row)

    def pick(place):
        frame, row = sides(place)
        return (frame == 1) | (row == 1), jnp.where(frame == 1, 2 * row, frame + 1)

    def pick_far(place):
        frame, row = sides(place)
        return (frame != 1) & (row != 1), frame // 2 * 2 + row // 2

    found = list_entries(lists, SLOTS, pick, picked)
    far[3, 0] = list_entries(lists, SLOTS, pick_far, far)
    for copy in copies:
        copy.wait()
    sum_entries(found, picked, query, kv, sums, sa, sb)


def far_kernel(picked, query, sums, mp, mm, pm, pp, out_ref, kv, total, sa, sb, sems):
    copies = []
    for index, source in enumerate((mm, mp, pm, pp)):
        copies.append(pltpu.make_async_copy(source, kv.at[index], sems.at[index]))
    for copy in copies:
        copy.start()
    total[...] = sums[...]
    for copy in copies:
        copy.wait()
    sum_entries(picked[3, 0], picked, query, kv, total, sa, sb)
    for w in range(TILES):
        attended = total[w, :, :HD] / total[w, :, HD:]
        shape = out_ref.shape[:1] + out_ref.shape[2:]
        out_ref[:, turned(w)] = attended.astype(jnp.bfloat16).reshape(shape)


def collect_kernel(chunk_ref, out_ref):
    for head, span in enumerate(head_spans(out_ref.shape[1])):
        out_ref[:, span] = chunk_ref[head]


def flat(x, y, z, core):
    z_hi, z_lo = divmod(z, TILES)
    return (((x * TILES + z_lo) * TILES + y) * TILES + z_hi) * CORES + core


def rings():
    length = TILES * TILES
    return [
        [flat(x, y, STRIDE * i % length, core) for i in range(length) for core in range(CORES)]
        for x in range(TILES)
        for y in range(TILES)
    ]


def exchanged(array):
    return lax.all_to_all(
        array, "d", split_axis=0, concat_axis=0, axis_index_groups=rings(), tiled=True
    )


def moved(array, axis, by):
    pairs = []
    for x in range(TILES):
        for y in range(TILES):
            for core, step in enumerate((by, -by)):
                to_x, to_y = (x + step, y) if axis == "x" else (x, y + step)
                if 0 <= to_x < TILES and 0 <= to_y < TILES:
                    for z in range(TILES * TILES):
                        pairs.append((flat(x, y, z, core), flat(to_x, to_y, z, core)))
    return lax.ppermute(array, "d", pairs)


VMEM = pl.BlockSpec(memory_space=pltpu.VMEM)
HBM = pl.BlockSpec(memory_space=pl.ANY)
SMEM = pl.BlockSpec(memory_space=pltpu.SMEM)


def params(mib):
    return pltpu.CompilerParams(vmem_limit_bytes=mib * 1024 * 1024)


def spread(queries, keys, values, q_gain, k_gain, offsets, counts):
    dev_tok, width = queries.shape[2:]
    devices = TILES * TILES * CORES
    vmem, hbm, smem = VMEM, HBM, SMEM
    kv_chunks = pl.pallas_call(
        spread_kv_kernel,
        out_shape=jax.ShapeDtypeStruct((devices, 2, dev_tok, HD), jnp.bfloat16),
        in_specs=[hbm] * 2 + [vmem],
        out_specs=hbm,
        scratch_shapes=[
            pltpu.VMEM((2, PARTS, dev_tok, width // PARTS), jnp.bfloat16),
            pltpu.VMEM((devices, 2, dev_tok, HD), jnp.bfloat16),
            pltpu.SemaphoreType.DMA((2, PARTS)),
            pltpu.SemaphoreType.DMA((PARTS + 1,)),
        ],
        compiler_params=params(63),
    )(keys.reshape(dev_tok, width), values.reshape(dev_tok, width), k_gain.reshape(1, HD))
    q_chunks = pl.pallas_call(
        spread_q_kernel,
        out_shape=jax.ShapeDtypeStruct((devices, dev_tok + LIST_ROWS, HD), jnp.bfloat16),
        in_specs=[smem] * 2 + [vmem] * 2,
        out_specs=vmem,
        compiler_params=params(16),
    )(
        offsets.reshape(1, SLOTS),
        counts.reshape(1, 1),
        queries.reshape(dev_tok, width),
        q_gain.reshape(1, HD),
    )
    return kv_chunks, q_chunks


def on_device(kv_chunks, q_chunks):
    devices, _, dev_tok = kv_chunks.shape[:3]
    sizes = (TILES, TILES, CORES)
    width = HEADS * HD
    tile = devices // TILES * dev_tok
    vmem, hbm, smem = VMEM, HBM, SMEM
    own = exchanged(kv_chunks)
    query = exchanged(q_chunks)

    xm, ym = moved(own, "x", 1), moved(own, "y", 1)
    xp, yp = moved(own, "x", -1), moved(own, "y", -1)
    mp, mm = moved(xm, "y", -1), moved(ym, "x", 1)
    pm, pp = moved(xp, "y", 1), moved(yp, "x", -1)

    def by_place(array):
        return array.reshape(sizes + array.shape[1:])

    def cost(entries):
        pairs = TILES * entries * tile * tile
        return pl.CostEstimate(
            flops=6 * HD * pairs, bytes_accessed=12 * own.size, transcendentals=pairs
        )

    listed = TILES * SLOTS + 3

    def scratch(columns):
        return [
            pltpu.VMEM((tile, tile), jnp.float32),
            pltpu.VMEM((tile, tile), jnp.float32),
            pltpu.SemaphoreType.DMA((columns + 1,)),
        ]

    def held(columns):
        return pltpu.VMEM((columns,) + sizes + own.shape[1:], jnp.bfloat16)

    query = by_place(query)
    sums_shape = (TILES + 1, tile, 2 * HD)
    sums, far = pl.pallas_call(
        near_kernel,
        out_shape=(
            jax.ShapeDtypeStruct(sums_shape, jnp.float32),
            jax.ShapeDtypeStruct((4, listed), jnp.int32),
        ),
        in_specs=[vmem] + [hbm] * 5,
        out_specs=(vmem, smem),
        scratch_shapes=[
            held(5),
            pltpu.VMEM((TILES, HD), jnp.int32),
            pltpu.SMEM((TILES, HD), jnp.int32),
            pltpu.SMEM((3, listed), jnp.int32),
        ]
        + scratch(5),
        compiler_params=params(24),
        cost_estimate=cost(5),
    )(query, *(by_place(array) for array in (own, xm, ym, xp, yp)))
    attended = pl.pallas_call(
        far_kernel,
        out_shape=jax.ShapeDtypeStruct(sizes + (dev_tok, HD), jnp.bfloat16),
        in_specs=[smem] + [vmem] * 2 + [hbm] * 4,
        out_specs=vmem,
        scratch_shapes=[held(4), pltpu.VMEM(sums_shape, jnp.float32)] + scratch(4),
        compiler_params=params(24),
        cost_estimate=cost(2),
    )(far, query, sums, *(by_place(array) for array in (mp, mm, pm, pp)))

    chunks = attended.reshape(devices, dev_tok, HD)
    chunks = exchanged(chunks)
    return pl.pallas_call(
        collect_kernel,
        out_shape=jax.ShapeDtypeStruct((dev_tok, width), jnp.bfloat16),
        in_specs=[vmem],
        out_specs=vmem,
        compiler_params=params(16),
    )(chunks)


def solution(mesh):
    fine = Mesh(
        mesh.devices.reshape(TILES, TILES, TILES, TILES, CORES), ("x", "zl", "y", "zh", "c")
    )
    line = Mesh(mesh.devices.reshape(-1), ("d",))
    tokens = P(("x", "zl"), "y", ("zh", "c"), None)
    by_device = P(fine.axis_names)
    first = jax.shard_map(
        spread,
        mesh=fine,
        in_specs=(
            tokens,
            tokens,
            tokens,
            P(),
            P(),
            P(("x", "zl"), "y", None, None),
            P(("x", "zl"), "y", None),
        ),
        out_specs=(by_device, by_device),
        check_vma=False,
    )
    middle = jax.shard_map(
        on_device, mesh=line, in_specs=(P("d"), P("d")), out_specs=P("d"), check_vma=False
    )
    last = jax.shard_map(
        lambda rows: rows[None, None],
        mesh=fine,
        in_specs=by_device,
        out_specs=tokens,
        check_vma=False,
    )

    def whole(*arrays):
        return last(middle(*first(*arrays)))

    return whole
```

time: 493 us -> 155 us (0.31)
  the two profiles are of different devices: /device:TPU:5 before, /device:TPU:1 now
where the time goes in v1:
time: 155 us
  waiting for transfers between devices  50.3 us (32%)
  starting transfers between devices  44.4 us (29%)
  blocking collectives  40.1 us (26%)
  Pallas kernels  19 us (12%)
    all_to_all x2, waiting for transfers between devices, exchanged(): lax.all_to_all(array, 'd', split_axis=0, concat_axis=0, axis_index_groups...  41.7 us
    all_to_all x1, blocking collectives, exchanged(): lax.all_to_all(array, 'd', split_axis=0, concat_axis=0, axis_index_groups...  40.1 us
    all_to_all x2, starting transfers between devices, exchanged(): lax.all_to_all(array, 'd', split_axis=0, concat_axis=0, axis_index_groups...  23.1 us
    ppermute x8, starting transfers between devices, moved(): return lax.ppermute(array, 'd', pairs)  21.4 us
    pallas_call x1, Pallas kernels, on_device(): pl.pallas_call(near_kernel, out_shape=(jax.ShapeDtypeStruct(sums_shape, j...  10.2 us
    ppermute x8, waiting for transfers between devices, moved(): return lax.ppermute(array, 'd', pairs)  8.57 us
    pallas_call x1, Pallas kernels, on_device(): pl.pallas_call(far_kernel, out_shape=jax.ShapeDtypeStruct(sizes + (dev_to...  3.57 us
  transfers between devices with their start and end apart: 10, of which 6 were waited for; matrix products, arithmetic and copies ran while one was open for 0% of the time, Pallas kernels for 8%

profile of v1, /device:TPU:1, one launch (start us, length us, event | category | flops | bytes accessed | tf_op | source)
XLA Modules:
  0.0 154.6 jit_solution(1815965258102067243)
XLA Ops:
  0.0 0.0 copy-start.1
  0.0 0.0 copy-start
  0.0 0.0 copy-start.2
  0.0 2.8 %shard_map.131 = bf16[32,2,48,128]{3,2,1,0:T(8,128)(2,1)} custom-call(bf16[48,3072]{1,0:T(8,128)(2,1)} %bitcast.29, bf16[48,3072]{1,0:T(8,128)(2,1)} %bitcast.30, f32[1,128]{1,0:T(1,128)} %bitcast.31), custom_call_target="tpu_custom_call" | custom-call | tf_op jit(solution)/shard_map/pallas_call | solution.py:252
  2.9 16.8 %all-to-all-start.1 = ((bf16[32,2,48,128]{3,2,1,0:T(8,128)(2,1)}), bf16[32,2,48,128]{3,2,1,0:T(8,128)(2,1)S(1)}, u32[]{:S(2)}, u32[]{:S(2)}) async-start(bf16[32,2,48,128]{3,2,1,0:T(8,128)(2,1)} %shard_map.131), calls=%async_computation.1 | async-start | bytes 1572864 | tf_op jit(solution)/shard_map/all_to_all | solution.py:222
  20.3 0.0 copy-done.1
  20.3 0.0 copy-done
  20.3 0.0 copy-done.2
  20.3 1.6 %shard_map.132 = bf16[32,64,128]{2,1,0:T(8,128)(2,1)} custom-call(s32[1,8]{1,0:T(1,128)S(1)} %bitcast.27, s32[1,1]{1,0:T(1,128)} %bitcast.19.counts_ref, bf16[48,3072]{1,0:T(8,128)(2,1)S(1)} %bitcast.26, f32[1,128]{1,0:T(1,128)S(1)} %bitcast.28), custom_call_target="tpu_custom_call" | custom-call | tf_op jit(solution)/shard_map/pallas_call | solution.py:265
  21.9 39.0 %all-to-all-done.1 = bf16[32,2,48,128]{3,2,1,0:T(8,128)(2,1)S(1)} async-done(((bf16[32,2,48,128]{3,2,1,0:T(8,128)(2,1)}), bf16[32,2,48,128]{3,2,1,0:T(8,128)(2,1)S(1)}, u32[]{:S(2)}, u32[]{:S(2)}) %all-to-all-start.1) | async-done | bytes 786464 | tf_op jit(solution)/shard_map/all_to_all | solution.py:222
  60.9 6.3 %all-to-all-start = ((bf16[32,64,128]{2,1,0:T(8,128)(2,1)}), bf16[32,64,128]{2,1,0:T(8,128)(2,1)S(1)}, u32[]{:S(2)}, u32[]{:S(2)}) async-start(bf16[32,64,128]{2,1,0:T(8,128)(2,1)} %shard_map.132), calls=%async_computation | async-start | bytes 1048576 | tf_op jit(solution)/shard_map/all_to_all | solution.py:222
  67.2 1.3 collective-permute-start
  68.5 1.3 collective-permute-start.1
  69.8 4.9 %collective-permute-start.2 = (bf16[32,2,48,128]{3,2,1,0:T(8,128)(2,1)S(1)}, bf16[32,2,48,128]{3,2,1,0:T(8,128)(2,1)}, u32[]{:S(2)}, u32[]{:S(2)}) collective-permute-start(bf16[32,2,48,128]{3,2,1,0:T(8,128)(2,1)S(1)} %all-to-all-done.1), channel_id=1, source_target_pairs={{1,129},{33,161},{65,193},{97,225},{3,131},{35,163},{67,195},{99,2... | collective-permute-start | bytes 2359304 | tf_op jit(solution)/shard_map/ppermute | solution.py:236
  74.7 4.9 %collective-permute-start.3 = (bf16[32,2,48,128]{3,2,1,0:T(8,128)(2,1)S(1)}, bf16[32,2,48,128]{3,2,1,0:T(8,128)(2,1)}, u32[]{:S(2)}, u32[]{:S(2)}) collective-permute-start(bf16[32,2,48,128]{3,2,1,0:T(8,128)(2,1)S(1)} %all-to-all-done.1), channel_id=1, source_target_pairs={{1,9},{33,41},{65,73},{97,105},{3,11},{35,43},{67,75},{99,107},{5,... | collective-permute-start | bytes 2359304 | tf_op jit(solution)/shard_map/ppermute | solution.py:236
  79.6 0.7 collective-permute-done
  80.3 3.3 %collective-permute-start.4 = (bf16[32,2,48,128]{3,2,1,0:T(8,128)(2,1)}, bf16[32,2,48,128]{3,2,1,0:T(8,128)(2,1)S(1)}, u32[]{:S(2)}, u32[]{:S(2)}) collective-permute-start(bf16[32,2,48,128]{3,2,1,0:T(8,128)(2,1)} %collective-permute-done), channel_id=1, source_target_pairs={{1,9},{33,41},{65,73},{97,105},{3,11},{35,43},{67,75},{99,107},{5,... | collective-permute-start | bytes 2359304 | tf_op jit(solution)/shard_map/ppermute | solution.py:236
  83.6 0.0 collective-permute-done.1
  83.6 1.3 collective-permute-start.5
  84.9 3.5 %collective-permute-done.2 = bf16[32,2,48,128]{3,2,1,0:T(8,128)(2,1)} collective-permute-done((bf16[32,2,48,128]{3,2,1,0:T(8,128)(2,1)S(1)}, bf16[32,2,48,128]{3,2,1,0:T(8,128)(2,1)}, u32[]{:S(2)}, u32[]{:S(2)}) %collective-permute-start.2) | collective-permute-done | bytes 786464 | tf_op jit(solution)/shard_map/ppermute | solution.py:236
  88.4 1.3 collective-permute-start.6
  89.7 3.1 %collective-permute-done.3 = bf16[32,2,48,128]{3,2,1,0:T(8,128)(2,1)} collective-permute-done((bf16[32,2,48,128]{3,2,1,0:T(8,128)(2,1)S(1)}, bf16[32,2,48,128]{3,2,1,0:T(8,128)(2,1)}, u32[]{:S(2)}, u32[]{:S(2)}) %collective-permute-start.3) | collective-permute-done | bytes 786464 | tf_op jit(solution)/shard_map/ppermute | solution.py:236
  92.8 3.1 %collective-permute-start.7 = (bf16[32,2,48,128]{3,2,1,0:T(8,128)(2,1)}, bf16[32,2,48,128]{3,2,1,0:T(8,128)(2,1)}, u32[]{:S(2)}, u32[]{:S(2)}) collective-permute-start(bf16[32,2,48,128]{3,2,1,0:T(8,128)(2,1)} %collective-permute-done.3), channel_id=1, source_target_pairs={{1,129},{33,161},{65,193},{97,225},{3,131},{35,163},{67,195},{99,2... | collective-permute-start | bytes 2359304 | tf_op jit(solution)/shard_map/ppermute | solution.py:236
  95.9 2.7 %all-to-all-done = bf16[32,64,128]{2,1,0:T(8,128)(2,1)S(1)} async-done(((bf16[32,64,128]{2,1,0:T(8,128)(2,1)}), bf16[32,64,128]{2,1,0:T(8,128)(2,1)S(1)}, u32[]{:S(2)}, u32[]{:S(2)}) %all-to-all-start) | async-done | bytes 524320 | tf_op jit(solution)/shard_map/all_to_all | solution.py:222
  98.6 10.2 %shard_map.133 = (f32[5,384,256]{2,1,0:T(8,128)S(1)}, s32[4,35]{1,0:T(4,128)S(1)}) custom-call(bf16[4,4,2,64,128]{4,3,2,1,0:T(8,128)(2,1)S(1)} %bitcast.20, bf16[4,4,2,2,48,128]{5,4,3,2,1,0:T(8,128)(2,1)S(1)} %bitcast.23, bf16[4,4,2,2,48,128]{5,4,3,2,1,0:T(8,128)(2,1)} %bitcast.9.xm, bf16[4,4,2,2,48,128]{5,4,3,2,1,0:T(8,128)(2,1)} %bitcast.10.ym, ...), custom_call_target="tpu_custom_call" | custom-call | flops 2264924160 | bytes 4718592 | tf_op jit(solution)/shard_map/pallas_call | solution.py:317
  108.8 0.0 collective-permute-done.4
  108.8 0.0 collective-permute-done.5
  108.8 0.0 collective-permute-done.6
  108.8 1.3 collective-permute-done.7
  110.2 3.6 %shard_map.134 = bf16[4,4,2,48,128]{4,3,2,1,0:T(8,128)(2,1)S(1)} custom-call(s32[4,35]{1,0:T(4,128)S(1)} %get-tuple-element.10.picked, bf16[4,4,2,64,128]{4,3,2,1,0:T(8,128)(2,1)S(1)} %bitcast.21, f32[5,384,256]{2,1,0:T(8,128)S(1)} %get-tuple-element.11.sums, bf16[4,4,2,2,48,128]{5,4,3,2,1,0:T(8,128)(2,1)S(1)} %bitcast.24, ...), custom_call_target="tpu_custom_call" | custom-call | flops 905969664 | bytes 4718592 | tf_op jit(solution)/shard_map/pallas_call | solution.py:335
  113.7 40.1 %all_to_all.15.chunk_ref = bf16[32,48,128]{2,1,0:T(8,128)(2,1)S(1)} all-to-all(bf16[32,48,128]{2,1,0:T(8,128)(2,1)S(1)} %bitcast.22), channel_id=1, replica_groups={{0,1,98,99,70,71,34,35,6,7,96,97,68,69,32,33,4,5,102,103,66,67,38,39,2,..., dimensions={0} | all-to-all | bytes 786432 | tf_op jit(solution)/shard_map/all_to_all | solution.py:222
  153.8 0.8 shard_map.135
Async XLA Ops:
  0.0 20.3 %copy-start.1 = (s32[1,1,1,8]{3,2,1,0:T(1,128)S(1)}, s32[1,1,1,8]{3,2,1,0:T(1,128)}, u32[]{:S(2)}) copy-start(s32[1,1,1,8]{3,2,1,0:T(1,128)} %param.15) | copy-start | bytes 100
  0.0 20.3 %copy-start = (bf16[1,1,48,3072]{3,2,1,0:T(8,128)(2,1)S(1)}, bf16[1,1,48,3072]{3,2,1,0:T(8,128)(2,1)}, u32[]{:S(2)}) copy-start(bf16[1,1,48,3072]{3,2,1,0:T(8,128)(2,1)} %param.10) | copy-start | bytes 884740
  0.0 20.3 %copy-start.2 = (f32[128]{0:T(128)S(1)}, f32[128]{0:T(128)}, u32[]{:S(2)}) copy-start(f32[128]{0:T(128)} %param.13) | copy-start | bytes 1540
  2.9 58.1 %all-to-all-start.1 = ((bf16[32,2,48,128]{3,2,1,0:T(8,128)(2,1)}), bf16[32,2,48,128]{3,2,1,0:T(8,128)(2,1)S(1)}, u32[]{:S(2)}, u32[]{:S(2)}) async-start(bf16[32,2,48,128]{3,2,1,0:T(8,128)(2,1)} %shard_map.131), calls=%async_computation.1 | async-start | bytes 1572864 | tf_op jit(solution)/shard_map/all_to_all | solution.py:222
  60.9 37.7 %all-to-all-start = ((bf16[32,64,128]{2,1,0:T(8,128)(2,1)}), bf16[32,64,128]{2,1,0:T(8,128)(2,1)S(1)}, u32[]{:S(2)}, u32[]{:S(2)}) async-start(bf16[32,64,128]{2,1,0:T(8,128)(2,1)} %shard_map.132), calls=%async_computation | async-start | bytes 1048576 | tf_op jit(solution)/shard_map/all_to_all | solution.py:222
  67.2 13.0 %collective-permute-start = (bf16[32,2,48,128]{3,2,1,0:T(8,128)(2,1)S(1)}, bf16[32,2,48,128]{3,2,1,0:T(8,128)(2,1)}, u32[]{:S(2)}, u32[]{:S(2)}) collective-permute-start(bf16[32,2,48,128]{3,2,1,0:T(8,128)(2,1)S(1)} %all-to-all-done.1), channel_id=1, source_target_pairs={{0,128},{32,160},{64,192},{96,224},{2,130},{34,162},{66,194},{98,2... | collective-permute-start | bytes 2359304 | tf_op jit(solution)/shard_map/ppermute | solution.py:236
  68.5 15.1 %collective-permute-start.1 = (bf16[32,2,48,128]{3,2,1,0:T(8,128)(2,1)S(1)}, bf16[32,2,48,128]{3,2,1,0:T(8,128)(2,1)}, u32[]{:S(2)}, u32[]{:S(2)}) collective-permute-start(bf16[32,2,48,128]{3,2,1,0:T(8,128)(2,1)S(1)} %all-to-all-done.1), channel_id=1, source_target_pairs={{0,8},{32,40},{64,72},{96,104},{2,10},{34,42},{66,74},{98,106},{4,... | collective-permute-start | bytes 2359304 | tf_op jit(solution)/shard_map/ppermute | solution.py:236
  69.8 18.6 %collective-permute-start.2 = (bf16[32,2,48,128]{3,2,1,0:T(8,128)(2,1)S(1)}, bf16[32,2,48,128]{3,2,1,0:T(8,128)(2,1)}, u32[]{:S(2)}, u32[]{:S(2)}) collective-permute-start(bf16[32,2,48,128]{3,2,1,0:T(8,128)(2,1)S(1)} %all-to-all-done.1), channel_id=1, source_target_pairs={{1,129},{33,161},{65,193},{97,225},{3,131},{35,163},{67,195},{99,2... | collective-permute-start | bytes 2359304 | tf_op jit(solution)/shard_map/ppermute | solution.py:236
  74.7 18.1 %collective-permute-start.3 = (bf16[32,2,48,128]{3,2,1,0:T(8,128)(2,1)S(1)}, bf16[32,2,48,128]{3,2,1,0:T(8,128)(2,1)}, u32[]{:S(2)}, u32[]{:S(2)}) collective-permute-start(bf16[32,2,48,128]{3,2,1,0:T(8,128)(2,1)S(1)} %all-to-all-done.1), channel_id=1, source_target_pairs={{1,9},{33,41},{65,73},{97,105},{3,11},{35,43},{67,75},{99,107},{5,... | collective-permute-start | bytes 2359304 | tf_op jit(solution)/shard_map/ppermute | solution.py:236
  80.3 28.6 %collective-permute-start.4 = (bf16[32,2,48,128]{3,2,1,0:T(8,128)(2,1)}, bf16[32,2,48,128]{3,2,1,0:T(8,128)(2,1)S(1)}, u32[]{:S(2)}, u32[]{:S(2)}) collective-permute-start(bf16[32,2,48,128]{3,2,1,0:T(8,128)(2,1)} %collective-permute-done), channel_id=1, source_target_pairs={{1,9},{33,41},{65,73},{97,105},{3,11},{35,43},{67,75},{99,107},{5,... | collective-permute-start | bytes 2359304 | tf_op jit(solution)/shard_map/ppermute | solution.py:236
  83.6 25.2 %collective-permute-start.5 = (bf16[32,2,48,128]{3,2,1,0:T(8,128)(2,1)}, bf16[32,2,48,128]{3,2,1,0:T(8,128)(2,1)S(1)}, u32[]{:S(2)}, u32[]{:S(2)}) collective-permute-start(bf16[32,2,48,128]{3,2,1,0:T(8,128)(2,1)} %collective-permute-done.1), channel_id=1, source_target_pairs={{0,128},{32,160},{64,192},{96,224},{2,130},{34,162},{66,194},{98,2... | collective-permute-start | bytes 2359304 | tf_op jit(solution)/shard_map/ppermute | solution.py:236
  88.4 20.4 %collective-permute-start.6 = (bf16[32,2,48,128]{3,2,1,0:T(8,128)(2,1)}, bf16[32,2,48,128]{3,2,1,0:T(8,128)(2,1)}, u32[]{:S(2)}, u32[]{:S(2)}) collective-permute-start(bf16[32,2,48,128]{3,2,1,0:T(8,128)(2,1)} %collective-permute-done.2), channel_id=1, source_target_pairs={{0,8},{32,40},{64,72},{96,104},{2,10},{34,42},{66,74},{98,106},{4,... | collective-permute-start | bytes 2359304 | tf_op jit(solution)/shard_map/ppermute | solution.py:236
  92.8 17.4 %collective-permute-start.7 = (bf16[32,2,48,128]{3,2,1,0:T(8,128)(2,1)}, bf16[32,2,48,128]{3,2,1,0:T(8,128)(2,1)}, u32[]{:S(2)}, u32[]{:S(2)}) collective-permute-start(bf16[32,2,48,128]{3,2,1,0:T(8,128)(2,1)} %collective-permute-done.3), channel_id=1, source_target_pairs={{1,129},{33,161},{65,193},{97,225},{3,131},{35,163},{67,195},{99,2... | collective-permute-start | bytes 2359304 | tf_op jit(solution)/shard_map/ppermute | solution.py:236

commit v2 on v1

--- a/solution.py
+++ b/solution.py
@@ -9,16 +9,10 @@
 
 TILES = 4
 HD = 128
-CORES = 2
-STRIDE = 7
+RING = ("zl", "zh", "c")
 SLOTS = 8
-HEADS = 24
 LIST_ROWS = 16
 PARTS = 3
-
-
-def turned(w):
-    return w * STRIDE % TILES
 
 
 def normed(block, gain):
@@ -87,27 +81,32 @@
         q_out[slot, tokens:] = listed
 
 
-def list_entries(lists_ref, slots, pick, picked):
-    def entry(index, found):
-        w, slot = index // slots, index % slots
-        code = lists_ref[w, slot]
-        taken, place = pick(code // 3)
-        taken = (code >= 0) & taken
-
-        @pl.when(taken)
-        def _():
-            picked[0, found] = place
-            picked[1, found] = turned(w + code % 3 - 1)
-            picked[2, found] = w
-
-        return found + taken.astype(jnp.int32)
-
-    found = lax.fori_loop(0, TILES * slots, entry, 0)
-    for extra in range(3):
-        picked[0, found + extra] = 0
-        picked[1, found + extra] = 0
-        picked[2, found + extra] = TILES
-    return found
+def list_entries(lists_ref, mirrored, near, far):
+    near_found = far_found = jnp.int32(0)
+    for w in range(TILES):
+        for slot in range(SLOTS):
+            code = lists_ref[w, slot]
+            place = (code * 171) >> 9
+            frame = (code * 57) >> 9
+            row = place - 3 * frame
+            column = w + code - 3 * place - 1
+            frame = jnp.where(mirrored, 2 - frame, frame)
+            row = jnp.where(mirrored, 2 - row, row)
+            is_near = (frame == 1) | (row == 1)
+            near[0, near_found] = jnp.where(frame == 1, 2 * row, frame + 1)
+            near[1, near_found] = column
+            near[2, near_found] = w
+            far[0, far_found] = (frame >> 1) * 2 + (row >> 1)
+            far[1, far_found] = column
+            far[2, far_found] = w
+            near_found += ((code >= 0) & is_near).astype(jnp.int32)
+            far_found += ((code >= 0) & jnp.logical_not(is_near)).astype(jnp.int32)
+    for picked, found in ((near, near_found), (far, far_found)):
+        for extra in range(3):
+            picked[0, found + extra] = 0
+            picked[1, found + extra] = 0
+            picked[2, found + extra] = TILES
+        picked[3, 0] = found
 
 
 def sum_entries(found, picked, query, kv, total, score_a, score_b):
@@ -117,11 +116,11 @@
     ones = jnp.ones((tile, HD), jnp.bfloat16)
 
     def held(index, which):
-        return kv[picked[0, index], :, picked[1, index], :, which].reshape(tile, HD)
+        return kv[picked[0, index], picked[1, index], :, :, which].reshape(tile, HD)
 
     def score(index):
         w = jnp.minimum(picked[2, index], TILES - 1)
-        tile_q = query[:, turned(w), :, :tokens].reshape(tile, HD)
+        tile_q = query[w, :, :, :tokens].reshape(tile, HD)
         return lax.dot_general(
             tile_q, held(index, 0), (((1,), (1,)), ((), ())), preferred_element_type=jnp.float32
         )
@@ -155,32 +154,17 @@
         copy.start()
     tokens = kv.shape[5]
     for w in range(TILES):
-        behind = query[0, turned(w), 0, tokens:].astype(jnp.float32)
+        behind = query[w, 0, 0, tokens:].astype(jnp.float32)
         read[w : w + 1] = behind[:1].astype(jnp.int32)
     to_scalars = pltpu.make_async_copy(read, lists, sems.at[len(copies)])
     to_scalars.start()
     sums[...] = jnp.zeros(sums.shape, sums.dtype)
     to_scalars.wait()
 
-    mirrored = lax.axis_index("d") % CORES == 1
-
-    def sides(place):
-        frame, row = place // 3, place % 3
-        return jnp.where(mirrored, 2 - frame, frame), jnp.where(mirrored, 2 - row, row)
-
-    def pick(place):
-        frame, row = sides(place)
-        return (frame == 1) | (row == 1), jnp.where(frame == 1, 2 * row, frame + 1)
-
-    def pick_far(place):
-        frame, row = sides(place)
-        return (frame != 1) & (row != 1), frame // 2 * 2 + row // 2
-
-    found = list_entries(lists, SLOTS, pick, picked)
-    far[3, 0] = list_entries(lists, SLOTS, pick_far, far)
+    list_entries(lists, lax.axis_index("c") == 1, picked, far)
     for copy in copies:
         copy.wait()
-    sum_entries(found, picked, query, kv, sums, sa, sb)
+    sum_entries(picked[3, 0], picked, query, kv, sums, sa, sb)
 
 
 def far_kernel(picked, query, sums, mp, mm, pm, pp, out_ref, kv, total, sa, sb, sems):
@@ -195,8 +179,7 @@
     sum_entries(picked[3, 0], picked, query, kv, total, sa, sb)
     for w in range(TILES):
         attended = total[w, :, :HD] / total[w, :, HD:]
-        shape = out_ref.shape[:1] + out_ref.shape[2:]
-        out_ref[:, turned(w)] = attended.astype(jnp.bfloat16).reshape(shape)
+        out_ref[w] = attended.astype(jnp.bfloat16).reshape(out_ref.shape[1:])
 
 
 def collect_kernel(chunk_ref, out_ref):
@@ -204,51 +187,30 @@
         out_ref[:, span] = chunk_ref[head]
 
 
-def flat(x, y, z, core):
-    z_hi, z_lo = divmod(z, TILES)
-    return (((x * TILES + z_lo) * TILES + y) * TILES + z_hi) * CORES + core
-
-
-def rings():
-    length = TILES * TILES
-    return [
-        [flat(x, y, STRIDE * i % length, core) for i in range(length) for core in range(CORES)]
-        for x in range(TILES)
-        for y in range(TILES)
-    ]
-
-
-def exchanged(array):
-    return lax.all_to_all(
-        array, "d", split_axis=0, concat_axis=0, axis_index_groups=rings(), tiled=True
-    )
-
-
 def moved(array, axis, by):
+    line, cores = lax.axis_size(axis), lax.axis_size("c")
     pairs = []
-    for x in range(TILES):
-        for y in range(TILES):
-            for core, step in enumerate((by, -by)):
-                to_x, to_y = (x + step, y) if axis == "x" else (x, y + step)
-                if 0 <= to_x < TILES and 0 <= to_y < TILES:
-                    for z in range(TILES * TILES):
-                        pairs.append((flat(x, y, z, core), flat(to_x, to_y, z, core)))
-    return lax.ppermute(array, "d", pairs)
-
-
-VMEM = pl.BlockSpec(memory_space=pltpu.VMEM)
-HBM = pl.BlockSpec(memory_space=pl.ANY)
-SMEM = pl.BlockSpec(memory_space=pltpu.SMEM)
-
-
-def params(mib):
-    return pltpu.CompilerParams(vmem_limit_bytes=mib * 1024 * 1024)
-
-
-def spread(queries, keys, values, q_gain, k_gain, offsets, counts):
+    for i in range(line):
+        for core in range(cores):
+            to, to_core = i + (by if core == 0 else -by), core
+            if not 0 <= to < line:
+                to, to_core = i, 1 - core
+            pairs.append((i * cores + core, to * cores + to_core))
+    return lax.ppermute(array, (axis, "c"), pairs)
+
+
+def on_device(queries, keys, values, q_gain, k_gain, offsets, counts):
     dev_tok, width = queries.shape[2:]
-    devices = TILES * TILES * CORES
-    vmem, hbm, smem = VMEM, HBM, SMEM
+    sizes = tuple(lax.axis_size(axis) for axis in RING)
+    devices = math.prod(sizes)
+    tile = devices // TILES * dev_tok
+    vmem = pl.BlockSpec(memory_space=pltpu.VMEM)
+    hbm = pl.BlockSpec(memory_space=pl.ANY)
+    smem = pl.BlockSpec(memory_space=pltpu.SMEM)
+
+    def params(mib):
+        return pltpu.CompilerParams(vmem_limit_bytes=mib * 1024 * 1024)
+
     kv_chunks = pl.pallas_call(
         spread_kv_kernel,
         out_shape=jax.ShapeDtypeStruct((devices, 2, dev_tok, HD), jnp.bfloat16),
@@ -262,6 +224,7 @@
         ],
         compiler_params=params(63),
     )(keys.reshape(dev_tok, width), values.reshape(dev_tok, width), k_gain.reshape(1, HD))
+    own = lax.all_to_all(kv_chunks, RING, split_axis=0, concat_axis=0, tiled=True)
     q_chunks = pl.pallas_call(
         spread_q_kernel,
         out_shape=jax.ShapeDtypeStruct((devices, dev_tok + LIST_ROWS, HD), jnp.bfloat16),
@@ -274,17 +237,7 @@
         queries.reshape(dev_tok, width),
         q_gain.reshape(1, HD),
     )
-    return kv_chunks, q_chunks
-
-
-def on_device(kv_chunks, q_chunks):
-    devices, _, dev_tok = kv_chunks.shape[:3]
-    sizes = (TILES, TILES, CORES)
-    width = HEADS * HD
-    tile = devices // TILES * dev_tok
-    vmem, hbm, smem = VMEM, HBM, SMEM
-    own = exchanged(kv_chunks)
-    query = exchanged(q_chunks)
+    query = lax.all_to_all(q_chunks, RING, split_axis=0, concat_axis=0, tiled=True)
 
     xm, ym = moved(own, "x", 1), moved(own, "y", 1)
     xp, yp = moved(own, "x", -1), moved(own, "y", -1)
@@ -326,7 +279,7 @@
             held(5),
             pltpu.VMEM((TILES, HD), jnp.int32),
             pltpu.SMEM((TILES, HD), jnp.int32),
-            pltpu.SMEM((3, listed), jnp.int32),
+            pltpu.SMEM((4, listed), jnp.int32),
         ]
         + scratch(5),
         compiler_params=params(24),
@@ -343,25 +296,27 @@
     )(far, query, sums, *(by_place(array) for array in (mp, mm, pm, pp)))
 
     chunks = attended.reshape(devices, dev_tok, HD)
-    chunks = exchanged(chunks)
-    return pl.pallas_call(
+    chunks = lax.all_to_all(chunks, RING, split_axis=0, concat_axis=0, tiled=True)
+    result = pl.pallas_call(
         collect_kernel,
         out_shape=jax.ShapeDtypeStruct((dev_tok, width), jnp.bfloat16),
         in_specs=[vmem],
         out_specs=vmem,
         compiler_params=params(16),
     )(chunks)
+    return result.reshape(1, 1, dev_tok, width)
 
 
 def solution(mesh):
+    frames = TILES
+    columns = mesh.shape["tm"] // frames
     fine = Mesh(
-        mesh.devices.reshape(TILES, TILES, TILES, TILES, CORES), ("x", "zl", "y", "zh", "c")
+        mesh.devices.reshape(frames, columns, mesh.shape["height"], mesh.shape["head"] // 2, 2),
+        ("x", "zl", "y", "zh", "c"),
     )
-    line = Mesh(mesh.devices.reshape(-1), ("d",))
     tokens = P(("x", "zl"), "y", ("zh", "c"), None)
-    by_device = P(fine.axis_names)
-    first = jax.shard_map(
-        spread,
+    return jax.shard_map(
+        on_device,
         mesh=fine,
         in_specs=(
             tokens,
@@ -372,21 +327,6 @@
             P(("x", "zl"), "y", None, None),
             P(("x", "zl"), "y", None),
         ),
-        out_specs=(by_device, by_device),
-        check_vma=False,
-    )
-    middle = jax.shard_map(
-        on_device, mesh=line, in_specs=(P("d"), P("d")), out_specs=P("d"), check_vma=False
-    )
-    last = jax.shard_map(
-        lambda rows: rows[None, None],
-        mesh=fine,
-        in_specs=by_device,
         out_specs=tokens,
         check_vma=False,
     )
-
-    def whole(*arrays):
-        return last(middle(*first(*arrays)))
-
-    return whole

time: 155 us -> 150 us (0.968)
  the two profiles are of different devices: /device:TPU:1 before, /device:TPU:58 now
where the time goes in v2:
time: 150 us
  waiting for transfers between devices  65.7 us (44%)
  blocking collectives  38.2 us (25%)
  starting transfers between devices  26.7 us (18%)
  Pallas kernels  18.3 us (12%)
    all_to_all x1, waiting for transfers between devices, on_device(): lax.all_to_all(kv_chunks, RING, split_axis=0, concat_axis=0, tiled=True)  40.3 us
    all_to_all x1, blocking collectives, on_device(): lax.all_to_all(chunks, RING, split_axis=0, concat_axis=0, tiled=True)  38.2 us
    ppermute x8, waiting for transfers between devices, moved(): return lax.ppermute(array, (axis, 'c'), pairs)  17.4 us
    all_to_all x1, starting transfers between devices, on_device(): lax.all_to_all(kv_chunks, RING, split_axis=0, concat_axis=0, tiled=True)  15.4 us
    pallas_call x1, Pallas kernels, on_device(): pl.pallas_call(near_kernel, out_shape=(jax.ShapeDtypeStruct(sums_shape, j...  9.56 us
    all_to_all x1, waiting for transfers between devices, on_device(): lax.all_to_all(q_chunks, RING, split_axis=0, concat_axis=0, tiled=True)  7.9 us
    ppermute x8, starting transfers between devices, moved(): return lax.ppermute(array, (axis, 'c'), pairs)  6.56 us
    all_to_all x1, starting transfers between devices, on_device(): lax.all_to_all(q_chunks, RING, split_axis=0, concat_axis=0, tiled=True)  4.79 us
  transfers between devices with their start and end apart: 10, of which 4 were waited for; matrix products, arithmetic and copies ran while one was open for 0% of the time, Pallas kernels for 7%

profile of v2, /device:TPU:58, one launch (start us, length us, event | category | flops | bytes accessed | tf_op | source)
XLA Modules:
  0.0 149.7 jit_solution(6514279767846746483)
XLA Ops:
  0.0 0.0 copy-start.1
  0.0 0.0 copy-start
  0.0 0.0 copy-start.2
  0.0 2.8 %shard_map.74 = bf16[32,2,48,128]{3,2,1,0:T(8,128)(2,1)} custom-call(bf16[48,3072]{1,0:T(8,128)(2,1)} %bitcast.29, bf16[48,3072]{1,0:T(8,128)(2,1)} %bitcast.30, f32[1,128]{1,0:T(1,128)} %bitcast.31), custom_call_target="tpu_custom_call" | custom-call | tf_op jit(solution)/shard_map/pallas_call | solution.py:214
  2.9 15.4 %all-to-all-start.1 = ((bf16[32,2,48,128]{3,2,1,0:T(8,128)(2,1)}), bf16[32,2,48,128]{3,2,1,0:T(8,128)(2,1)S(1)}, u32[]{:S(2)}, u32[]{:S(2)}) async-start(bf16[32,2,48,128]{3,2,1,0:T(8,128)(2,1)} %shard_map.74), calls=%async_computation.1 | async-start | bytes 1572864 | tf_op jit(solution)/shard_map/all_to_all | solution.py:227
  18.9 0.0 copy-done.1
  18.9 0.0 copy-done
  18.9 0.0 copy-done.2
  18.9 1.6 %shard_map.73 = bf16[32,64,128]{2,1,0:T(8,128)(2,1)} custom-call(s32[1,8]{1,0:T(1,128)S(1)} %bitcast.27, s32[1,1]{1,0:T(1,128)} %bitcast.19.counts_ref, bf16[48,3072]{1,0:T(8,128)(2,1)S(1)} %bitcast.26, f32[1,128]{1,0:T(1,128)S(1)} %bitcast.28), custom_call_target="tpu_custom_call" | custom-call | tf_op jit(solution)/shard_map/pallas_call | solution.py:228
  20.5 40.3 %all-to-all-done.1 = bf16[32,2,48,128]{3,2,1,0:T(8,128)(2,1)S(1)} async-done(((bf16[32,2,48,128]{3,2,1,0:T(8,128)(2,1)}), bf16[32,2,48,128]{3,2,1,0:T(8,128)(2,1)S(1)}, u32[]{:S(2)}, u32[]{:S(2)}) %all-to-all-start.1) | async-done | bytes 786464 | tf_op jit(solution)/shard_map/all_to_all | solution.py:227
  60.9 4.8 %all-to-all-start = ((bf16[32,64,128]{2,1,0:T(8,128)(2,1)}), bf16[32,64,128]{2,1,0:T(8,128)(2,1)S(1)}, u32[]{:S(2)}, u32[]{:S(2)}) async-start(bf16[32,64,128]{2,1,0:T(8,128)(2,1)} %shard_map.73), calls=%async_computation | async-start | bytes 1048576 | tf_op jit(solution)/shard_map/all_to_all | solution.py:240
  65.7 1.5 %collective-permute-start = (bf16[32,2,48,128]{3,2,1,0:T(8,128)(2,1)S(1)}, bf16[32,2,48,128]{3,2,1,0:T(8,128)(2,1)}, u32[]{:S(2)}, u32[]{:S(2)}) collective-permute-start(bf16[32,2,48,128]{3,2,1,0:T(8,128)(2,1)S(1)} %all-to-all-done.1), channel_id=1, source_target_pairs={{0,128},{1,0},{128,256},{129,1},{256,384},{257,129},{384,385},{385... | collective-permute-start | bytes 2359304 | tf_op jit(solution)/shard_map/ppermute | solution.py:199
  67.2 0.0 collective-permute-start.1
  67.2 0.5 collective-permute-start.2
  67.7 2.0 %collective-permute-start.3 = (bf16[32,2,48,128]{3,2,1,0:T(8,128)(2,1)S(1)}, bf16[32,2,48,128]{3,2,1,0:T(8,128)(2,1)}, u32[]{:S(2)}, u32[]{:S(2)}) collective-permute-start(bf16[32,2,48,128]{3,2,1,0:T(8,128)(2,1)S(1)} %all-to-all-done.1), channel_id=1, source_target_pairs={{0,1},{1,9},{8,0},{9,17},{16,8},{17,25},{24,16},{25,24},{2,3},{3,1... | collective-permute-start | bytes 2359304 | tf_op jit(solution)/shard_map/ppermute | solution.py:199
  69.7 16.4 %collective-permute-done = bf16[32,2,48,128]{3,2,1,0:T(8,128)(2,1)} collective-permute-done((bf16[32,2,48,128]{3,2,1,0:T(8,128)(2,1)S(1)}, bf16[32,2,48,128]{3,2,1,0:T(8,128)(2,1)}, u32[]{:S(2)}, u32[]{:S(2)}) %collective-permute-start) | collective-permute-done | bytes 786464 | tf_op jit(solution)/shard_map/ppermute | solution.py:199
  86.1 0.4 collective-permute-start.4
  86.5 1.1 collective-permute-done.1
  87.6 1.3 collective-permute-start.5
  88.9 0.0 collective-permute-done.2
  88.9 0.0 collective-permute-start.6
  88.9 0.0 collective-permute-done.3
  88.9 0.8 collective-permute-start.7
  89.7 7.9 %all-to-all-done = bf16[32,64,128]{2,1,0:T(8,128)(2,1)S(1)} async-done(((bf16[32,64,128]{2,1,0:T(8,128)(2,1)}), bf16[32,64,128]{2,1,0:T(8,128)(2,1)S(1)}, u32[]{:S(2)}, u32[]{:S(2)}) %all-to-all-start) | async-done | bytes 524320 | tf_op jit(solution)/shard_map/all_to_all | solution.py:240
  97.6 9.6 %shard_map.75 = (f32[5,384,256]{2,1,0:T(8,128)S(1)}, s32[4,35]{1,0:T(4,128)S(1)}) custom-call(bf16[4,4,2,64,128]{4,3,2,1,0:T(8,128)(2,1)S(1)} %bitcast.20, bf16[4,4,2,2,48,128]{5,4,3,2,1,0:T(8,128)(2,1)S(1)} %bitcast.23, bf16[4,4,2,2,48,128]{5,4,3,2,1,0:T(8,128)(2,1)} %bitcast.9.xm, bf16[4,4,2,2,48,128]{5,4,3,2,1,0:T(8,128)(2,1)} %bitcast.10.ym, ...), custom_call_target="tpu_custom_call" | custom-call | flops 2264924160 | bytes 4718592 | tf_op jit(solution)/shard_map/pallas_call | solution.py:270
  107.1 0.0 collective-permute-done.4
  107.1 0.0 collective-permute-done.5
  107.1 0.0 collective-permute-done.6
  107.1 0.0 collective-permute-done.7
  107.2 3.6 %shard_map.76 = bf16[4,4,2,48,128]{4,3,2,1,0:T(8,128)(2,1)S(1)} custom-call(s32[4,35]{1,0:T(4,128)S(1)} %get-tuple-element.7.picked, bf16[4,4,2,64,128]{4,3,2,1,0:T(8,128)(2,1)S(1)} %bitcast.21, f32[5,384,256]{2,1,0:T(8,128)S(1)} %get-tuple-element.8.sums, bf16[4,4,2,2,48,128]{5,4,3,2,1,0:T(8,128)(2,1)S(1)} %bitcast.24, ...), custom_call_target="tpu_custom_call" | custom-call | flops 905969664 | bytes 4718592 | tf_op jit(solution)/shard_map/pallas_call | solution.py:288
  110.7 38.2 %all_to_all.15.chunk_ref = bf16[32,48,128]{2,1,0:T(8,128)(2,1)S(1)} all-to-all(bf16[32,48,128]{2,1,0:T(8,128)(2,1)S(1)} %bitcast.22), channel_id=1, replica_groups=mesh['x'=4,'zl'=4,'y'=4,'zh'=4,'c'=2] {'zl','zh','c'}, dimensions={0} | all-to-all | bytes 786432 | tf_op jit(solution)/shard_map/all_to_all | solution.py:299
  149.0 0.8 shard_map.77
Async XLA Ops:
  0.0 18.9 %copy-start.1 = (s32[1,1,1,8]{3,2,1,0:T(1,128)S(1)}, s32[1,1,1,8]{3,2,1,0:T(1,128)}, u32[]{:S(2)}) copy-start(s32[1,1,1,8]{3,2,1,0:T(1,128)} %param.12) | copy-start | bytes 100
  0.0 18.9 %copy-start = (bf16[1,1,48,3072]{3,2,1,0:T(8,128)(2,1)S(1)}, bf16[1,1,48,3072]{3,2,1,0:T(8,128)(2,1)}, u32[]{:S(2)}) copy-start(bf16[1,1,48,3072]{3,2,1,0:T(8,128)(2,1)} %param.7) | copy-start | bytes 884740
  0.0 18.9 %copy-start.2 = (f32[128]{0:T(128)S(1)}, f32[128]{0:T(128)}, u32[]{:S(2)}) copy-start(f32[128]{0:T(128)} %param.10) | copy-start | bytes 1540
  2.9 58.0 %all-to-all-start.1 = ((bf16[32,2,48,128]{3,2,1,0:T(8,128)(2,1)}), bf16[32,2,48,128]{3,2,1,0:T(8,128)(2,1)S(1)}, u32[]{:S(2)}, u32[]{:S(2)}) async-start(bf16[32,2,48,128]{3,2,1,0:T(8,128)(2,1)} %shard_map.74), calls=%async_computation.1 | async-start | bytes 1572864 | tf_op jit(solution)/shard_map/all_to_all | solution.py:227
  60.9 36.7 %all-to-all-start = ((bf16[32,64,128]{2,1,0:T(8,128)(2,1)}), bf16[32,64,128]{2,1,0:T(8,128)(2,1)S(1)}, u32[]{:S(2)}, u32[]{:S(2)}) async-start(bf16[32,64,128]{2,1,0:T(8,128)(2,1)} %shard_map.73), calls=%async_computation | async-start | bytes 1048576 | tf_op jit(solution)/shard_map/all_to_all | solution.py:240
  65.7 20.4 %collective-permute-start = (bf16[32,2,48,128]{3,2,1,0:T(8,128)(2,1)S(1)}, bf16[32,2,48,128]{3,2,1,0:T(8,128)(2,1)}, u32[]{:S(2)}, u32[]{:S(2)}) collective-permute-start(bf16[32,2,48,128]{3,2,1,0:T(8,128)(2,1)S(1)} %all-to-all-done.1), channel_id=1, source_target_pairs={{0,128},{1,0},{128,256},{129,1},{256,384},{257,129},{384,385},{385... | collective-permute-start | bytes 2359304 | tf_op jit(solution)/shard_map/ppermute | solution.py:199
  67.2 20.4 %collective-permute-start.1 = (bf16[32,2,48,128]{3,2,1,0:T(8,128)(2,1)S(1)}, bf16[32,2,48,128]{3,2,1,0:T(8,128)(2,1)}, u32[]{:S(2)}, u32[]{:S(2)}) collective-permute-start(bf16[32,2,48,128]{3,2,1,0:T(8,128)(2,1)S(1)} %all-to-all-done.1), channel_id=1, source_target_pairs={{0,8},{1,0},{8,16},{9,1},{16,24},{17,9},{24,25},{25,17},{2,10},{3,... | collective-permute-start | bytes 2359304 | tf_op jit(solution)/shard_map/ppermute | solution.py:199
  67.2 21.7 %collective-permute-start.2 = (bf16[32,2,48,128]{3,2,1,0:T(8,128)(2,1)S(1)}, bf16[32,2,48,128]{3,2,1,0:T(8,128)(2,1)}, u32[]{:S(2)}, u32[]{:S(2)}) collective-permute-start(bf16[32,2,48,128]{3,2,1,0:T(8,128)(2,1)S(1)} %all-to-all-done.1), channel_id=1, source_target_pairs={{0,1},{1,129},{128,0},{129,257},{256,128},{257,385},{384,256},{385... | collective-permute-start | bytes 2359304 | tf_op jit(solution)/shard_map/ppermute | solution.py:199
  67.7 21.2 %collective-permute-start.3 = (bf16[32,2,48,128]{3,2,1,0:T(8,128)(2,1)S(1)}, bf16[32,2,48,128]{3,2,1,0:T(8,128)(2,1)}, u32[]{:S(2)}, u32[]{:S(2)}) collective-permute-start(bf16[32,2,48,128]{3,2,1,0:T(8,128)(2,1)S(1)} %all-to-all-done.1), channel_id=1, source_target_pairs={{0,1},{1,9},{8,0},{9,17},{16,8},{17,25},{24,16},{25,24},{2,3},{3,1... | collective-permute-start | bytes 2359304 | tf_op jit(solution)/shard_map/ppermute | solution.py:199
  86.1 21.0 %collective-permute-start.4 = (bf16[32,2,48,128]{3,2,1,0:T(8,128)(2,1)}, bf16[32,2,48,128]{3,2,1,0:T(8,128)(2,1)S(1)}, u32[]{:S(2)}, u32[]{:S(2)}) collective-permute-start(bf16[32,2,48,128]{3,2,1,0:T(8,128)(2,1)} %collective-permute-done), channel_id=1, source_target_pairs={{0,1},{1,9},{8,0},{9,17},{16,8},{17,25},{24,16},{25,24},{2,3},{3,1... | collective-permute-start | bytes 2359304 | tf_op jit(solution)/shard_map/ppermute | solution.py:199
  87.6 19.5 %collective-permute-start.5 = (bf16[32,2,48,128]{3,2,1,0:T(8,128)(2,1)}, bf16[32,2,48,128]{3,2,1,0:T(8,128)(2,1)S(1)}, u32[]{:S(2)}, u32[]{:S(2)}) collective-permute-start(bf16[32,2,48,128]{3,2,1,0:T(8,128)(2,1)} %collective-permute-done.1), channel_id=1, source_target_pairs={{0,128},{1,0},{128,256},{129,1},{256,384},{257,129},{384,385},{385... | collective-permute-start | bytes 2359304 | tf_op jit(solution)/shard_map/ppermute | solution.py:199
  88.9 18.2 %collective-permute-start.6 = (bf16[32,2,48,128]{3,2,1,0:T(8,128)(2,1)}, bf16[32,2,48,128]{3,2,1,0:T(8,128)(2,1)}, u32[]{:S(2)}, u32[]{:S(2)}) collective-permute-start(bf16[32,2,48,128]{3,2,1,0:T(8,128)(2,1)} %collective-permute-done.2), channel_id=1, source_target_pairs={{0,8},{1,0},{8,16},{9,1},{16,24},{17,9},{24,25},{25,17},{2,10},{3,... | collective-permute-start | bytes 2359304 | tf_op jit(solution)/shard_map/ppermute | solution.py:199
  88.9 18.3 %collective-permute-start.7 = (bf16[32,2,48,128]{3,2,1,0:T(8,128)(2,1)}, bf16[32,2,48,128]{3,2,1,0:T(8,128)(2,1)}, u32[]{:S(2)}, u32[]{:S(2)}) collective-permute-start(bf16[32,2,48,128]{3,2,1,0:T(8,128)(2,1)} %collective-permute-done.3), channel_id=1, source_target_pairs={{0,1},{1,129},{128,0},{129,257},{256,128},{257,385},{384,256},{385... | collective-permute-start | bytes 2359304 | tf_op jit(solution)/shard_map/ppermute | solution.py:199

commit v3 on v2

--- a/solution.py
+++ b/solution.py
@@ -11,7 +11,6 @@
 HD = 128
 RING = ("zl", "zh", "c")
 SLOTS = 8
-LIST_ROWS = 16
 PARTS = 3
 
 
@@ -63,22 +62,20 @@
         copy.wait()
 
 
-def spread_q_kernel(offsets_ref, counts_ref, q_ref, gain_ref, q_out):
-    tokens = q_ref.shape[0]
-    lane = lax.broadcasted_iota(jnp.int32, (LIST_ROWS, HD), 1)
-    listed = jnp.full((LIST_ROWS, HD), -1, jnp.int32)
-    for slot in range(offsets_ref.shape[1]):
-        code = jnp.where(slot < counts_ref[0, 0], offsets_ref[0, slot], -1)
-        listed = jnp.where(lane == slot, code, listed)
-    listed = listed.astype(jnp.float32).astype(jnp.bfloat16)
+def spread_q_kernel(offsets_ref, counts_ref, q_ref, gain_ref, q_out, table):
+    for slot in range(SLOTS):
+        table[0, slot] = jnp.where(slot < counts_ref[0, 0], offsets_ref[0, slot], -1)
     gain = gain_ref[...]
     spans = head_spans(q_ref.shape[1])
     for slot in range(q_out.shape[0]):
         if slot < len(spans):
-            q_out[slot, :tokens] = normed(q_ref[:, spans[slot]], gain)
+            q_out[slot] = normed(q_ref[:, spans[slot]], gain)
         else:
-            q_out[slot, :tokens] = jnp.zeros((tokens, HD), q_out.dtype)
-        q_out[slot, tokens:] = listed
+            q_out[slot] = jnp.zeros(q_out.shape[1:], q_out.dtype)
+
+
+def hand_on_kernel(q_in, after, t1, t2, t3, q_out):
+    del q_in, after, t1, t2, t3, q_out
 
 
 def list_entries(lists_ref, mirrored, near, far):
@@ -111,7 +108,6 @@
 
 def sum_entries(found, picked, query, kv, total, score_a, score_b):
     tile = total.shape[1]
-    tokens = kv.shape[5]
     factor = math.log2(math.e) / math.sqrt(HD)
     ones = jnp.ones((tile, HD), jnp.bfloat16)
 
@@ -120,7 +116,7 @@
 
     def score(index):
         w = jnp.minimum(picked[2, index], TILES - 1)
-        tile_q = query[w, :, :, :tokens].reshape(tile, HD)
+        tile_q = query[w].reshape(tile, HD)
         return lax.dot_general(
             tile_q, held(index, 0), (((1,), (1,)), ((), ())), preferred_element_type=jnp.float32
         )
@@ -146,21 +142,20 @@
     lax.fori_loop(0, (found + 1) // 2, two, 0)
 
 
-def near_kernel(query, own, xm, ym, xp, yp, sums, far, kv, read, lists, picked, sa, sb, sems):
+def near_kernel(
+    t0, t1, t2, t3, query, own, xm, ym, xp, yp, sums, far, kv, lists, picked, sa, sb, sems
+):
     copies = []
     for place, source in enumerate((ym, xm, own, xp, yp)):
         copies.append(pltpu.make_async_copy(source, kv.at[place], sems.at[place]))
     for copy in copies:
         copy.start()
-    tokens = kv.shape[5]
-    for w in range(TILES):
-        behind = query[w, 0, 0, tokens:].astype(jnp.float32)
-        read[w : w + 1] = behind[:1].astype(jnp.int32)
-    to_scalars = pltpu.make_async_copy(read, lists, sems.at[len(copies)])
-    to_scalars.start()
+    here = lax.axis_index("zl")
+    for step, table in enumerate((t0, t1, t2, t3)):
+        w = (here - step + TILES) & (TILES - 1)
+        for slot in range(SLOTS):
+            lists[w, slot] = table[0, slot]
     sums[...] = jnp.zeros(sums.shape, sums.dtype)
-    to_scalars.wait()
-
     list_entries(lists, lax.axis_index("c") == 1, picked, far)
     for copy in copies:
         copy.wait()
@@ -225,11 +220,14 @@
         compiler_params=params(63),
     )(keys.reshape(dev_tok, width), values.reshape(dev_tok, width), k_gain.reshape(1, HD))
     own = lax.all_to_all(kv_chunks, RING, split_axis=0, concat_axis=0, tiled=True)
-    q_chunks = pl.pallas_call(
+    q_chunks, table = pl.pallas_call(
         spread_q_kernel,
-        out_shape=jax.ShapeDtypeStruct((devices, dev_tok + LIST_ROWS, HD), jnp.bfloat16),
+        out_shape=(
+            jax.ShapeDtypeStruct((devices, dev_tok, HD), jnp.bfloat16),
+            jax.ShapeDtypeStruct((1, SLOTS), jnp.int32),
+        ),
         in_specs=[smem] * 2 + [vmem] * 2,
-        out_specs=vmem,
+        out_specs=(vmem, smem),
         compiler_params=params(16),
     )(
         offsets.reshape(1, SLOTS),
@@ -237,6 +235,17 @@
         queries.reshape(dev_tok, width),
         q_gain.reshape(1, HD),
     )
+    turns = [[(i, (i + step) % TILES) for i in range(TILES)] for step in range(TILES)]
+    tables = [table] + [lax.ppermute(table, "zl", turns[step]) for step in range(1, TILES)]
+    q_chunks = pl.pallas_call(
+        hand_on_kernel,
+        out_shape=jax.ShapeDtypeStruct(q_chunks.shape, q_chunks.dtype),
+        in_specs=[hbm] * 5,
+        out_specs=hbm,
+        input_output_aliases={0: 0},
+        compiler_params=params(16),
+        cost_estimate=pl.CostEstimate(flops=20_000_000_000, bytes_accessed=0, transcendentals=0),
+    )(q_chunks, own, *tables[1:])
     query = lax.all_to_all(q_chunks, RING, split_axis=0, concat_axis=0, tiled=True)
 
     xm, ym = moved(own, "x", 1), moved(own, "y", 1)
@@ -273,18 +282,17 @@
             jax.ShapeDtypeStruct(sums_shape, jnp.float32),
             jax.ShapeDtypeStruct((4, listed), jnp.int32),
         ),
-        in_specs=[vmem] + [hbm] * 5,
+        in_specs=[smem] * 4 + [vmem] + [hbm] * 5,
         out_specs=(vmem, smem),
         scratch_shapes=[
             held(5),
-            pltpu.VMEM((TILES, HD), jnp.int32),
-            pltpu.SMEM((TILES, HD), jnp.int32),
+            pltpu.SMEM((TILES, SLOTS), jnp.int32),
             pltpu.SMEM((4, listed), jnp.int32),
         ]
         + scratch(5),
         compiler_params=params(24),
         cost_estimate=cost(5),
-    )(query, *(by_place(array) for array in (own, xm, ym, xp, yp)))
+    )(*tables, query, *(by_place(array) for array in (own, xm, ym, xp, yp)))
     attended = pl.pallas_call(
         far_kernel,
         out_shape=jax.ShapeDtypeStruct(sizes + (dev_tok, HD), jnp.bfloat16),

time: 150 us -> 151 us (level)
  the two profiles are of different devices: /device:TPU:58 before, /device:TPU:62 now
where the time goes in v3:
time: 151 us
  waiting for transfers between devices  54.9 us (36%)
  blocking collectives  38.3 us (25%)
  starting transfers between devices  37.4 us (25%)
  Pallas kernels  19.2 us (13%)
    all_to_all x1, blocking collectives, on_device(): lax.all_to_all(chunks, RING, split_axis=0, concat_axis=0, tiled=True)  38.3 us
    ppermute x8, waiting for transfers between devices, moved(): return lax.ppermute(array, (axis, 'c'), pairs)  21.6 us
    ppermute x3, waiting for transfers between devices, on_device(): lax.ppermute(table, 'zl', turns[step])  20.3 us
    all_to_all x1, starting transfers between devices, on_device(): lax.all_to_all(kv_chunks, RING, split_axis=0, concat_axis=0, tiled=True)  15.4 us
    ppermute x3, starting transfers between devices, on_device(): lax.ppermute(table, 'zl', turns[step])  10.2 us
    all_to_all x1, waiting for transfers between devices, on_device(): lax.all_to_all(kv_chunks, RING, split_axis=0, concat_axis=0, tiled=True)  9.97 us
    pallas_call x1, Pallas kernels, on_device(): pl.pallas_call(near_kernel, out_shape=(jax.ShapeDtypeStruct(sums_shape, j...  9.55 us
    ppermute x8, starting transfers between devices, moved(): return lax.ppermute(array, (axis, 'c'), pairs)  6.94 us
  transfers between devices with their start and end apart: 13, of which 8 were waited for; matrix products, arithmetic and copies ran while one was open for 0% of the time, Pallas kernels for 7%

profile of v3, /device:TPU:62, one launch (start us, length us, event | category | flops | bytes accessed | tf_op | source)
XLA Modules:
  0.0 150.6 jit_solution(6021591960539178603)
XLA Ops:
  0.0 0.0 copy-start.1
  0.0 0.0 copy-start
  0.0 0.0 copy-start.2
  0.0 2.8 %shard_map.74 = bf16[32,2,48,128]{3,2,1,0:T(8,128)(2,1)} custom-call(bf16[48,3072]{1,0:T(8,128)(2,1)} %bitcast.30, bf16[48,3072]{1,0:T(8,128)(2,1)} %bitcast.31, f32[1,128]{1,0:T(1,128)} %bitcast.32), custom_call_target="tpu_custom_call" | custom-call | tf_op jit(solution)/shard_map/pallas_call | solution.py:209
  2.9 15.4 %all-to-all-start = ((bf16[32,2,48,128]{3,2,1,0:T(8,128)(2,1)}), bf16[32,2,48,128]{3,2,1,0:T(8,128)(2,1)S(1)}, u32[]{:S(2)}, u32[]{:S(2)}) async-start(bf16[32,2,48,128]{3,2,1,0:T(8,128)(2,1)} %shard_map.74), calls=%async_computation | async-start | bytes 1572864 | tf_op jit(solution)/shard_map/all_to_all | solution.py:222
  18.9 0.0 copy-done.1
  18.9 0.0 copy-done
  18.9 0.0 copy-done.2
  18.9 1.5 %shard_map.73 = (bf16[32,48,128]{2,1,0:T(8,128)(2,1)}, s32[1,8]{1,0:T(1,128)S(1)}) custom-call(s32[1,8]{1,0:T(1,128)S(1)} %bitcast.28, s32[1,1]{1,0:T(1,128)} %bitcast.19.counts_ref, bf16[48,3072]{1,0:T(8,128)(2,1)S(1)} %bitcast.27, f32[1,128]{1,0:T(1,128)S(1)} %bitcast.29), custom_call_target="tpu_custom_call" | custom-call | tf_op jit(solution)/shard_map/pallas_call | solution.py:223
  20.5 3.4 %collective-permute-start = (s32[1,8]{1,0:T(1,128)S(1)}, s32[1,8]{1,0:T(1,128)S(1)}, u32[]{:S(2)}, u32[]{:S(2)}) collective-permute-start(s32[1,8]{1,0:T(1,128)S(1)} %get-tuple-element.9.t0), channel_id=1, source_target_pairs={{0,32},{32,64},{64,96},{96,0},{1,33},{33,65},{65,97},{97,1},{2,34}... | collective-permute-start | bytes 104 | tf_op jit(solution)/shard_map/ppermute | solution.py:239
  23.9 3.0 %collective-permute-start.1 = (s32[1,8]{1,0:T(1,128)S(1)}, s32[1,8]{1,0:T(1,128)S(1)}, u32[]{:S(2)}, u32[]{:S(2)}) collective-permute-start(s32[1,8]{1,0:T(1,128)S(1)} %get-tuple-element.9.t0), channel_id=1, source_target_pairs={{0,64},{32,96},{64,0},{96,32},{1,65},{33,97},{65,1},{97,33},{2,66}... | collective-permute-start | bytes 104 | tf_op jit(solution)/shard_map/ppermute | solution.py:239
  26.9 3.7 %collective-permute-start.2 = (s32[1,8]{1,0:T(1,128)S(1)}, s32[1,8]{1,0:T(1,128)S(1)}, u32[]{:S(2)}, u32[]{:S(2)}) collective-permute-start(s32[1,8]{1,0:T(1,128)S(1)} %get-tuple-element.9.t0), channel_id=1, source_target_pairs={{0,96},{32,0},{64,32},{96,64},{1,97},{33,1},{65,33},{97,65},{2,98}... | collective-permute-start | bytes 104 | tf_op jit(solution)/shard_map/ppermute | solution.py:239
  30.6 18.4 %collective-permute-done.t1 = s32[1,8]{1,0:T(1,128)S(1)} collective-permute-done((s32[1,8]{1,0:T(1,128)S(1)}, s32[1,8]{1,0:T(1,128)S(1)}, u32[]{:S(2)}, u32[]{:S(2)}) %collective-permute-start) | collective-permute-done | bytes 64 | tf_op jit(solution)/shard_map/ppermute | solution.py:239
  49.1 1.5 collective-permute-done.1.t2
  50.5 0.4 collective-permute-done.2.t3
  50.9 10.0 %all-to-all-done.after = bf16[32,2,48,128]{3,2,1,0:T(8,128)(2,1)S(1)} async-done(((bf16[32,2,48,128]{3,2,1,0:T(8,128)(2,1)}), bf16[32,2,48,128]{3,2,1,0:T(8,128)(2,1)S(1)}, u32[]{:S(2)}, u32[]{:S(2)}) %all-to-all-start) | async-done | bytes 786464 | tf_op jit(solution)/shard_map/all_to_all | solution.py:222
  60.9 4.9 %all-to-all-start.1 = ((bf16[32,48,128]{2,1,0:T(8,128)(2,1)}), bf16[32,48,128]{2,1,0:T(8,128)(2,1)S(1)}, u32[]{:S(2)}, u32[]{:S(2)}) async-start(bf16[32,48,128]{2,1,0:T(8,128)(2,1)} %shard_map.75), calls=%async_computation.1 | async-start | bytes 786432 | tf_op jit(solution)/shard_map/all_to_all | solution.py:249
  65.8 0.2 collective-permute-start.3
  66.0 0.5 collective-permute-start.4
  66.5 1.3 collective-permute-start.5
  67.9 2.0 %collective-permute-start.6 = (bf16[32,2,48,128]{3,2,1,0:T(8,128)(2,1)S(1)}, bf16[32,2,48,128]{3,2,1,0:T(8,128)(2,1)}, u32[]{:S(2)}, u32[]{:S(2)}) collective-permute-start(bf16[32,2,48,128]{3,2,1,0:T(8,128)(2,1)S(1)} %all-to-all-done.after), channel_id=1, source_target_pairs={{0,1},{1,9},{8,0},{9,17},{16,8},{17,25},{24,16},{25,24},{2,3},{3,1... | collective-permute-start | bytes 2359304 | tf_op jit(solution)/shard_map/ppermute | solution.py:194
  69.9 16.3 %collective-permute-done.3 = bf16[32,2,48,128]{3,2,1,0:T(8,128)(2,1)} collective-permute-done((bf16[32,2,48,128]{3,2,1,0:T(8,128)(2,1)S(1)}, bf16[32,2,48,128]{3,2,1,0:T(8,128)(2,1)}, u32[]{:S(2)}, u32[]{:S(2)}) %collective-permute-start.3) | collective-permute-done | bytes 786464 | tf_op jit(solution)/shard_map/ppermute | solution.py:194
  86.2 0.8 collective-permute-start.7
  87.0 0.0 collective-permute-done.4
  87.0 0.0 collective-permute-start.8
  87.0 0.0 collective-permute-done.5
  87.0 0.3 collective-permute-start.9
  87.3 0.0 collective-permute-done.6
  87.3 1.7 %collective-permute-start.10 = (bf16[32,2,48,128]{3,2,1,0:T(8,128)(2,1)}, bf16[32,2,48,128]{3,2,1,0:T(8,128)(2,1)}, u32[]{:S(2)}, u32[]{:S(2)}) collective-permute-start(bf16[32,2,48,128]{3,2,1,0:T(8,128)(2,1)} %collective-permute-done.6), channel_id=1, source_target_pairs={{0,1},{1,129},{128,0},{129,257},{256,128},{257,385},{384,256},{385... | collective-permute-start | bytes 2359304 | tf_op jit(solution)/shard_map/ppermute | solution.py:194
  89.0 3.1 %all-to-all-done.1 = bf16[32,48,128]{2,1,0:T(8,128)(2,1)S(1)} async-done(((bf16[32,48,128]{2,1,0:T(8,128)(2,1)}), bf16[32,48,128]{2,1,0:T(8,128)(2,1)S(1)}, u32[]{:S(2)}, u32[]{:S(2)}) %all-to-all-start.1) | async-done | bytes 393248 | tf_op jit(solution)/shard_map/all_to_all | solution.py:249
  92.1 9.5 %shard_map.76 = (f32[5,384,256]{2,1,0:T(8,128)S(1)}, s32[4,35]{1,0:T(4,128)S(1)}) custom-call(s32[1,8]{1,0:T(1,128)S(1)} %get-tuple-element.9.t0, s32[1,8]{1,0:T(1,128)S(1)} %collective-permute-done.t1, s32[1,8]{1,0:T(1,128)S(1)} %collective-permute-done.1.t2, s32[1,8]{1,0:T(1,128)S(1)} %collective-permute-done.2.t3, ...), custom_call_target="tpu_custom_call" | custom-call | flops 2264924160 | bytes 4718592 | tf_op jit(solution)/shard_map/pallas_call | solution.py:279
  101.7 3.2 %collective-permute-done.7 = bf16[32,2,48,128]{3,2,1,0:T(8,128)(2,1)S(1)} collective-permute-done((bf16[32,2,48,128]{3,2,1,0:T(8,128)(2,1)}, bf16[32,2,48,128]{3,2,1,0:T(8,128)(2,1)S(1)}, u32[]{:S(2)}, u32[]{:S(2)}) %collective-permute-start.7) | collective-permute-done | bytes 786464 | tf_op jit(solution)/shard_map/ppermute | solution.py:194
  104.9 2.1 %collective-permute-done.8 = bf16[32,2,48,128]{3,2,1,0:T(8,128)(2,1)S(1)} collective-permute-done((bf16[32,2,48,128]{3,2,1,0:T(8,128)(2,1)}, bf16[32,2,48,128]{3,2,1,0:T(8,128)(2,1)S(1)}, u32[]{:S(2)}, u32[]{:S(2)}) %collective-permute-start.8) | collective-permute-done | bytes 786464 | tf_op jit(solution)/shard_map/ppermute | solution.py:194
  107.0 0.0 collective-permute-done.9
  107.0 0.0 collective-permute-done.10
  107.0 4.5 %shard_map.77 = bf16[4,4,2,48,128]{4,3,2,1,0:T(8,128)(2,1)S(1)} custom-call(s32[4,35]{1,0:T(4,128)S(1)} %get-tuple-element.11.picked, bf16[4,4,2,48,128]{4,3,2,1,0:T(8,128)(2,1)S(1)} %bitcast.21, f32[5,384,256]{2,1,0:T(8,128)S(1)} %get-tuple-element.12.sums, bf16[4,4,2,2,48,128]{5,4,3,2,1,0:T(8,128)(2,1)S(1)} %bitcast.24, ...), custom_call_target="tpu_custom_call" | custom-call | flops 905969664 | bytes 4718592 | tf_op jit(solution)/shard_map/pallas_call | solution.py:296
  111.5 38.3 %all_to_all.15.chunk_ref = bf16[32,48,128]{2,1,0:T(8,128)(2,1)S(1)} all-to-all(bf16[32,48,128]{2,1,0:T(8,128)(2,1)S(1)} %bitcast.22), channel_id=1, replica_groups=mesh['x'=4,'zl'=4,'y'=4,'zh'=4,'c'=2] {'zl','zh','c'}, dimensions={0} | all-to-all | bytes 786432 | tf_op jit(solution)/shard_map/all_to_all | solution.py:307
  149.8 0.8 shard_map.78
  (1 shorter events, 0.0 us)
Async XLA Ops:
  0.0 18.9 %copy-start.1 = (s32[1,1,1,8]{3,2,1,0:T(1,128)S(1)}, s32[1,1,1,8]{3,2,1,0:T(1,128)}, u32[]{:S(2)}) copy-start(s32[1,1,1,8]{3,2,1,0:T(1,128)} %param.12) | copy-start | bytes 100
  0.0 18.9 %copy-start = (bf16[1,1,48,3072]{3,2,1,0:T(8,128)(2,1)S(1)}, bf16[1,1,48,3072]{3,2,1,0:T(8,128)(2,1)}, u32[]{:S(2)}) copy-start(bf16[1,1,48,3072]{3,2,1,0:T(8,128)(2,1)} %param.7) | copy-start | bytes 884740
  0.0 18.9 %copy-start.2 = (f32[128]{0:T(128)S(1)}, f32[128]{0:T(128)}, u32[]{:S(2)}) copy-start(f32[128]{0:T(128)} %param.10) | copy-start | bytes 1540
  2.9 58.0 %all-to-all-start = ((bf16[32,2,48,128]{3,2,1,0:T(8,128)(2,1)}), bf16[32,2,48,128]{3,2,1,0:T(8,128)(2,1)S(1)}, u32[]{:S(2)}, u32[]{:S(2)}) async-start(bf16[32,2,48,128]{3,2,1,0:T(8,128)(2,1)} %shard_map.74), calls=%async_computation | async-start | bytes 1572864 | tf_op jit(solution)/shard_map/all_to_all | solution.py:222
  20.5 28.6 %collective-permute-start = (s32[1,8]{1,0:T(1,128)S(1)}, s32[1,8]{1,0:T(1,128)S(1)}, u32[]{:S(2)}, u32[]{:S(2)}) collective-permute-start(s32[1,8]{1,0:T(1,128)S(1)} %get-tuple-element.9.t0), channel_id=1, source_target_pairs={{0,32},{32,64},{64,96},{96,0},{1,33},{33,65},{65,97},{97,1},{2,34}... | collective-permute-start | bytes 104 | tf_op jit(solution)/shard_map/ppermute | solution.py:239
  23.9 26.7 %collective-permute-start.1 = (s32[1,8]{1,0:T(1,128)S(1)}, s32[1,8]{1,0:T(1,128)S(1)}, u32[]{:S(2)}, u32[]{:S(2)}) collective-permute-start(s32[1,8]{1,0:T(1,128)S(1)} %get-tuple-element.9.t0), channel_id=1, source_target_pairs={{0,64},{32,96},{64,0},{96,32},{1,65},{33,97},{65,1},{97,33},{2,66}... | collective-permute-start | bytes 104 | tf_op jit(solution)/shard_map/ppermute | solution.py:239
  26.9 24.0 %collective-permute-start.2 = (s32[1,8]{1,0:T(1,128)S(1)}, s32[1,8]{1,0:T(1,128)S(1)}, u32[]{:S(2)}, u32[]{:S(2)}) collective-permute-start(s32[1,8]{1,0:T(1,128)S(1)} %get-tuple-element.9.t0), channel_id=1, source_target_pairs={{0,96},{32,0},{64,32},{96,64},{1,97},{33,1},{65,33},{97,65},{2,98}... | collective-permute-start | bytes 104 | tf_op jit(solution)/shard_map/ppermute | solution.py:239
  60.9 31.3 %all-to-all-start.1 = ((bf16[32,48,128]{2,1,0:T(8,128)(2,1)}), bf16[32,48,128]{2,1,0:T(8,128)(2,1)S(1)}, u32[]{:S(2)}, u32[]{:S(2)}) async-start(bf16[32,48,128]{2,1,0:T(8,128)(2,1)} %shard_map.75), calls=%async_computation.1 | async-start | bytes 786432 | tf_op jit(solution)/shard_map/all_to_all | solution.py:249
  65.8 20.3 %collective-permute-start.3 = (bf16[32,2,48,128]{3,2,1,0:T(8,128)(2,1)S(1)}, bf16[32,2,48,128]{3,2,1,0:T(8,128)(2,1)}, u32[]{:S(2)}, u32[]{:S(2)}) collective-permute-start(bf16[32,2,48,128]{3,2,1,0:T(8,128)(2,1)S(1)} %all-to-all-done.after), channel_id=1, source_target_pairs={{0,128},{1,0},{128,256},{129,1},{256,384},{257,129},{384,385},{385... | collective-permute-start | bytes 2359304 | tf_op jit(solution)/shard_map/ppermute | solution.py:194
  66.0 21.0 %collective-permute-start.4 = (bf16[32,2,48,128]{3,2,1,0:T(8,128)(2,1)S(1)}, bf16[32,2,48,128]{3,2,1,0:T(8,128)(2,1)}, u32[]{:S(2)}, u32[]{:S(2)}) collective-permute-start(bf16[32,2,48,128]{3,2,1,0:T(8,128)(2,1)S(1)} %all-to-all-done.after), channel_id=1, source_target_pairs={{0,8},{1,0},{8,16},{9,1},{16,24},{17,9},{24,25},{25,17},{2,10},{3,... | collective-permute-start | bytes 2359304 | tf_op jit(solution)/shard_map/ppermute | solution.py:194
  66.5 20.5 %collective-permute-start.5 = (bf16[32,2,48,128]{3,2,1,0:T(8,128)(2,1)S(1)}, bf16[32,2,48,128]{3,2,1,0:T(8,128)(2,1)}, u32[]{:S(2)}, u32[]{:S(2)}) collective-permute-start(bf16[32,2,48,128]{3,2,1,0:T(8,128)(2,1)S(1)} %all-to-all-done.after), channel_id=1, source_target_pairs={{0,1},{1,129},{128,0},{129,257},{256,128},{257,385},{384,256},{385... | collective-permute-start | bytes 2359304 | tf_op jit(solution)/shard_map/ppermute | solution.py:194
  67.9 19.5 %collective-permute-start.6 = (bf16[32,2,48,128]{3,2,1,0:T(8,128)(2,1)S(1)}, bf16[32,2,48,128]{3,2,1,0:T(8,128)(2,1)}, u32[]{:S(2)}, u32[]{:S(2)}) collective-permute-start(bf16[32,2,48,128]{3,2,1,0:T(8,128)(2,1)S(1)} %all-to-all-done.after), channel_id=1, source_target_pairs={{0,1},{1,9},{8,0},{9,17},{16,8},{17,25},{24,16},{25,24},{2,3},{3,1... | collective-permute-start | bytes 2359304 | tf_op jit(solution)/shard_map/ppermute | solution.py:194
  86.2 18.7 %collective-permute-start.7 = (bf16[32,2,48,128]{3,2,1,0:T(8,128)(2,1)}, bf16[32,2,48,128]{3,2,1,0:T(8,128)(2,1)S(1)}, u32[]{:S(2)}, u32[]{:S(2)}) collective-permute-start(bf16[32,2,48,128]{3,2,1,0:T(8,128)(2,1)} %collective-permute-done.3), channel_id=1, source_target_pairs={{0,1},{1,9},{8,0},{9,17},{16,8},{17,25},{24,16},{25,24},{2,3},{3,1... | collective-permute-start | bytes 2359304 | tf_op jit(solution)/shard_map/ppermute | solution.py:194
  87.0 20.0 %collective-permute-start.8 = (bf16[32,2,48,128]{3,2,1,0:T(8,128)(2,1)}, bf16[32,2,48,128]{3,2,1,0:T(8,128)(2,1)S(1)}, u32[]{:S(2)}, u32[]{:S(2)}) collective-permute-start(bf16[32,2,48,128]{3,2,1,0:T(8,128)(2,1)} %collective-permute-done.4), channel_id=1, source_target_pairs={{0,128},{1,0},{128,256},{129,1},{256,384},{257,129},{384,385},{385... | collective-permute-start | bytes 2359304 | tf_op jit(solution)/shard_map/ppermute | solution.py:194
  87.0 20.0 %collective-permute-start.9 = (bf16[32,2,48,128]{3,2,1,0:T(8,128)(2,1)}, bf16[32,2,48,128]{3,2,1,0:T(8,128)(2,1)S(1)}, u32[]{:S(2)}, u32[]{:S(2)}) collective-permute-start(bf16[32,2,48,128]{3,2,1,0:T(8,128)(2,1)} %collective-permute-done.5), channel_id=1, source_target_pairs={{0,8},{1,0},{8,16},{9,1},{16,24},{17,9},{24,25},{25,17},{2,10},{3,... | collective-permute-start | bytes 2359304 | tf_op jit(solution)/shard_map/ppermute | solution.py:194
  87.3 19.7 %collective-permute-start.10 = (bf16[32,2,48,128]{3,2,1,0:T(8,128)(2,1)}, bf16[32,2,48,128]{3,2,1,0:T(8,128)(2,1)}, u32[]{:S(2)}, u32[]{:S(2)}) collective-permute-start(bf16[32,2,48,128]{3,2,1,0:T(8,128)(2,1)} %collective-permute-done.6), channel_id=1, source_target_pairs={{0,1},{1,129},{128,0},{129,257},{256,128},{257,385},{384,256},{385... | collective-permute-start | bytes 2359304 | tf_op jit(solution)/shard_map/ppermute | solution.py:194

commit v4 on v3

--- a/solution.py
+++ b/solution.py
@@ -76,6 +76,10 @@
 
 def hand_on_kernel(q_in, after, t1, t2, t3, q_out):
     del q_in, after, t1, t2, t3, q_out
+
+
+def pause_kernel(table, xm, ym, xp, yp, table_out):
+    del table, xm, ym, xp, yp, table_out
 
 
 def list_entries(lists_ref, mirrored, near, far):
@@ -253,6 +257,16 @@
     mp, mm = moved(xm, "y", -1), moved(ym, "x", 1)
     pm, pp = moved(xp, "y", 1), moved(yp, "x", -1)
 
+    tables[1] = pl.pallas_call(
+        pause_kernel,
+        out_shape=jax.ShapeDtypeStruct(table.shape, table.dtype),
+        in_specs=[hbm] * 5,
+        out_specs=hbm,
+        input_output_aliases={0: 0},
+        compiler_params=params(16),
+        cost_estimate=pl.CostEstimate(flops=24_000_000_000, bytes_accessed=0, transcendentals=0),
+    )(tables[1], xm, ym, xp, yp)
+
     def by_place(array):
         return array.reshape(sizes + array.shape[1:])
 

time: 151 us -> 142 us (0.940)
  the two profiles are of different devices: /device:TPU:62 before, /device:TPU:52 now
where the time goes in v4:
time: 142 us; the launch traced here: 141 us
  waiting for transfers between devices  52.9 us (37%)
  starting transfers between devices  38.1 us (27%)
  blocking collectives  30.4 us (21%)
  Pallas kernels  19.2 us (14%)
    all_to_all x1, blocking collectives, on_device(): lax.all_to_all(chunks, RING, split_axis=0, concat_axis=0, tiled=True)  30.4 us
    all_to_all x1, waiting for transfers between devices, on_device(): lax.all_to_all(kv_chunks, RING, split_axis=0, concat_axis=0, tiled=True)  30.2 us
    all_to_all x1, starting transfers between devices, on_device(): lax.all_to_all(kv_chunks, RING, split_axis=0, concat_axis=0, tiled=True)  15.4 us
    ppermute x8, waiting for transfers between devices, moved(): return lax.ppermute(array, (axis, 'c'), pairs)  12.4 us
    pallas_call x1, Pallas kernels, on_device(): pl.pallas_call(near_kernel, out_shape=(jax.ShapeDtypeStruct(sums_shape, j...  11.2 us
    all_to_all x1, waiting for transfers between devices, on_device(): lax.all_to_all(q_chunks, RING, split_axis=0, concat_axis=0, tiled=True)  10.2 us
    ppermute x3, starting transfers between devices, on_device(): lax.ppermute(table, 'zl', turns[step])  10.2 us
    ppermute x8, starting transfers between devices, moved(): return lax.ppermute(array, (axis, 'c'), pairs)  7.77 us
  transfers between devices with their start and end apart: 13, of which 4 were waited for; matrix products, arithmetic and copies ran while one was open for 0% of the time, Pallas kernels for 9%

profile of v4, /device:TPU:52, one launch (start us, length us, event | category | flops | bytes accessed | tf_op | source)
XLA Modules:
  0.0 141.4 jit_solution(9122341883799170119)
XLA Ops:
  0.0 0.0 copy-start.1
  0.0 0.0 copy-start
  0.0 0.0 copy-start.2
  0.0 2.8 %shard_map.74 = bf16[32,2,48,128]{3,2,1,0:T(8,128)(2,1)} custom-call(bf16[48,3072]{1,0:T(8,128)(2,1)} %bitcast.30, bf16[48,3072]{1,0:T(8,128)(2,1)} %bitcast.31, f32[1,128]{1,0:T(1,128)} %bitcast.32), custom_call_target="tpu_custom_call" | custom-call | tf_op jit(solution)/shard_map/pallas_call | solution.py:213
  2.9 15.4 %all-to-all-start = ((bf16[32,2,48,128]{3,2,1,0:T(8,128)(2,1)}), bf16[32,2,48,128]{3,2,1,0:T(8,128)(2,1)S(1)}, u32[]{:S(2)}, u32[]{:S(2)}) async-start(bf16[32,2,48,128]{3,2,1,0:T(8,128)(2,1)} %shard_map.74), calls=%async_computation | async-start | bytes 1572864 | tf_op jit(solution)/shard_map/all_to_all | solution.py:226
  18.9 0.0 copy-done.1
  18.9 0.0 copy-done
  18.9 0.0 copy-done.2
  18.9 1.5 %shard_map.73 = (bf16[32,48,128]{2,1,0:T(8,128)(2,1)}, s32[1,8]{1,0:T(1,128)S(1)}) custom-call(s32[1,8]{1,0:T(1,128)S(1)} %bitcast.28, s32[1,1]{1,0:T(1,128)} %bitcast.19.counts_ref, bf16[48,3072]{1,0:T(8,128)(2,1)S(1)} %bitcast.27, f32[1,128]{1,0:T(1,128)S(1)} %bitcast.29), custom_call_target="tpu_custom_call" | custom-call | tf_op jit(solution)/shard_map/pallas_call | solution.py:227
  20.5 3.4 %collective-permute-start = (s32[1,8]{1,0:T(1,128)S(1)}, s32[1,8]{1,0:T(1,128)S(1)}, u32[]{:S(2)}, u32[]{:S(2)}) collective-permute-start(s32[1,8]{1,0:T(1,128)S(1)} %get-tuple-element.9.t0), channel_id=1, source_target_pairs={{0,32},{32,64},{64,96},{96,0},{1,33},{33,65},{65,97},{97,1},{2,34}... | collective-permute-start | bytes 104 | tf_op jit(solution)/shard_map/ppermute | solution.py:243
  23.9 3.0 %collective-permute-start.5 = (s32[1,8]{1,0:T(1,128)S(1)}, s32[1,8]{1,0:T(1,128)S(1)}, u32[]{:S(2)}, u32[]{:S(2)}) collective-permute-start(s32[1,8]{1,0:T(1,128)S(1)} %get-tuple-element.9.t0), channel_id=1, source_target_pairs={{0,64},{32,96},{64,0},{96,32},{1,65},{33,97},{65,1},{97,33},{2,66}... | collective-permute-start | bytes 104 | tf_op jit(solution)/shard_map/ppermute | solution.py:243
  26.9 3.7 %collective-permute-start.6 = (s32[1,8]{1,0:T(1,128)S(1)}, s32[1,8]{1,0:T(1,128)S(1)}, u32[]{:S(2)}, u32[]{:S(2)}) collective-permute-start(s32[1,8]{1,0:T(1,128)S(1)} %get-tuple-element.9.t0), channel_id=1, source_target_pairs={{0,96},{32,0},{64,32},{96,64},{1,97},{33,1},{65,33},{97,65},{2,98}... | collective-permute-start | bytes 104 | tf_op jit(solution)/shard_map/ppermute | solution.py:243
  30.6 30.2 %all-to-all-done.after = bf16[32,2,48,128]{3,2,1,0:T(8,128)(2,1)S(1)} async-done(((bf16[32,2,48,128]{3,2,1,0:T(8,128)(2,1)}), bf16[32,2,48,128]{3,2,1,0:T(8,128)(2,1)S(1)}, u32[]{:S(2)}, u32[]{:S(2)}) %all-to-all-start) | async-done | bytes 786464 | tf_op jit(solution)/shard_map/all_to_all | solution.py:226
  60.9 1.2 collective-permute-start.1
  62.1 1.3 collective-permute-start.2
  63.4 0.0 collective-permute-done.table.t1
  63.4 0.8 collective-permute-start.3
  64.2 0.0 collective-permute-done.5.t2
  64.2 0.7 collective-permute-start.4
  64.9 0.0 collective-permute-done.6.t3
  65.0 4.8 %all-to-all-start.1 = ((bf16[32,48,128]{2,1,0:T(8,128)(2,1)}), bf16[32,48,128]{2,1,0:T(8,128)(2,1)S(1)}, u32[]{:S(2)}, u32[]{:S(2)}) async-start(bf16[32,48,128]{2,1,0:T(8,128)(2,1)} %shard_map.76), calls=%async_computation.1 | async-start | bytes 786432 | tf_op jit(solution)/shard_map/all_to_all | solution.py:253
  69.8 10.5 %collective-permute-done.1.xm = bf16[32,2,48,128]{3,2,1,0:T(8,128)(2,1)} collective-permute-done((bf16[32,2,48,128]{3,2,1,0:T(8,128)(2,1)S(1)}, bf16[32,2,48,128]{3,2,1,0:T(8,128)(2,1)}, u32[]{:S(2)}, u32[]{:S(2)}) %collective-permute-start.1) | collective-permute-done | bytes 786464 | tf_op jit(solution)/shard_map/ppermute | solution.py:198
  80.3 0.4 collective-permute-start.7
  80.7 1.9 %collective-permute-done.2.ym = bf16[32,2,48,128]{3,2,1,0:T(8,128)(2,1)} collective-permute-done((bf16[32,2,48,128]{3,2,1,0:T(8,128)(2,1)S(1)}, bf16[32,2,48,128]{3,2,1,0:T(8,128)(2,1)}, u32[]{:S(2)}, u32[]{:S(2)}) %collective-permute-start.2) | collective-permute-done | bytes 786464 | tf_op jit(solution)/shard_map/ppermute | solution.py:198
  82.6 0.0 collective-permute-start.8
  82.6 0.0 collective-permute-done.3.xp
  82.6 1.3 collective-permute-start.9
  83.9 0.0 collective-permute-done.4.yp
  83.9 2.0 %collective-permute-start.10 = (bf16[32,2,48,128]{3,2,1,0:T(8,128)(2,1)}, bf16[32,2,48,128]{3,2,1,0:T(8,128)(2,1)}, u32[]{:S(2)}, u32[]{:S(2)}) collective-permute-start(bf16[32,2,48,128]{3,2,1,0:T(8,128)(2,1)} %collective-permute-done.4.yp), channel_id=1, source_target_pairs={{0,1},{1,129},{128,0},{129,257},{256,128},{257,385},{384,256},{385... | collective-permute-start | bytes 2359304 | tf_op jit(solution)/shard_map/ppermute | solution.py:198
  85.9 10.2 %all-to-all-done.1 = bf16[32,48,128]{2,1,0:T(8,128)(2,1)S(1)} async-done(((bf16[32,48,128]{2,1,0:T(8,128)(2,1)}), bf16[32,48,128]{2,1,0:T(8,128)(2,1)S(1)}, u32[]{:S(2)}, u32[]{:S(2)}) %all-to-all-start.1) | async-done | bytes 393248 | tf_op jit(solution)/shard_map/all_to_all | solution.py:253
  96.1 11.2 %shard_map.77 = (f32[5,384,256]{2,1,0:T(8,128)S(1)}, s32[4,35]{1,0:T(4,128)S(1)}) custom-call(s32[1,8]{1,0:T(1,128)S(1)} %get-tuple-element.9.t0, s32[1,8]{1,0:T(1,128)S(1)} %shard_map.75.t1, s32[1,8]{1,0:T(1,128)S(1)} %collective-permute-done.5.t2, s32[1,8]{1,0:T(1,128)S(1)} %collective-permute-done.6.t3, bf16[4,4,2,48,128]{4,3,2,1,0:T(8,128)(2,1)S(1)} %bitcast.20, ...), custom_call_target="tpu_custom_call" | custom-call | flops 2264924160 | bytes 4718592 | tf_op jit(solution)/shard_map/pallas_call | solution.py:293
  107.3 0.0 collective-permute-done.7
  107.4 0.0 collective-permute-done.8
  107.4 0.0 collective-permute-done.9
  107.4 0.0 collective-permute-done.10
  107.4 2.8 %shard_map.78 = bf16[4,4,2,48,128]{4,3,2,1,0:T(8,128)(2,1)S(1)} custom-call(s32[4,35]{1,0:T(4,128)S(1)} %get-tuple-element.11.picked, bf16[4,4,2,48,128]{4,3,2,1,0:T(8,128)(2,1)S(1)} %bitcast.21, f32[5,384,256]{2,1,0:T(8,128)S(1)} %get-tuple-element.12.sums, bf16[4,4,2,2,48,128]{5,4,3,2,1,0:T(8,128)(2,1)S(1)} %bitcast.24, ...), custom_call_target="tpu_custom_call" | custom-call | flops 905969664 | bytes 4718592 | tf_op jit(solution)/shard_map/pallas_call | solution.py:310
  110.2 30.4 %all_to_all.15.chunk_ref = bf16[32,48,128]{2,1,0:T(8,128)(2,1)S(1)} all-to-all(bf16[32,48,128]{2,1,0:T(8,128)(2,1)S(1)} %bitcast.22), channel_id=1, replica_groups=mesh['x'=4,'zl'=4,'y'=4,'zh'=4,'c'=2] {'zl','zh','c'}, dimensions={0} | all-to-all | bytes 786432 | tf_op jit(solution)/shard_map/all_to_all | solution.py:321
  140.7 0.8 shard_map.79
  (2 shorter events, 0.0 us)
Async XLA Ops:
  0.0 18.9 %copy-start.1 = (s32[1,1,1,8]{3,2,1,0:T(1,128)S(1)}, s32[1,1,1,8]{3,2,1,0:T(1,128)}, u32[]{:S(2)}) copy-start(s32[1,1,1,8]{3,2,1,0:T(1,128)} %param.12) | copy-start | bytes 100
  0.0 18.9 %copy-start = (bf16[1,1,48,3072]{3,2,1,0:T(8,128)(2,1)S(1)}, bf16[1,1,48,3072]{3,2,1,0:T(8,128)(2,1)}, u32[]{:S(2)}) copy-start(bf16[1,1,48,3072]{3,2,1,0:T(8,128)(2,1)} %param.7) | copy-start | bytes 884740
  0.0 18.9 %copy-start.2 = (f32[128]{0:T(128)S(1)}, f32[128]{0:T(128)}, u32[]{:S(2)}) copy-start(f32[128]{0:T(128)} %param.10) | copy-start | bytes 1540
  2.9 58.0 %all-to-all-start = ((bf16[32,2,48,128]{3,2,1,0:T(8,128)(2,1)}), bf16[32,2,48,128]{3,2,1,0:T(8,128)(2,1)S(1)}, u32[]{:S(2)}, u32[]{:S(2)}) async-start(bf16[32,2,48,128]{3,2,1,0:T(8,128)(2,1)} %shard_map.74), calls=%async_computation | async-start | bytes 1572864 | tf_op jit(solution)/shard_map/all_to_all | solution.py:226
  20.5 42.9 %collective-permute-start = (s32[1,8]{1,0:T(1,128)S(1)}, s32[1,8]{1,0:T(1,128)S(1)}, u32[]{:S(2)}, u32[]{:S(2)}) collective-permute-start(s32[1,8]{1,0:T(1,128)S(1)} %get-tuple-element.9.t0), channel_id=1, source_target_pairs={{0,32},{32,64},{64,96},{96,0},{1,33},{33,65},{65,97},{97,1},{2,34}... | collective-permute-start | bytes 104 | tf_op jit(solution)/shard_map/ppermute | solution.py:243
  23.9 40.3 %collective-permute-start.5 = (s32[1,8]{1,0:T(1,128)S(1)}, s32[1,8]{1,0:T(1,128)S(1)}, u32[]{:S(2)}, u32[]{:S(2)}) collective-permute-start(s32[1,8]{1,0:T(1,128)S(1)} %get-tuple-element.9.t0), channel_id=1, source_target_pairs={{0,64},{32,96},{64,0},{96,32},{1,65},{33,97},{65,1},{97,33},{2,66}... | collective-permute-start | bytes 104 | tf_op jit(solution)/shard_map/ppermute | solution.py:243
  26.9 38.1 %collective-permute-start.6 = (s32[1,8]{1,0:T(1,128)S(1)}, s32[1,8]{1,0:T(1,128)S(1)}, u32[]{:S(2)}, u32[]{:S(2)}) collective-permute-start(s32[1,8]{1,0:T(1,128)S(1)} %get-tuple-element.9.t0), channel_id=1, source_target_pairs={{0,96},{32,0},{64,32},{96,64},{1,97},{33,1},{65,33},{97,65},{2,98}... | collective-permute-start | bytes 104 | tf_op jit(solution)/shard_map/ppermute | solution.py:243
  60.9 19.4 %collective-permute-start.1 = (bf16[32,2,48,128]{3,2,1,0:T(8,128)(2,1)S(1)}, bf16[32,2,48,128]{3,2,1,0:T(8,128)(2,1)}, u32[]{:S(2)}, u32[]{:S(2)}) collective-permute-start(bf16[32,2,48,128]{3,2,1,0:T(8,128)(2,1)S(1)} %all-to-all-done.after), channel_id=1, source_target_pairs={{0,128},{1,0},{128,256},{129,1},{256,384},{257,129},{384,385},{385... | collective-permute-start | bytes 2359304 | tf_op jit(solution)/shard_map/ppermute | solution.py:198
  62.1 20.5 %collective-permute-start.2 = (bf16[32,2,48,128]{3,2,1,0:T(8,128)(2,1)S(1)}, bf16[32,2,48,128]{3,2,1,0:T(8,128)(2,1)}, u32[]{:S(2)}, u32[]{:S(2)}) collective-permute-start(bf16[32,2,48,128]{3,2,1,0:T(8,128)(2,1)S(1)} %all-to-all-done.after), channel_id=1, source_target_pairs={{0,8},{1,0},{8,16},{9,1},{16,24},{17,9},{24,25},{25,17},{2,10},{3,... | collective-permute-start | bytes 2359304 | tf_op jit(solution)/shard_map/ppermute | solution.py:198
  63.4 19.3 %collective-permute-start.3 = (bf16[32,2,48,128]{3,2,1,0:T(8,128)(2,1)S(1)}, bf16[32,2,48,128]{3,2,1,0:T(8,128)(2,1)}, u32[]{:S(2)}, u32[]{:S(2)}) collective-permute-start(bf16[32,2,48,128]{3,2,1,0:T(8,128)(2,1)S(1)} %all-to-all-done.after), channel_id=1, source_target_pairs={{0,1},{1,129},{128,0},{129,257},{256,128},{257,385},{384,256},{385... | collective-permute-start | bytes 2359304 | tf_op jit(solution)/shard_map/ppermute | solution.py:198
  64.2 19.7 %collective-permute-start.4 = (bf16[32,2,48,128]{3,2,1,0:T(8,128)(2,1)S(1)}, bf16[32,2,48,128]{3,2,1,0:T(8,128)(2,1)}, u32[]{:S(2)}, u32[]{:S(2)}) collective-permute-start(bf16[32,2,48,128]{3,2,1,0:T(8,128)(2,1)S(1)} %all-to-all-done.after), channel_id=1, source_target_pairs={{0,1},{1,9},{8,0},{9,17},{16,8},{17,25},{24,16},{25,24},{2,3},{3,1... | collective-permute-start | bytes 2359304 | tf_op jit(solution)/shard_map/ppermute | solution.py:198
  65.0 31.1 %all-to-all-start.1 = ((bf16[32,48,128]{2,1,0:T(8,128)(2,1)}), bf16[32,48,128]{2,1,0:T(8,128)(2,1)S(1)}, u32[]{:S(2)}, u32[]{:S(2)}) async-start(bf16[32,48,128]{2,1,0:T(8,128)(2,1)} %shard_map.76), calls=%async_computation.1 | async-start | bytes 786432 | tf_op jit(solution)/shard_map/all_to_all | solution.py:253
  80.3 27.1 %collective-permute-start.7 = (bf16[32,2,48,128]{3,2,1,0:T(8,128)(2,1)}, bf16[32,2,48,128]{3,2,1,0:T(8,128)(2,1)S(1)}, u32[]{:S(2)}, u32[]{:S(2)}) collective-permute-start(bf16[32,2,48,128]{3,2,1,0:T(8,128)(2,1)} %collective-permute-done.1.xm), channel_id=1, source_target_pairs={{0,1},{1,9},{8,0},{9,17},{16,8},{17,25},{24,16},{25,24},{2,3},{3,1... | collective-permute-start | bytes 2359304 | tf_op jit(solution)/shard_map/ppermute | solution.py:198
  82.6 24.7 %collective-permute-start.8 = (bf16[32,2,48,128]{3,2,1,0:T(8,128)(2,1)}, bf16[32,2,48,128]{3,2,1,0:T(8,128)(2,1)S(1)}, u32[]{:S(2)}, u32[]{:S(2)}) collective-permute-start(bf16[32,2,48,128]{3,2,1,0:T(8,128)(2,1)} %collective-permute-done.2.ym), channel_id=1, source_target_pairs={{0,128},{1,0},{128,256},{129,1},{256,384},{257,129},{384,385},{385... | collective-permute-start | bytes 2359304 | tf_op jit(solution)/shard_map/ppermute | solution.py:198
  82.6 24.7 %collective-permute-start.9 = (bf16[32,2,48,128]{3,2,1,0:T(8,128)(2,1)}, bf16[32,2,48,128]{3,2,1,0:T(8,128)(2,1)S(1)}, u32[]{:S(2)}, u32[]{:S(2)}) collective-permute-start(bf16[32,2,48,128]{3,2,1,0:T(8,128)(2,1)} %collective-permute-done.3.xp), channel_id=1, source_target_pairs={{0,8},{1,0},{8,16},{9,1},{16,24},{17,9},{24,25},{25,17},{2,10},{3,... | collective-permute-start | bytes 2359304 | tf_op jit(solution)/shard_map/ppermute | solution.py:198
  83.9 23.5 %collective-permute-start.10 = (bf16[32,2,48,128]{3,2,1,0:T(8,128)(2,1)}, bf16[32,2,48,128]{3,2,1,0:T(8,128)(2,1)}, u32[]{:S(2)}, u32[]{:S(2)}) collective-permute-start(bf16[32,2,48,128]{3,2,1,0:T(8,128)(2,1)} %collective-permute-done.4.yp), channel_id=1, source_target_pairs={{0,1},{1,129},{128,0},{129,257},{256,128},{257,385},{384,256},{385... | collective-permute-start | bytes 2359304 | tf_op jit(solution)/shard_map/ppermute | solution.py:198

commit v5 on v3

--- a/solution.py
+++ b/solution.py
@@ -142,9 +142,7 @@
     lax.fori_loop(0, (found + 1) // 2, two, 0)
 
 
-def near_kernel(
-    t0, t1, t2, t3, query, own, xm, ym, xp, yp, sums, far, kv, lists, picked, sa, sb, sems
-):
+def gather_kernel(t0, t1, t2, t3, own, xm, ym, xp, yp, kv, near, far, lists, sems):
     copies = []
     for place, source in enumerate((ym, xm, own, xp, yp)):
         copies.append(pltpu.make_async_copy(source, kv.at[place], sems.at[place]))
@@ -155,10 +153,13 @@
         w = (here - step + TILES) & (TILES - 1)
         for slot in range(SLOTS):
             lists[w, slot] = table[0, slot]
-    sums[...] = jnp.zeros(sums.shape, sums.dtype)
-    list_entries(lists, lax.axis_index("c") == 1, picked, far)
+    list_entries(lists, lax.axis_index("c") == 1, near, far)
     for copy in copies:
         copy.wait()
+
+
+def near_kernel(picked, query, kv, sums, sa, sb):
+    sums[...] = jnp.zeros(sums.shape, sums.dtype)
     sum_entries(picked[3, 0], picked, query, kv, sums, sa, sb)
 
 
@@ -262,46 +263,46 @@
             flops=6 * HD * pairs, bytes_accessed=12 * own.size, transcendentals=pairs
         )
 
-    listed = TILES * SLOTS + 3
-
-    def scratch(columns):
-        return [
-            pltpu.VMEM((tile, tile), jnp.float32),
-            pltpu.VMEM((tile, tile), jnp.float32),
-            pltpu.SemaphoreType.DMA((columns + 1,)),
-        ]
-
-    def held(columns):
-        return pltpu.VMEM((columns,) + sizes + own.shape[1:], jnp.bfloat16)
-
     query = by_place(query)
-    sums_shape = (TILES + 1, tile, 2 * HD)
-    sums, far = pl.pallas_call(
+    listed = jax.ShapeDtypeStruct((4, TILES * SLOTS + 3), jnp.int32)
+    scores = [pltpu.VMEM((tile, tile), jnp.float32)] * 2
+    sums = jax.ShapeDtypeStruct((TILES + 1, tile, 2 * HD), jnp.float32)
+    near_kv, near, far = pl.pallas_call(
+        gather_kernel,
+        out_shape=(
+            jax.ShapeDtypeStruct((5,) + sizes + own.shape[1:], jnp.bfloat16),
+            listed,
+            listed,
+        ),
+        in_specs=[smem] * 4 + [hbm] * 5,
+        out_specs=(vmem, smem, smem),
+        scratch_shapes=[pltpu.SMEM((TILES, SLOTS), jnp.int32), pltpu.SemaphoreType.DMA((5,))],
+        compiler_params=params(16),
+        cost_estimate=pl.CostEstimate(flops=24_000_000_000, bytes_accessed=0, transcendentals=0),
+    )(*tables, *(by_place(array) for array in (own, xm, ym, xp, yp)))
+    near_sums = pl.pallas_call(
         near_kernel,
-        out_shape=(
-            jax.ShapeDtypeStruct(sums_shape, jnp.float32),
-            jax.ShapeDtypeStruct((4, listed), jnp.int32),
-        ),
-        in_specs=[smem] * 4 + [vmem] + [hbm] * 5,
-        out_specs=(vmem, smem),
-        scratch_shapes=[
-            held(5),
-            pltpu.SMEM((TILES, SLOTS), jnp.int32),
-            pltpu.SMEM((4, listed), jnp.int32),
-        ]
-        + scratch(5),
-        compiler_params=params(24),
+        out_shape=sums,
+        in_specs=[smem] + [vmem] * 2,
+        out_specs=vmem,
+        scratch_shapes=scores,
+        compiler_params=params(16),
         cost_estimate=cost(5),
-    )(*tables, query, *(by_place(array) for array in (own, xm, ym, xp, yp)))
+    )(near, query, near_kv)
     attended = pl.pallas_call(
         far_kernel,
         out_shape=jax.ShapeDtypeStruct(sizes + (dev_tok, HD), jnp.bfloat16),
         in_specs=[smem] + [vmem] * 2 + [hbm] * 4,
         out_specs=vmem,
-        scratch_shapes=[held(4), pltpu.VMEM(sums_shape, jnp.float32)] + scratch(4),
+        scratch_shapes=[
+            pltpu.VMEM((4,) + sizes + own.shape[1:], jnp.bfloat16),
+            pltpu.VMEM(sums.shape, sums.dtype),
+        ]
+        + scores
+        + [pltpu.SemaphoreType.DMA((4,))],
         compiler_params=params(24),
         cost_estimate=cost(2),
-    )(far, query, sums, *(by_place(array) for array in (mp, mm, pm, pp)))
+    )(far, query, near_sums, *(by_place(array) for array in (mp, mm, pm, pp)))
 
     chunks = attended.reshape(devices, dev_tok, HD)
     chunks = lax.all_to_all(chunks, RING, split_axis=0, concat_axis=0, tiled=True)

time: 151 us -> 143 us (0.947)
  the two profiles are of different devices: /device:TPU:62 before, /device:TPU:50 now
where the time goes in v5:
time: 143 us; the launch traced here: 142 us
  waiting for transfers between devices  44.3 us (31%)
  starting transfers between devices  38.1 us (27%)
  blocking collectives  30.4 us (21%)
  Pallas kernels  19.9 us (14%)
  local copies, waits for them, and re-layouts  8.66 us (6%)
    all_to_all x1, blocking collectives, on_device(): lax.all_to_all(chunks, RING, split_axis=0, concat_axis=0, tiled=True)  30.4 us
    all_to_all x1, waiting for transfers between devices, on_device(): lax.all_to_all(kv_chunks, RING, split_axis=0, concat_axis=0, tiled=True)  27.9 us
    all_to_all x1, starting transfers between devices, on_device(): lax.all_to_all(kv_chunks, RING, split_axis=0, concat_axis=0, tiled=True)  15.4 us
    ppermute x8, waiting for transfers between devices, moved(): return lax.ppermute(array, (axis, 'c'), pairs)  12.2 us
    ppermute x3, starting transfers between devices, on_device(): lax.ppermute(table, 'zl', turns[step])  10.2 us
    pallas_call x1, Pallas kernels, on_device(): pl.pallas_call(near_kernel, out_shape=sums, in_specs=[smem] + [vmem] * 2,...  8.74 us
    unnamed x18, local copies, waits for them, and re-layouts  8.66 us
    ppermute x8, starting transfers between devices, moved(): return lax.ppermute(array, (axis, 'c'), pairs)  7.78 us
  transfers between devices with their start and end apart: 13, of which 4 were waited for; matrix products, arithmetic and copies ran while one was open for 0% of the time, Pallas kernels for 9%

profile of v5, /device:TPU:50, one launch (start us, length us, event | category | flops | bytes accessed | tf_op | source)
XLA Modules:
  0.0 142.2 jit_solution(17042219645069959539)
XLA Ops:
  0.0 2.8 %shard_map.74 = bf16[32,2,48,128]{3,2,1,0:T(8,128)(2,1)} custom-call(bf16[48,3072]{1,0:T(8,128)(2,1)} %bitcast.30, bf16[48,3072]{1,0:T(8,128)(2,1)} %bitcast.31, f32[1,128]{1,0:T(1,128)} %bitcast.32), custom_call_target="tpu_custom_call" | custom-call | tf_op jit(solution)/shard_map/pallas_call | solution.py:210
  2.8 15.4 %all-to-all-start = ((bf16[32,2,48,128]{3,2,1,0:T(8,128)(2,1)}), bf16[32,2,48,128]{3,2,1,0:T(8,128)(2,1)S(1)}, u32[]{:S(2)}, u32[]{:S(2)}) async-start(bf16[32,2,48,128]{3,2,1,0:T(8,128)(2,1)} %shard_map.74), calls=%async_computation | async-start | bytes 1572864 | tf_op jit(solution)/shard_map/all_to_all | solution.py:223
  18.8 0.0 copy-start
  18.9 1.0 copy-done
  19.8 0.0 copy-start.1
  19.8 0.7 copy-done.1
  20.5 0.0 copy-start.2
  20.5 0.7 copy-done.2
  21.1 1.6 %shard_map.73 = (bf16[32,48,128]{2,1,0:T(8,128)(2,1)}, s32[1,8]{1,0:T(1,128)S(1)}) custom-call(s32[1,8]{1,0:T(1,128)S(1)} %bitcast.28, s32[1,1]{1,0:T(1,128)} %bitcast.19.counts_ref, bf16[48,3072]{1,0:T(8,128)(2,1)S(1)} %bitcast.27, f32[1,128]{1,0:T(1,128)S(1)} %bitcast.29), custom_call_target="tpu_custom_call" | custom-call | tf_op jit(solution)/shard_map/pallas_call | solution.py:224
  22.7 3.4 %collective-permute-start = (s32[1,8]{1,0:T(1,128)S(1)}, s32[1,8]{1,0:T(1,128)S(1)}, u32[]{:S(2)}, u32[]{:S(2)}) collective-permute-start(s32[1,8]{1,0:T(1,128)S(1)} %get-tuple-element.10.t0), channel_id=1, source_target_pairs={{0,32},{32,64},{64,96},{96,0},{1,33},{33,65},{65,97},{97,1},{2,34}... | collective-permute-start | bytes 104 | tf_op jit(solution)/shard_map/ppermute | solution.py:240
  26.1 3.0 %collective-permute-start.1 = (s32[1,8]{1,0:T(1,128)S(1)}, s32[1,8]{1,0:T(1,128)S(1)}, u32[]{:S(2)}, u32[]{:S(2)}) collective-permute-start(s32[1,8]{1,0:T(1,128)S(1)} %get-tuple-element.10.t0), channel_id=1, source_target_pairs={{0,64},{32,96},{64,0},{96,32},{1,65},{33,97},{65,1},{97,33},{2,66}... | collective-permute-start | bytes 104 | tf_op jit(solution)/shard_map/ppermute | solution.py:240
  29.1 3.7 %collective-permute-start.2 = (s32[1,8]{1,0:T(1,128)S(1)}, s32[1,8]{1,0:T(1,128)S(1)}, u32[]{:S(2)}, u32[]{:S(2)}) collective-permute-start(s32[1,8]{1,0:T(1,128)S(1)} %get-tuple-element.10.t0), channel_id=1, source_target_pairs={{0,96},{32,0},{64,32},{96,64},{1,97},{33,1},{65,33},{97,65},{2,98}... | collective-permute-start | bytes 104 | tf_op jit(solution)/shard_map/ppermute | solution.py:240
  32.9 27.9 %all-to-all-done.after = bf16[32,2,48,128]{3,2,1,0:T(8,128)(2,1)S(1)} async-done(((bf16[32,2,48,128]{3,2,1,0:T(8,128)(2,1)}), bf16[32,2,48,128]{3,2,1,0:T(8,128)(2,1)S(1)}, u32[]{:S(2)}, u32[]{:S(2)}) %all-to-all-start) | async-done | bytes 786464 | tf_op jit(solution)/shard_map/all_to_all | solution.py:223
  60.8 1.5 %collective-permute-start.3 = (bf16[32,2,48,128]{3,2,1,0:T(8,128)(2,1)S(1)}, bf16[32,2,48,128]{3,2,1,0:T(8,128)(2,1)}, u32[]{:S(2)}, u32[]{:S(2)}) collective-permute-start(bf16[32,2,48,128]{3,2,1,0:T(8,128)(2,1)S(1)} %all-to-all-done.after), channel_id=1, source_target_pairs={{0,128},{1,0},{128,256},{129,1},{256,384},{257,129},{384,385},{385... | collective-permute-start | bytes 2359304 | tf_op jit(solution)/shard_map/ppermute | solution.py:195
  62.3 1.3 collective-permute-start.4
  63.6 0.0 collective-permute-done.t1
  63.6 0.5 collective-permute-start.5
  64.2 0.0 collective-permute-done.1.t2
  64.2 0.7 collective-permute-start.6
  64.9 0.0 collective-permute-done.2.t3
  64.9 0.0 copy-start.3
  64.9 0.5 copy-done.3
  65.4 4.8 %all-to-all-start.1 = ((bf16[32,48,128]{2,1,0:T(8,128)(2,1)}), bf16[32,48,128]{2,1,0:T(8,128)(2,1)S(1)}, u32[]{:S(2)}, u32[]{:S(2)}) async-start(bf16[32,48,128]{2,1,0:T(8,128)(2,1)} %shard_map.76), calls=%async_computation.1 | async-start | bytes 786432 | tf_op jit(solution)/shard_map/all_to_all | solution.py:250
  70.2 10.0 %collective-permute-done.3 = bf16[32,2,48,128]{3,2,1,0:T(8,128)(2,1)} collective-permute-done((bf16[32,2,48,128]{3,2,1,0:T(8,128)(2,1)S(1)}, bf16[32,2,48,128]{3,2,1,0:T(8,128)(2,1)}, u32[]{:S(2)}, u32[]{:S(2)}) %collective-permute-start.3) | collective-permute-done | bytes 786464 | tf_op jit(solution)/shard_map/ppermute | solution.py:195
  80.2 0.4 collective-permute-start.7
  80.7 2.2 %collective-permute-done.4 = bf16[32,2,48,128]{3,2,1,0:T(8,128)(2,1)} collective-permute-done((bf16[32,2,48,128]{3,2,1,0:T(8,128)(2,1)S(1)}, bf16[32,2,48,128]{3,2,1,0:T(8,128)(2,1)}, u32[]{:S(2)}, u32[]{:S(2)}) %collective-permute-start.4) | collective-permute-done | bytes 786464 | tf_op jit(solution)/shard_map/ppermute | solution.py:195
  82.9 1.2 collective-permute-start.8
  84.1 0.0 collective-permute-done.5
  84.1 1.2 collective-permute-start.9
  85.3 0.0 collective-permute-done.6
  85.3 0.9 collective-permute-start.10
  86.2 0.0 copy-start.4
  86.2 0.7 copy-done.4
  86.8 3.1 %shard_map.75 = (bf16[5,4,4,2,2,48,128]{6,5,4,3,2,1,0:T(8,128)(2,1)S(1)}, s32[4,35]{1,0:T(4,128)S(1)}, s32[4,35]{1,0:T(4,128)S(1)}) custom-call(s32[1,8]{1,0:T(1,128)S(1)} %get-tuple-element.10.t0, s32[1,8]{1,0:T(1,128)S(1)} %collective-permute-done.t1, s32[1,8]{1,0:T(1,128)S(1)} %collective-permute-done.1.t2, s32[1,8]{1,0:T(1,128)S(1)} %copy-done.4, ...), custom_call_target="tpu_custom_call" | custom-call | flops 24000000000 | tf_op jit(solution)/shard_map/pallas_call | solution.py:270
  90.0 0.0 copy-start.5
  90.0 1.9 %copy-done.5 = bf16[5,4,4,2,2,48,128]{6,5,4,3,2,1,0:T(8,128)(2,1)} copy-done((bf16[5,4,4,2,2,48,128]{6,5,4,3,2,1,0:T(8,128)(2,1)}, bf16[5,4,4,2,2,48,128]{6,5,4,3,2,1,0:T(8,128)(2,1)S(1)}, u32[]{:S(2)}) %copy-start.5) | copy-done | bytes 3932184
  91.8 0.0 copy-start.7
  91.8 0.6 copy-done.7
  92.4 4.1 %all-to-all-done.1 = bf16[32,48,128]{2,1,0:T(8,128)(2,1)S(1)} async-done(((bf16[32,48,128]{2,1,0:T(8,128)(2,1)}), bf16[32,48,128]{2,1,0:T(8,128)(2,1)S(1)}, u32[]{:S(2)}, u32[]{:S(2)}) %all-to-all-start.1) | async-done | bytes 393248 | tf_op jit(solution)/shard_map/all_to_all | solution.py:250
  96.6 0.0 copy-start.6
  96.6 2.1 %copy-done.6 = bf16[5,4,4,2,2,48,128]{6,5,4,3,2,1,0:T(8,128)(2,1)S(1)} copy-done((bf16[5,4,4,2,2,48,128]{6,5,4,3,2,1,0:T(8,128)(2,1)S(1)}, bf16[5,4,4,2,2,48,128]{6,5,4,3,2,1,0:T(8,128)(2,1)}, u32[]{:S(2)}) %copy-start.6) | copy-done | bytes 3932184
  98.7 0.0 copy-start.8
  98.7 0.7 copy-done.8
  99.4 8.7 %shard_map.77.sums = f32[5,384,256]{2,1,0:T(8,128)S(1)} custom-call(s32[4,35]{1,0:T(4,128)S(1)} %copy-done.8, bf16[4,4,2,48,128]{4,3,2,1,0:T(8,128)(2,1)S(1)} %bitcast.20, bf16[5,4,4,2,2,48,128]{6,5,4,3,2,1,0:T(8,128)(2,1)S(1)} %copy-done.6), custom_call_target="tpu_custom_call" | custom-call | flops 2264924160 | bytes 4718592 | tf_op jit(solution)/shard_map/pallas_call | solution.py:283
  108.1 0.0 collective-permute-done.7
  108.1 0.0 collective-permute-done.8
  108.1 0.0 collective-permute-done.9
  108.1 0.0 collective-permute-done.10
  108.1 2.8 %shard_map.78 = bf16[4,4,2,48,128]{4,3,2,1,0:T(8,128)(2,1)S(1)} custom-call(s32[4,35]{1,0:T(4,128)S(1)} %get-tuple-element.11.picked, bf16[4,4,2,48,128]{4,3,2,1,0:T(8,128)(2,1)S(1)} %bitcast.21, f32[5,384,256]{2,1,0:T(8,128)S(1)} %shard_map.77.sums, bf16[4,4,2,2,48,128]{5,4,3,2,1,0:T(8,128)(2,1)S(1)} %bitcast.24, ...), custom_call_target="tpu_custom_call" | custom-call | flops 905969664 | bytes 4718592 | tf_op jit(solution)/shard_map/pallas_call | solution.py:292
  111.0 30.4 %all_to_all.15.chunk_ref = bf16[32,48,128]{2,1,0:T(8,128)(2,1)S(1)} all-to-all(bf16[32,48,128]{2,1,0:T(8,128)(2,1)S(1)} %bitcast.22), channel_id=1, replica_groups=mesh['x'=4,'zl'=4,'y'=4,'zh'=4,'c'=2] {'zl','zh','c'}, dimensions={0} | all-to-all | bytes 786432 | tf_op jit(solution)/shard_map/all_to_all | solution.py:308
  141.4 0.8 shard_map.79
  (1 shorter events, 0.0 us)
Async XLA Ops:
  2.8 58.0 %all-to-all-start = ((bf16[32,2,48,128]{3,2,1,0:T(8,128)(2,1)}), bf16[32,2,48,128]{3,2,1,0:T(8,128)(2,1)S(1)}, u32[]{:S(2)}, u32[]{:S(2)}) async-start(bf16[32,2,48,128]{3,2,1,0:T(8,128)(2,1)} %shard_map.74), calls=%async_computation | async-start | bytes 1572864 | tf_op jit(solution)/shard_map/all_to_all | solution.py:223
  18.8 1.0 copy-start
  19.8 0.7 copy-start.1
  20.5 0.7 copy-start.2
  22.7 40.9 %collective-permute-start = (s32[1,8]{1,0:T(1,128)S(1)}, s32[1,8]{1,0:T(1,128)S(1)}, u32[]{:S(2)}, u32[]{:S(2)}) collective-permute-start(s32[1,8]{1,0:T(1,128)S(1)} %get-tuple-element.10.t0), channel_id=1, source_target_pairs={{0,32},{32,64},{64,96},{96,0},{1,33},{33,65},{65,97},{97,1},{2,34}... | collective-permute-start | bytes 104 | tf_op jit(solution)/shard_map/ppermute | solution.py:240
  26.1 38.1 %collective-permute-start.1 = (s32[1,8]{1,0:T(1,128)S(1)}, s32[1,8]{1,0:T(1,128)S(1)}, u32[]{:S(2)}, u32[]{:S(2)}) collective-permute-start(s32[1,8]{1,0:T(1,128)S(1)} %get-tuple-element.10.t0), channel_id=1, source_target_pairs={{0,64},{32,96},{64,0},{96,32},{1,65},{33,97},{65,1},{97,33},{2,66}... | collective-permute-start | bytes 104 | tf_op jit(solution)/shard_map/ppermute | solution.py:240
  29.1 35.8 %collective-permute-start.2 = (s32[1,8]{1,0:T(1,128)S(1)}, s32[1,8]{1,0:T(1,128)S(1)}, u32[]{:S(2)}, u32[]{:S(2)}) collective-permute-start(s32[1,8]{1,0:T(1,128)S(1)} %get-tuple-element.10.t0), channel_id=1, source_target_pairs={{0,96},{32,0},{64,32},{96,64},{1,97},{33,1},{65,33},{97,65},{2,98}... | collective-permute-start | bytes 104 | tf_op jit(solution)/shard_map/ppermute | solution.py:240
  60.8 19.4 %collective-permute-start.3 = (bf16[32,2,48,128]{3,2,1,0:T(8,128)(2,1)S(1)}, bf16[32,2,48,128]{3,2,1,0:T(8,128)(2,1)}, u32[]{:S(2)}, u32[]{:S(2)}) collective-permute-start(bf16[32,2,48,128]{3,2,1,0:T(8,128)(2,1)S(1)} %all-to-all-done.after), channel_id=1, source_target_pairs={{0,128},{1,0},{128,256},{129,1},{256,384},{257,129},{384,385},{385... | collective-permute-start | bytes 2359304 | tf_op jit(solution)/shard_map/ppermute | solution.py:195
  62.3 20.6 %collective-permute-start.4 = (bf16[32,2,48,128]{3,2,1,0:T(8,128)(2,1)S(1)}, bf16[32,2,48,128]{3,2,1,0:T(8,128)(2,1)}, u32[]{:S(2)}, u32[]{:S(2)}) collective-permute-start(bf16[32,2,48,128]{3,2,1,0:T(8,128)(2,1)S(1)} %all-to-all-done.after), channel_id=1, source_target_pairs={{0,8},{1,0},{8,16},{9,1},{16,24},{17,9},{24,25},{25,17},{2,10},{3,... | collective-permute-start | bytes 2359304 | tf_op jit(solution)/shard_map/ppermute | solution.py:195
  63.6 20.5 %collective-permute-start.5 = (bf16[32,2,48,128]{3,2,1,0:T(8,128)(2,1)S(1)}, bf16[32,2,48,128]{3,2,1,0:T(8,128)(2,1)}, u32[]{:S(2)}, u32[]{:S(2)}) collective-permute-start(bf16[32,2,48,128]{3,2,1,0:T(8,128)(2,1)S(1)} %all-to-all-done.after), channel_id=1, source_target_pairs={{0,1},{1,129},{128,0},{129,257},{256,128},{257,385},{384,256},{385... | collective-permute-start | bytes 2359304 | tf_op jit(solution)/shard_map/ppermute | solution.py:195
  64.2 21.2 %collective-permute-start.6 = (bf16[32,2,48,128]{3,2,1,0:T(8,128)(2,1)S(1)}, bf16[32,2,48,128]{3,2,1,0:T(8,128)(2,1)}, u32[]{:S(2)}, u32[]{:S(2)}) collective-permute-start(bf16[32,2,48,128]{3,2,1,0:T(8,128)(2,1)S(1)} %all-to-all-done.after), channel_id=1, source_target_pairs={{0,1},{1,9},{8,0},{9,17},{16,8},{17,25},{24,16},{25,24},{2,3},{3,1... | collective-permute-start | bytes 2359304 | tf_op jit(solution)/shard_map/ppermute | solution.py:195
  64.9 0.5 copy-start.3
  65.4 31.1 %all-to-all-start.1 = ((bf16[32,48,128]{2,1,0:T(8,128)(2,1)}), bf16[32,48,128]{2,1,0:T(8,128)(2,1)S(1)}, u32[]{:S(2)}, u32[]{:S(2)}) async-start(bf16[32,48,128]{2,1,0:T(8,128)(2,1)} %shard_map.76), calls=%async_computation.1 | async-start | bytes 786432 | tf_op jit(solution)/shard_map/all_to_all | solution.py:250
  80.2 27.9 %collective-permute-start.7 = (bf16[32,2,48,128]{3,2,1,0:T(8,128)(2,1)}, bf16[32,2,48,128]{3,2,1,0:T(8,128)(2,1)S(1)}, u32[]{:S(2)}, u32[]{:S(2)}) collective-permute-start(bf16[32,2,48,128]{3,2,1,0:T(8,128)(2,1)} %collective-permute-done.3), channel_id=1, source_target_pairs={{0,1},{1,9},{8,0},{9,17},{16,8},{17,25},{24,16},{25,24},{2,3},{3,1... | collective-permute-start | bytes 2359304 | tf_op jit(solution)/shard_map/ppermute | solution.py:195
  82.9 25.2 %collective-permute-start.8 = (bf16[32,2,48,128]{3,2,1,0:T(8,128)(2,1)}, bf16[32,2,48,128]{3,2,1,0:T(8,128)(2,1)S(1)}, u32[]{:S(2)}, u32[]{:S(2)}) collective-permute-start(bf16[32,2,48,128]{3,2,1,0:T(8,128)(2,1)} %collective-permute-done.4), channel_id=1, source_target_pairs={{0,128},{1,0},{128,256},{129,1},{256,384},{257,129},{384,385},{385... | collective-permute-start | bytes 2359304 | tf_op jit(solution)/shard_map/ppermute | solution.py:195
  84.1 24.1 %collective-permute-start.9 = (bf16[32,2,48,128]{3,2,1,0:T(8,128)(2,1)}, bf16[32,2,48,128]{3,2,1,0:T(8,128)(2,1)S(1)}, u32[]{:S(2)}, u32[]{:S(2)}) collective-permute-start(bf16[32,2,48,128]{3,2,1,0:T(8,128)(2,1)} %collective-permute-done.5), channel_id=1, source_target_pairs={{0,8},{1,0},{8,16},{9,1},{16,24},{17,9},{24,25},{25,17},{2,10},{3,... | collective-permute-start | bytes 2359304 | tf_op jit(solution)/shard_map/ppermute | solution.py:195
  85.3 22.8 %collective-permute-start.10 = (bf16[32,2,48,128]{3,2,1,0:T(8,128)(2,1)}, bf16[32,2,48,128]{3,2,1,0:T(8,128)(2,1)}, u32[]{:S(2)}, u32[]{:S(2)}) collective-permute-start(bf16[32,2,48,128]{3,2,1,0:T(8,128)(2,1)} %collective-permute-done.6), channel_id=1, source_target_pairs={{0,1},{1,129},{128,0},{129,257},{256,128},{257,385},{384,256},{385... | collective-permute-start | bytes 2359304 | tf_op jit(solution)/shard_map/ppermute | solution.py:195
  86.2 0.7 copy-start.4
  90.0 1.9 %copy-start.5 = (bf16[5,4,4,2,2,48,128]{6,5,4,3,2,1,0:T(8,128)(2,1)}, bf16[5,4,4,2,2,48,128]{6,5,4,3,2,1,0:T(8,128)(2,1)S(1)}, u32[]{:S(2)}) copy-start(bf16[5,4,4,2,2,48,128]{6,5,4,3,2,1,0:T(8,128)(2,1)S(1)} %get-tuple-element.14.kv) | copy-start | bytes 11796484
  91.8 0.6 copy-start.7
  96.6 2.1 %copy-start.6 = (bf16[5,4,4,2,2,48,128]{6,5,4,3,2,1,0:T(8,128)(2,1)S(1)}, bf16[5,4,4,2,2,48,128]{6,5,4,3,2,1,0:T(8,128)(2,1)}, u32[]{:S(2)}) copy-start(bf16[5,4,4,2,2,48,128]{6,5,4,3,2,1,0:T(8,128)(2,1)} %copy-done.5) | copy-start | bytes 11796484
  98.7 0.7 copy-start.8

commit v6 on v4

--- a/solution.py
+++ b/solution.py
@@ -9,7 +9,7 @@
 
 TILES = 4
 HD = 128
-RING = ("zl", "zh", "c")
+RING = ("zl", "c", "zh")
 SLOTS = 8
 PARTS = 3
 

time: 142 us -> 143 us (level)
  no operation moved by 1% of the time
where the time goes in v6:
time: 143 us; the launch traced here: 142 us
  waiting for transfers between devices  53 us (37%)
  starting transfers between devices  38.2 us (27%)
  blocking collectives  30.3 us (21%)
  Pallas kernels  19.2 us (13%)
    all_to_all x1, blocking collectives, on_device(): lax.all_to_all(chunks, RING, split_axis=0, concat_axis=0, tiled=True)  30.3 us
    all_to_all x1, waiting for transfers between devices, on_device(): lax.all_to_all(kv_chunks, RING, split_axis=0, concat_axis=0, tiled=True)  30.3 us
    all_to_all x1, starting transfers between devices, on_device(): lax.all_to_all(kv_chunks, RING, split_axis=0, concat_axis=0, tiled=True)  15.4 us
    ppermute x8, waiting for transfers between devices, moved(): return lax.ppermute(array, (axis, 'c'), pairs)  12.4 us
    pallas_call x1, Pallas kernels, on_device(): pl.pallas_call(near_kernel, out_shape=(jax.ShapeDtypeStruct(sums_shape, j...  11.2 us
    all_to_all x1, waiting for transfers between devices, on_device(): lax.all_to_all(q_chunks, RING, split_axis=0, concat_axis=0, tiled=True)  10.4 us
    ppermute x3, starting transfers between devices, on_device(): lax.ppermute(table, 'zl', turns[step])  10.2 us
    ppermute x8, starting transfers between devices, moved(): return lax.ppermute(array, (axis, 'c'), pairs)  7.76 us
  transfers between devices with their start and end apart: 13, of which 4 were waited for; matrix products, arithmetic and copies ran while one was open for 0% of the time, Pallas kernels for 9%

profile of v6, /device:TPU:52, one launch (start us, length us, event | category | flops | bytes accessed | tf_op | source)
XLA Modules:
  0.0 141.6 jit_solution(2093986951124372093)
XLA Ops:
  0.0 0.0 copy-start.1
  0.0 0.0 copy-start
  0.0 0.0 copy-start.2
  0.0 2.8 %shard_map.74 = bf16[32,2,48,128]{3,2,1,0:T(8,128)(2,1)} custom-call(bf16[48,3072]{1,0:T(8,128)(2,1)} %bitcast.30, bf16[48,3072]{1,0:T(8,128)(2,1)} %bitcast.31, f32[1,128]{1,0:T(1,128)} %bitcast.32), custom_call_target="tpu_custom_call" | custom-call | tf_op jit(solution)/shard_map/pallas_call | solution.py:213
  2.9 15.4 %all-to-all-start = ((bf16[32,2,48,128]{3,2,1,0:T(8,128)(2,1)}), bf16[32,2,48,128]{3,2,1,0:T(8,128)(2,1)S(1)}, u32[]{:S(2)}, u32[]{:S(2)}) async-start(bf16[32,2,48,128]{3,2,1,0:T(8,128)(2,1)} %shard_map.74), calls=%async_computation | async-start | bytes 1572864 | tf_op jit(solution)/shard_map/all_to_all | solution.py:226
  18.9 0.0 copy-done.1
  18.9 0.0 copy-done
  18.9 0.0 copy-done.2
  18.9 1.5 %shard_map.73 = (bf16[32,48,128]{2,1,0:T(8,128)(2,1)}, s32[1,8]{1,0:T(1,128)S(1)}) custom-call(s32[1,8]{1,0:T(1,128)S(1)} %bitcast.28, s32[1,1]{1,0:T(1,128)} %bitcast.19.counts_ref, bf16[48,3072]{1,0:T(8,128)(2,1)S(1)} %bitcast.27, f32[1,128]{1,0:T(1,128)S(1)} %bitcast.29), custom_call_target="tpu_custom_call" | custom-call | tf_op jit(solution)/shard_map/pallas_call | solution.py:227
  20.5 3.4 %collective-permute-start = (s32[1,8]{1,0:T(1,128)S(1)}, s32[1,8]{1,0:T(1,128)S(1)}, u32[]{:S(2)}, u32[]{:S(2)}) collective-permute-start(s32[1,8]{1,0:T(1,128)S(1)} %get-tuple-element.9.t0), channel_id=1, source_target_pairs={{0,32},{32,64},{64,96},{96,0},{1,33},{33,65},{65,97},{97,1},{2,34}... | collective-permute-start | bytes 104 | tf_op jit(solution)/shard_map/ppermute | solution.py:243
  23.9 3.0 %collective-permute-start.5 = (s32[1,8]{1,0:T(1,128)S(1)}, s32[1,8]{1,0:T(1,128)S(1)}, u32[]{:S(2)}, u32[]{:S(2)}) collective-permute-start(s32[1,8]{1,0:T(1,128)S(1)} %get-tuple-element.9.t0), channel_id=1, source_target_pairs={{0,64},{32,96},{64,0},{96,32},{1,65},{33,97},{65,1},{97,33},{2,66}... | collective-permute-start | bytes 104 | tf_op jit(solution)/shard_map/ppermute | solution.py:243
  26.9 3.7 %collective-permute-start.6 = (s32[1,8]{1,0:T(1,128)S(1)}, s32[1,8]{1,0:T(1,128)S(1)}, u32[]{:S(2)}, u32[]{:S(2)}) collective-permute-start(s32[1,8]{1,0:T(1,128)S(1)} %get-tuple-element.9.t0), channel_id=1, source_target_pairs={{0,96},{32,0},{64,32},{96,64},{1,97},{33,1},{65,33},{97,65},{2,98}... | collective-permute-start | bytes 104 | tf_op jit(solution)/shard_map/ppermute | solution.py:243
  30.6 30.3 %all-to-all-done.after = bf16[32,2,48,128]{3,2,1,0:T(8,128)(2,1)S(1)} async-done(((bf16[32,2,48,128]{3,2,1,0:T(8,128)(2,1)}), bf16[32,2,48,128]{3,2,1,0:T(8,128)(2,1)S(1)}, u32[]{:S(2)}, u32[]{:S(2)}) %all-to-all-start) | async-done | bytes 786464 | tf_op jit(solution)/shard_map/all_to_all | solution.py:226
  60.9 1.2 collective-permute-start.1
  62.1 1.3 collective-permute-start.2
  63.4 0.0 collective-permute-done.table.t1
  63.4 0.8 collective-permute-start.3
  64.2 0.0 collective-permute-done.5.t2
  64.2 0.7 collective-permute-start.4
  65.0 0.0 collective-permute-done.6.t3
  65.0 4.9 %all-to-all-start.1 = ((bf16[32,48,128]{2,1,0:T(8,128)(2,1)}), bf16[32,48,128]{2,1,0:T(8,128)(2,1)S(1)}, u32[]{:S(2)}, u32[]{:S(2)}) async-start(bf16[32,48,128]{2,1,0:T(8,128)(2,1)} %shard_map.76), calls=%async_computation.1 | async-start | bytes 786432 | tf_op jit(solution)/shard_map/all_to_all | solution.py:253
  69.9 10.1 %collective-permute-done.1.xm = bf16[32,2,48,128]{3,2,1,0:T(8,128)(2,1)} collective-permute-done((bf16[32,2,48,128]{3,2,1,0:T(8,128)(2,1)S(1)}, bf16[32,2,48,128]{3,2,1,0:T(8,128)(2,1)}, u32[]{:S(2)}, u32[]{:S(2)}) %collective-permute-start.1) | collective-permute-done | bytes 786464 | tf_op jit(solution)/shard_map/ppermute | solution.py:198
  80.0 0.4 collective-permute-start.7
  80.5 2.2 %collective-permute-done.2.ym = bf16[32,2,48,128]{3,2,1,0:T(8,128)(2,1)} collective-permute-done((bf16[32,2,48,128]{3,2,1,0:T(8,128)(2,1)S(1)}, bf16[32,2,48,128]{3,2,1,0:T(8,128)(2,1)}, u32[]{:S(2)}, u32[]{:S(2)}) %collective-permute-start.2) | collective-permute-done | bytes 786464 | tf_op jit(solution)/shard_map/ppermute | solution.py:198
  82.7 0.0 collective-permute-start.8
  82.7 0.0 collective-permute-done.3.xp
  82.7 1.2 collective-permute-start.9
  83.9 0.0 collective-permute-done.4.yp
  83.9 2.0 %collective-permute-start.10 = (bf16[32,2,48,128]{3,2,1,0:T(8,128)(2,1)}, bf16[32,2,48,128]{3,2,1,0:T(8,128)(2,1)}, u32[]{:S(2)}, u32[]{:S(2)}) collective-permute-start(bf16[32,2,48,128]{3,2,1,0:T(8,128)(2,1)} %collective-permute-done.4.yp), channel_id=1, source_target_pairs={{0,1},{1,129},{128,0},{129,257},{256,128},{257,385},{384,256},{385... | collective-permute-start | bytes 2359304 | tf_op jit(solution)/shard_map/ppermute | solution.py:198
  85.9 10.4 %all-to-all-done.1 = bf16[32,48,128]{2,1,0:T(8,128)(2,1)S(1)} async-done(((bf16[32,48,128]{2,1,0:T(8,128)(2,1)}), bf16[32,48,128]{2,1,0:T(8,128)(2,1)S(1)}, u32[]{:S(2)}, u32[]{:S(2)}) %all-to-all-start.1) | async-done | bytes 393248 | tf_op jit(solution)/shard_map/all_to_all | solution.py:253
  96.3 11.2 %shard_map.77 = (f32[5,384,256]{2,1,0:T(8,128)S(1)}, s32[4,35]{1,0:T(4,128)S(1)}) custom-call(s32[1,8]{1,0:T(1,128)S(1)} %get-tuple-element.9.t0, s32[1,8]{1,0:T(1,128)S(1)} %shard_map.75.t1, s32[1,8]{1,0:T(1,128)S(1)} %collective-permute-done.5.t2, s32[1,8]{1,0:T(1,128)S(1)} %collective-permute-done.6.t3, bf16[4,2,4,48,128]{4,3,2,1,0:T(8,128)(2,1)S(1)} %bitcast.20, ...), custom_call_target="tpu_custom_call" | custom-call | flops 2264924160 | bytes 4718592 | tf_op jit(solution)/shard_map/pallas_call | solution.py:293
  107.6 0.0 collective-permute-done.7
  107.6 0.0 collective-permute-done.8
  107.6 0.0 collective-permute-done.9
  107.6 0.0 collective-permute-done.10
  107.6 2.8 %shard_map.78 = bf16[4,2,4,48,128]{4,3,2,1,0:T(8,128)(2,1)S(1)} custom-call(s32[4,35]{1,0:T(4,128)S(1)} %get-tuple-element.11.picked, bf16[4,2,4,48,128]{4,3,2,1,0:T(8,128)(2,1)S(1)} %bitcast.21, f32[5,384,256]{2,1,0:T(8,128)S(1)} %get-tuple-element.12.sums, bf16[4,2,4,2,48,128]{5,4,3,2,1,0:T(8,128)(2,1)S(1)} %bitcast.24, ...), custom_call_target="tpu_custom_call" | custom-call | flops 905969664 | bytes 4718592 | tf_op jit(solution)/shard_map/pallas_call | solution.py:310
  110.5 30.3 %all_to_all.15.chunk_ref = bf16[32,48,128]{2,1,0:T(8,128)(2,1)S(1)} all-to-all(bf16[32,48,128]{2,1,0:T(8,128)(2,1)S(1)} %bitcast.22), channel_id=1, replica_groups=mesh['x'=4,'zl'=4,'y'=4,'zh'=4,'c'=2] {'zl','c','zh'}, dimensions={0} | all-to-all | bytes 786432 | tf_op jit(solution)/shard_map/all_to_all | solution.py:321
  140.8 0.8 shard_map.79
  (2 shorter events, 0.0 us)
Async XLA Ops:
  0.0 18.9 %copy-start.1 = (s32[1,1,1,8]{3,2,1,0:T(1,128)S(1)}, s32[1,1,1,8]{3,2,1,0:T(1,128)}, u32[]{:S(2)}) copy-start(s32[1,1,1,8]{3,2,1,0:T(1,128)} %param.12) | copy-start | bytes 100
  0.0 18.9 %copy-start = (bf16[1,1,48,3072]{3,2,1,0:T(8,128)(2,1)S(1)}, bf16[1,1,48,3072]{3,2,1,0:T(8,128)(2,1)}, u32[]{:S(2)}) copy-start(bf16[1,1,48,3072]{3,2,1,0:T(8,128)(2,1)} %param.7) | copy-start | bytes 884740
  0.0 18.9 %copy-start.2 = (f32[128]{0:T(128)S(1)}, f32[128]{0:T(128)}, u32[]{:S(2)}) copy-start(f32[128]{0:T(128)} %param.10) | copy-start | bytes 1540
  2.9 58.0 %all-to-all-start = ((bf16[32,2,48,128]{3,2,1,0:T(8,128)(2,1)}), bf16[32,2,48,128]{3,2,1,0:T(8,128)(2,1)S(1)}, u32[]{:S(2)}, u32[]{:S(2)}) async-start(bf16[32,2,48,128]{3,2,1,0:T(8,128)(2,1)} %shard_map.74), calls=%async_computation | async-start | bytes 1572864 | tf_op jit(solution)/shard_map/all_to_all | solution.py:226
  20.5 42.9 %collective-permute-start = (s32[1,8]{1,0:T(1,128)S(1)}, s32[1,8]{1,0:T(1,128)S(1)}, u32[]{:S(2)}, u32[]{:S(2)}) collective-permute-start(s32[1,8]{1,0:T(1,128)S(1)} %get-tuple-element.9.t0), channel_id=1, source_target_pairs={{0,32},{32,64},{64,96},{96,0},{1,33},{33,65},{65,97},{97,1},{2,34}... | collective-permute-start | bytes 104 | tf_op jit(solution)/shard_map/ppermute | solution.py:243
  23.9 40.4 %collective-permute-start.5 = (s32[1,8]{1,0:T(1,128)S(1)}, s32[1,8]{1,0:T(1,128)S(1)}, u32[]{:S(2)}, u32[]{:S(2)}) collective-permute-start(s32[1,8]{1,0:T(1,128)S(1)} %get-tuple-element.9.t0), channel_id=1, source_target_pairs={{0,64},{32,96},{64,0},{96,32},{1,65},{33,97},{65,1},{97,33},{2,66}... | collective-permute-start | bytes 104 | tf_op jit(solution)/shard_map/ppermute | solution.py:243
  26.9 38.1 %collective-permute-start.6 = (s32[1,8]{1,0:T(1,128)S(1)}, s32[1,8]{1,0:T(1,128)S(1)}, u32[]{:S(2)}, u32[]{:S(2)}) collective-permute-start(s32[1,8]{1,0:T(1,128)S(1)} %get-tuple-element.9.t0), channel_id=1, source_target_pairs={{0,96},{32,0},{64,32},{96,64},{1,97},{33,1},{65,33},{97,65},{2,98}... | collective-permute-start | bytes 104 | tf_op jit(solution)/shard_map/ppermute | solution.py:243
  60.9 19.1 %collective-permute-start.1 = (bf16[32,2,48,128]{3,2,1,0:T(8,128)(2,1)S(1)}, bf16[32,2,48,128]{3,2,1,0:T(8,128)(2,1)}, u32[]{:S(2)}, u32[]{:S(2)}) collective-permute-start(bf16[32,2,48,128]{3,2,1,0:T(8,128)(2,1)S(1)} %all-to-all-done.after), channel_id=1, source_target_pairs={{0,128},{1,0},{128,256},{129,1},{256,384},{257,129},{384,385},{385... | collective-permute-start | bytes 2359304 | tf_op jit(solution)/shard_map/ppermute | solution.py:198
  62.1 20.6 %collective-permute-start.2 = (bf16[32,2,48,128]{3,2,1,0:T(8,128)(2,1)S(1)}, bf16[32,2,48,128]{3,2,1,0:T(8,128)(2,1)}, u32[]{:S(2)}, u32[]{:S(2)}) collective-permute-start(bf16[32,2,48,128]{3,2,1,0:T(8,128)(2,1)S(1)} %all-to-all-done.after), channel_id=1, source_target_pairs={{0,8},{1,0},{8,16},{9,1},{16,24},{17,9},{24,25},{25,17},{2,10},{3,... | collective-permute-start | bytes 2359304 | tf_op jit(solution)/shard_map/ppermute | solution.py:198
  63.4 19.3 %collective-permute-start.3 = (bf16[32,2,48,128]{3,2,1,0:T(8,128)(2,1)S(1)}, bf16[32,2,48,128]{3,2,1,0:T(8,128)(2,1)}, u32[]{:S(2)}, u32[]{:S(2)}) collective-permute-start(bf16[32,2,48,128]{3,2,1,0:T(8,128)(2,1)S(1)} %all-to-all-done.after), channel_id=1, source_target_pairs={{0,1},{1,129},{128,0},{129,257},{256,128},{257,385},{384,256},{385... | collective-permute-start | bytes 2359304 | tf_op jit(solution)/shard_map/ppermute | solution.py:198
  64.2 19.7 %collective-permute-start.4 = (bf16[32,2,48,128]{3,2,1,0:T(8,128)(2,1)S(1)}, bf16[32,2,48,128]{3,2,1,0:T(8,128)(2,1)}, u32[]{:S(2)}, u32[]{:S(2)}) collective-permute-start(bf16[32,2,48,128]{3,2,1,0:T(8,128)(2,1)S(1)} %all-to-all-done.after), channel_id=1, source_target_pairs={{0,1},{1,9},{8,0},{9,17},{16,8},{17,25},{24,16},{25,24},{2,3},{3,1... | collective-permute-start | bytes 2359304 | tf_op jit(solution)/shard_map/ppermute | solution.py:198
  65.0 31.4 %all-to-all-start.1 = ((bf16[32,48,128]{2,1,0:T(8,128)(2,1)}), bf16[32,48,128]{2,1,0:T(8,128)(2,1)S(1)}, u32[]{:S(2)}, u32[]{:S(2)}) async-start(bf16[32,48,128]{2,1,0:T(8,128)(2,1)} %shard_map.76), calls=%async_computation.1 | async-start | bytes 786432 | tf_op jit(solution)/shard_map/all_to_all | solution.py:253
  80.0 27.6 %collective-permute-start.7 = (bf16[32,2,48,128]{3,2,1,0:T(8,128)(2,1)}, bf16[32,2,48,128]{3,2,1,0:T(8,128)(2,1)S(1)}, u32[]{:S(2)}, u32[]{:S(2)}) collective-permute-start(bf16[32,2,48,128]{3,2,1,0:T(8,128)(2,1)} %collective-permute-done.1.xm), channel_id=1, source_target_pairs={{0,1},{1,9},{8,0},{9,17},{16,8},{17,25},{24,16},{25,24},{2,3},{3,1... | collective-permute-start | bytes 2359304 | tf_op jit(solution)/shard_map/ppermute | solution.py:198
  82.7 24.9 %collective-permute-start.8 = (bf16[32,2,48,128]{3,2,1,0:T(8,128)(2,1)}, bf16[32,2,48,128]{3,2,1,0:T(8,128)(2,1)S(1)}, u32[]{:S(2)}, u32[]{:S(2)}) collective-permute-start(bf16[32,2,48,128]{3,2,1,0:T(8,128)(2,1)} %collective-permute-done.2.ym), channel_id=1, source_target_pairs={{0,128},{1,0},{128,256},{129,1},{256,384},{257,129},{384,385},{385... | collective-permute-start | bytes 2359304 | tf_op jit(solution)/shard_map/ppermute | solution.py:198
  82.7 24.9 %collective-permute-start.9 = (bf16[32,2,48,128]{3,2,1,0:T(8,128)(2,1)}, bf16[32,2,48,128]{3,2,1,0:T(8,128)(2,1)S(1)}, u32[]{:S(2)}, u32[]{:S(2)}) collective-permute-start(bf16[32,2,48,128]{3,2,1,0:T(8,128)(2,1)} %collective-permute-done.3.xp), channel_id=1, source_target_pairs={{0,8},{1,0},{8,16},{9,1},{16,24},{17,9},{24,25},{25,17},{2,10},{3,... | collective-permute-start | bytes 2359304 | tf_op jit(solution)/shard_map/ppermute | solution.py:198
  83.9 23.7 %collective-permute-start.10 = (bf16[32,2,48,128]{3,2,1,0:T(8,128)(2,1)}, bf16[32,2,48,128]{3,2,1,0:T(8,128)(2,1)}, u32[]{:S(2)}, u32[]{:S(2)}) collective-permute-start(bf16[32,2,48,128]{3,2,1,0:T(8,128)(2,1)} %collective-permute-done.4.yp), channel_id=1, source_target_pairs={{0,1},{1,129},{128,0},{129,257},{256,128},{257,385},{384,256},{385... | collective-permute-start | bytes 2359304 | tf_op jit(solution)/shard_map/ppermute | solution.py:198

commit v7 on v4

--- a/solution.py
+++ b/solution.py
@@ -151,7 +151,9 @@
 ):
     copies = []
     for place, source in enumerate((ym, xm, own, xp, yp)):
-        copies.append(pltpu.make_async_copy(source, kv.at[place], sems.at[place]))
+        for w in range(TILES):
+            sem = sems.at[place * TILES + w]
+            copies.append(pltpu.make_async_copy(source.at[w], kv.at[place, w], sem))
     for copy in copies:
         copy.start()
     here = lax.axis_index("zl")
@@ -169,7 +171,9 @@
 def far_kernel(picked, query, sums, mp, mm, pm, pp, out_ref, kv, total, sa, sb, sems):
     copies = []
     for index, source in enumerate((mm, mp, pm, pp)):
-        copies.append(pltpu.make_async_copy(source, kv.at[index], sems.at[index]))
+        for w in range(TILES):
+            sem = sems.at[index * TILES + w]
+            copies.append(pltpu.make_async_copy(source.at[w], kv.at[index, w], sem))
     for copy in copies:
         copy.start()
     total[...] = sums[...]
@@ -282,7 +286,7 @@
         return [
             pltpu.VMEM((tile, tile), jnp.float32),
             pltpu.VMEM((tile, tile), jnp.float32),
-            pltpu.SemaphoreType.DMA((columns + 1,)),
+            pltpu.SemaphoreType.DMA((columns * TILES,)),
         ]
 
     def held(columns):

time: 142 us -> 146 us (1.028)
  Pallas kernels: 19.2 us -> 23 us
    pallas_call x1, Pallas kernels: 2.83 us -> 5.89 us  [on_device(): pl.pallas_call(far_kernel, out_shape=jax.ShapeDtypeStruct(sizes + (dev_to...]
where the time goes in v7:
time: 146 us; the launch traced here: 145 us
  waiting for transfers between devices  52.9 us (36%)
  starting transfers between devices  38.1 us (26%)
  blocking collectives  30.4 us (21%)
  Pallas kernels  23 us (16%)
    all_to_all x1, blocking collectives, on_device(): lax.all_to_all(chunks, RING, split_axis=0, concat_axis=0, tiled=True)  30.4 us
    all_to_all x1, waiting for transfers between devices, on_device(): lax.all_to_all(kv_chunks, RING, split_axis=0, concat_axis=0, tiled=True)  30.2 us
    all_to_all x1, starting transfers between devices, on_device(): lax.all_to_all(kv_chunks, RING, split_axis=0, concat_axis=0, tiled=True)  15.4 us
    ppermute x8, waiting for transfers between devices, moved(): return lax.ppermute(array, (axis, 'c'), pairs)  12.4 us
    pallas_call x1, Pallas kernels, on_device(): pl.pallas_call(near_kernel, out_shape=(jax.ShapeDtypeStruct(sums_shape, j...  12 us
    all_to_all x1, waiting for transfers between devices, on_device(): lax.all_to_all(q_chunks, RING, split_axis=0, concat_axis=0, tiled=True)  10.2 us
    ppermute x3, starting transfers between devices, on_device(): lax.ppermute(table, 'zl', turns[step])  10.2 us
    ppermute x8, starting transfers between devices, moved(): return lax.ppermute(array, (axis, 'c'), pairs)  7.77 us
  transfers between devices with their start and end apart: 13, of which 4 were waited for; matrix products, arithmetic and copies ran while one was open for 0% of the time, Pallas kernels for 9%

profile of v7, /device:TPU:52, one launch (start us, length us, event | category | flops | bytes accessed | tf_op | source)
XLA Modules:
  0.0 145.2 jit_solution(11884605789679311683)
XLA Ops:
  0.0 0.0 copy-start.1
  0.0 0.0 copy-start
  0.0 0.0 copy-start.2
  0.0 2.8 %shard_map.74 = bf16[32,2,48,128]{3,2,1,0:T(8,128)(2,1)} custom-call(bf16[48,3072]{1,0:T(8,128)(2,1)} %bitcast.30, bf16[48,3072]{1,0:T(8,128)(2,1)} %bitcast.31, f32[1,128]{1,0:T(1,128)} %bitcast.32), custom_call_target="tpu_custom_call" | custom-call | tf_op jit(solution)/shard_map/pallas_call | solution.py:217
  2.9 15.4 %all-to-all-start = ((bf16[32,2,48,128]{3,2,1,0:T(8,128)(2,1)}), bf16[32,2,48,128]{3,2,1,0:T(8,128)(2,1)S(1)}, u32[]{:S(2)}, u32[]{:S(2)}) async-start(bf16[32,2,48,128]{3,2,1,0:T(8,128)(2,1)} %shard_map.74), calls=%async_computation | async-start | bytes 1572864 | tf_op jit(solution)/shard_map/all_to_all | solution.py:230
  18.9 0.0 copy-done.1
  18.9 0.0 copy-done
  18.9 0.0 copy-done.2
  18.9 1.5 %shard_map.73 = (bf16[32,48,128]{2,1,0:T(8,128)(2,1)}, s32[1,8]{1,0:T(1,128)S(1)}) custom-call(s32[1,8]{1,0:T(1,128)S(1)} %bitcast.28, s32[1,1]{1,0:T(1,128)} %bitcast.19.counts_ref, bf16[48,3072]{1,0:T(8,128)(2,1)S(1)} %bitcast.27, f32[1,128]{1,0:T(1,128)S(1)} %bitcast.29), custom_call_target="tpu_custom_call" | custom-call | tf_op jit(solution)/shard_map/pallas_call | solution.py:231
  20.5 3.4 %collective-permute-start = (s32[1,8]{1,0:T(1,128)S(1)}, s32[1,8]{1,0:T(1,128)S(1)}, u32[]{:S(2)}, u32[]{:S(2)}) collective-permute-start(s32[1,8]{1,0:T(1,128)S(1)} %get-tuple-element.9.t0), channel_id=1, source_target_pairs={{0,32},{32,64},{64,96},{96,0},{1,33},{33,65},{65,97},{97,1},{2,34}... | collective-permute-start | bytes 104 | tf_op jit(solution)/shard_map/ppermute | solution.py:247
  23.9 3.0 %collective-permute-start.5 = (s32[1,8]{1,0:T(1,128)S(1)}, s32[1,8]{1,0:T(1,128)S(1)}, u32[]{:S(2)}, u32[]{:S(2)}) collective-permute-start(s32[1,8]{1,0:T(1,128)S(1)} %get-tuple-element.9.t0), channel_id=1, source_target_pairs={{0,64},{32,96},{64,0},{96,32},{1,65},{33,97},{65,1},{97,33},{2,66}... | collective-permute-start | bytes 104 | tf_op jit(solution)/shard_map/ppermute | solution.py:247
  26.9 3.7 %collective-permute-start.6 = (s32[1,8]{1,0:T(1,128)S(1)}, s32[1,8]{1,0:T(1,128)S(1)}, u32[]{:S(2)}, u32[]{:S(2)}) collective-permute-start(s32[1,8]{1,0:T(1,128)S(1)} %get-tuple-element.9.t0), channel_id=1, source_target_pairs={{0,96},{32,0},{64,32},{96,64},{1,97},{33,1},{65,33},{97,65},{2,98}... | collective-permute-start | bytes 104 | tf_op jit(solution)/shard_map/ppermute | solution.py:247
  30.6 30.2 %all-to-all-done.after = bf16[32,2,48,128]{3,2,1,0:T(8,128)(2,1)S(1)} async-done(((bf16[32,2,48,128]{3,2,1,0:T(8,128)(2,1)}), bf16[32,2,48,128]{3,2,1,0:T(8,128)(2,1)S(1)}, u32[]{:S(2)}, u32[]{:S(2)}) %all-to-all-start) | async-done | bytes 786464 | tf_op jit(solution)/shard_map/all_to_all | solution.py:230
  60.9 1.2 collective-permute-start.1
  62.1 1.3 collective-permute-start.2
  63.4 0.0 collective-permute-done.table.t1
  63.4 0.8 collective-permute-start.3
  64.2 0.0 collective-permute-done.5.t2
  64.2 0.7 collective-permute-start.4
  64.9 0.0 collective-permute-done.6.t3
  65.0 4.8 %all-to-all-start.1 = ((bf16[32,48,128]{2,1,0:T(8,128)(2,1)}), bf16[32,48,128]{2,1,0:T(8,128)(2,1)S(1)}, u32[]{:S(2)}, u32[]{:S(2)}) async-start(bf16[32,48,128]{2,1,0:T(8,128)(2,1)} %shard_map.76), calls=%async_computation.1 | async-start | bytes 786432 | tf_op jit(solution)/shard_map/all_to_all | solution.py:257
  69.8 10.5 %collective-permute-done.1.xm = bf16[32,2,48,128]{3,2,1,0:T(8,128)(2,1)} collective-permute-done((bf16[32,2,48,128]{3,2,1,0:T(8,128)(2,1)S(1)}, bf16[32,2,48,128]{3,2,1,0:T(8,128)(2,1)}, u32[]{:S(2)}, u32[]{:S(2)}) %collective-permute-start.1) | collective-permute-done | bytes 786464 | tf_op jit(solution)/shard_map/ppermute | solution.py:202
  80.3 0.4 collective-permute-start.7
  80.7 1.9 %collective-permute-done.2.ym = bf16[32,2,48,128]{3,2,1,0:T(8,128)(2,1)} collective-permute-done((bf16[32,2,48,128]{3,2,1,0:T(8,128)(2,1)S(1)}, bf16[32,2,48,128]{3,2,1,0:T(8,128)(2,1)}, u32[]{:S(2)}, u32[]{:S(2)}) %collective-permute-start.2) | collective-permute-done | bytes 786464 | tf_op jit(solution)/shard_map/ppermute | solution.py:202
  82.6 0.0 collective-permute-start.8
  82.6 0.0 collective-permute-done.3.xp
  82.6 1.3 collective-permute-start.9
  83.9 0.0 collective-permute-done.4.yp
  83.9 2.0 %collective-permute-start.10 = (bf16[32,2,48,128]{3,2,1,0:T(8,128)(2,1)}, bf16[32,2,48,128]{3,2,1,0:T(8,128)(2,1)}, u32[]{:S(2)}, u32[]{:S(2)}) collective-permute-start(bf16[32,2,48,128]{3,2,1,0:T(8,128)(2,1)} %collective-permute-done.4.yp), channel_id=1, source_target_pairs={{0,1},{1,129},{128,0},{129,257},{256,128},{257,385},{384,256},{385... | collective-permute-start | bytes 2359304 | tf_op jit(solution)/shard_map/ppermute | solution.py:202
  85.9 10.2 %all-to-all-done.1 = bf16[32,48,128]{2,1,0:T(8,128)(2,1)S(1)} async-done(((bf16[32,48,128]{2,1,0:T(8,128)(2,1)}), bf16[32,48,128]{2,1,0:T(8,128)(2,1)S(1)}, u32[]{:S(2)}, u32[]{:S(2)}) %all-to-all-start.1) | async-done | bytes 393248 | tf_op jit(solution)/shard_map/all_to_all | solution.py:257
  96.1 12.0 %shard_map.77 = (f32[5,384,256]{2,1,0:T(8,128)S(1)}, s32[4,35]{1,0:T(4,128)S(1)}) custom-call(s32[1,8]{1,0:T(1,128)S(1)} %get-tuple-element.9.t0, s32[1,8]{1,0:T(1,128)S(1)} %shard_map.75.t1, s32[1,8]{1,0:T(1,128)S(1)} %collective-permute-done.5.t2, s32[1,8]{1,0:T(1,128)S(1)} %collective-permute-done.6.t3, bf16[4,4,2,48,128]{4,3,2,1,0:T(8,128)(2,1)S(1)} %bitcast.20, ...), custom_call_target="tpu_custom_call" | custom-call | flops 2264924160 | bytes 4718592 | tf_op jit(solution)/shard_map/pallas_call | solution.py:297
  108.1 0.0 collective-permute-done.7
  108.1 0.0 collective-permute-done.8
  108.1 0.0 collective-permute-done.9
  108.1 0.0 collective-permute-done.10
  108.1 5.9 %shard_map.78 = bf16[4,4,2,48,128]{4,3,2,1,0:T(8,128)(2,1)S(1)} custom-call(s32[4,35]{1,0:T(4,128)S(1)} %get-tuple-element.11.picked, bf16[4,4,2,48,128]{4,3,2,1,0:T(8,128)(2,1)S(1)} %bitcast.21, f32[5,384,256]{2,1,0:T(8,128)S(1)} %get-tuple-element.12.sums, bf16[4,4,2,2,48,128]{5,4,3,2,1,0:T(8,128)(2,1)S(1)} %bitcast.24, ...), custom_call_target="tpu_custom_call" | custom-call | flops 905969664 | bytes 4718592 | tf_op jit(solution)/shard_map/pallas_call | solution.py:314
  114.0 30.4 %all_to_all.15.chunk_ref = bf16[32,48,128]{2,1,0:T(8,128)(2,1)S(1)} all-to-all(bf16[32,48,128]{2,1,0:T(8,128)(2,1)S(1)} %bitcast.22), channel_id=1, replica_groups=mesh['x'=4,'zl'=4,'y'=4,'zh'=4,'c'=2] {'zl','zh','c'}, dimensions={0} | all-to-all | bytes 786432 | tf_op jit(solution)/shard_map/all_to_all | solution.py:325
  144.4 0.8 shard_map.79
  (2 shorter events, 0.0 us)
Async XLA Ops:
  0.0 18.9 %copy-start.1 = (s32[1,1,1,8]{3,2,1,0:T(1,128)S(1)}, s32[1,1,1,8]{3,2,1,0:T(1,128)}, u32[]{:S(2)}) copy-start(s32[1,1,1,8]{3,2,1,0:T(1,128)} %param.12) | copy-start | bytes 100
  0.0 18.9 %copy-start = (bf16[1,1,48,3072]{3,2,1,0:T(8,128)(2,1)S(1)}, bf16[1,1,48,3072]{3,2,1,0:T(8,128)(2,1)}, u32[]{:S(2)}) copy-start(bf16[1,1,48,3072]{3,2,1,0:T(8,128)(2,1)} %param.7) | copy-start | bytes 884740
  0.0 18.9 %copy-start.2 = (f32[128]{0:T(128)S(1)}, f32[128]{0:T(128)}, u32[]{:S(2)}) copy-start(f32[128]{0:T(128)} %param.10) | copy-start | bytes 1540
  2.9 58.0 %all-to-all-start = ((bf16[32,2,48,128]{3,2,1,0:T(8,128)(2,1)}), bf16[32,2,48,128]{3,2,1,0:T(8,128)(2,1)S(1)}, u32[]{:S(2)}, u32[]{:S(2)}) async-start(bf16[32,2,48,128]{3,2,1,0:T(8,128)(2,1)} %shard_map.74), calls=%async_computation | async-start | bytes 1572864 | tf_op jit(solution)/shard_map/all_to_all | solution.py:230
  20.5 42.9 %collective-permute-start = (s32[1,8]{1,0:T(1,128)S(1)}, s32[1,8]{1,0:T(1,128)S(1)}, u32[]{:S(2)}, u32[]{:S(2)}) collective-permute-start(s32[1,8]{1,0:T(1,128)S(1)} %get-tuple-element.9.t0), channel_id=1, source_target_pairs={{0,32},{32,64},{64,96},{96,0},{1,33},{33,65},{65,97},{97,1},{2,34}... | collective-permute-start | bytes 104 | tf_op jit(solution)/shard_map/ppermute | solution.py:247
  23.9 40.3 %collective-permute-start.5 = (s32[1,8]{1,0:T(1,128)S(1)}, s32[1,8]{1,0:T(1,128)S(1)}, u32[]{:S(2)}, u32[]{:S(2)}) collective-permute-start(s32[1,8]{1,0:T(1,128)S(1)} %get-tuple-element.9.t0), channel_id=1, source_target_pairs={{0,64},{32,96},{64,0},{96,32},{1,65},{33,97},{65,1},{97,33},{2,66}... | collective-permute-start | bytes 104 | tf_op jit(solution)/shard_map/ppermute | solution.py:247
  26.9 38.1 %collective-permute-start.6 = (s32[1,8]{1,0:T(1,128)S(1)}, s32[1,8]{1,0:T(1,128)S(1)}, u32[]{:S(2)}, u32[]{:S(2)}) collective-permute-start(s32[1,8]{1,0:T(1,128)S(1)} %get-tuple-element.9.t0), channel_id=1, source_target_pairs={{0,96},{32,0},{64,32},{96,64},{1,97},{33,1},{65,33},{97,65},{2,98}... | collective-permute-start | bytes 104 | tf_op jit(solution)/shard_map/ppermute | solution.py:247
  60.9 19.4 %collective-permute-start.1 = (bf16[32,2,48,128]{3,2,1,0:T(8,128)(2,1)S(1)}, bf16[32,2,48,128]{3,2,1,0:T(8,128)(2,1)}, u32[]{:S(2)}, u32[]{:S(2)}) collective-permute-start(bf16[32,2,48,128]{3,2,1,0:T(8,128)(2,1)S(1)} %all-to-all-done.after), channel_id=1, source_target_pairs={{0,128},{1,0},{128,256},{129,1},{256,384},{257,129},{384,385},{385... | collective-permute-start | bytes 2359304 | tf_op jit(solution)/shard_map/ppermute | solution.py:202
  62.1 20.5 %collective-permute-start.2 = (bf16[32,2,48,128]{3,2,1,0:T(8,128)(2,1)S(1)}, bf16[32,2,48,128]{3,2,1,0:T(8,128)(2,1)}, u32[]{:S(2)}, u32[]{:S(2)}) collective-permute-start(bf16[32,2,48,128]{3,2,1,0:T(8,128)(2,1)S(1)} %all-to-all-done.after), channel_id=1, source_target_pairs={{0,8},{1,0},{8,16},{9,1},{16,24},{17,9},{24,25},{25,17},{2,10},{3,... | collective-permute-start | bytes 2359304 | tf_op jit(solution)/shard_map/ppermute | solution.py:202
  63.4 19.3 %collective-permute-start.3 = (bf16[32,2,48,128]{3,2,1,0:T(8,128)(2,1)S(1)}, bf16[32,2,48,128]{3,2,1,0:T(8,128)(2,1)}, u32[]{:S(2)}, u32[]{:S(2)}) collective-permute-start(bf16[32,2,48,128]{3,2,1,0:T(8,128)(2,1)S(1)} %all-to-all-done.after), channel_id=1, source_target_pairs={{0,1},{1,129},{128,0},{129,257},{256,128},{257,385},{384,256},{385... | collective-permute-start | bytes 2359304 | tf_op jit(solution)/shard_map/ppermute | solution.py:202
  64.2 19.7 %collective-permute-start.4 = (bf16[32,2,48,128]{3,2,1,0:T(8,128)(2,1)S(1)}, bf16[32,2,48,128]{3,2,1,0:T(8,128)(2,1)}, u32[]{:S(2)}, u32[]{:S(2)}) collective-permute-start(bf16[32,2,48,128]{3,2,1,0:T(8,128)(2,1)S(1)} %all-to-all-done.after), channel_id=1, source_target_pairs={{0,1},{1,9},{8,0},{9,17},{16,8},{17,25},{24,16},{25,24},{2,3},{3,1... | collective-permute-start | bytes 2359304 | tf_op jit(solution)/shard_map/ppermute | solution.py:202
  65.0 31.1 %all-to-all-start.1 = ((bf16[32,48,128]{2,1,0:T(8,128)(2,1)}), bf16[32,48,128]{2,1,0:T(8,128)(2,1)S(1)}, u32[]{:S(2)}, u32[]{:S(2)}) async-start(bf16[32,48,128]{2,1,0:T(8,128)(2,1)} %shard_map.76), calls=%async_computation.1 | async-start | bytes 786432 | tf_op jit(solution)/shard_map/all_to_all | solution.py:257
  80.3 27.8 %collective-permute-start.7 = (bf16[32,2,48,128]{3,2,1,0:T(8,128)(2,1)}, bf16[32,2,48,128]{3,2,1,0:T(8,128)(2,1)S(1)}, u32[]{:S(2)}, u32[]{:S(2)}) collective-permute-start(bf16[32,2,48,128]{3,2,1,0:T(8,128)(2,1)} %collective-permute-done.1.xm), channel_id=1, source_target_pairs={{0,1},{1,9},{8,0},{9,17},{16,8},{17,25},{24,16},{25,24},{2,3},{3,1... | collective-permute-start | bytes 2359304 | tf_op jit(solution)/shard_map/ppermute | solution.py:202
  82.6 25.5 %collective-permute-start.8 = (bf16[32,2,48,128]{3,2,1,0:T(8,128)(2,1)}, bf16[32,2,48,128]{3,2,1,0:T(8,128)(2,1)S(1)}, u32[]{:S(2)}, u32[]{:S(2)}) collective-permute-start(bf16[32,2,48,128]{3,2,1,0:T(8,128)(2,1)} %collective-permute-done.2.ym), channel_id=1, source_target_pairs={{0,128},{1,0},{128,256},{129,1},{256,384},{257,129},{384,385},{385... | collective-permute-start | bytes 2359304 | tf_op jit(solution)/shard_map/ppermute | solution.py:202
  82.6 25.5 %collective-permute-start.9 = (bf16[32,2,48,128]{3,2,1,0:T(8,128)(2,1)}, bf16[32,2,48,128]{3,2,1,0:T(8,128)(2,1)S(1)}, u32[]{:S(2)}, u32[]{:S(2)}) collective-permute-start(bf16[32,2,48,128]{3,2,1,0:T(8,128)(2,1)} %collective-permute-done.3.xp), channel_id=1, source_target_pairs={{0,8},{1,0},{8,16},{9,1},{16,24},{17,9},{24,25},{25,17},{2,10},{3,... | collective-permute-start | bytes 2359304 | tf_op jit(solution)/shard_map/ppermute | solution.py:202
  83.9 24.2 %collective-permute-start.10 = (bf16[32,2,48,128]{3,2,1,0:T(8,128)(2,1)}, bf16[32,2,48,128]{3,2,1,0:T(8,128)(2,1)}, u32[]{:S(2)}, u32[]{:S(2)}) collective-permute-start(bf16[32,2,48,128]{3,2,1,0:T(8,128)(2,1)} %collective-permute-done.4.yp), channel_id=1, source_target_pairs={{0,1},{1,129},{128,0},{129,257},{256,128},{257,385},{384,256},{385... | collective-permute-start | bytes 2359304 | tf_op jit(solution)/shard_map/ppermute | solution.py:202
